TPU v7x, 32 devices: a whole 2x2x4 slice. The times are simulated.
32 devices in a mesh: leaf: 8 (over z, y), sep: 4 (over x, core).
Axes of the slice: x: 2, y: 2, z: 4, core: 2. Of those that a mesh axis runs over, the one named last changes fastest.
Arguments:
- leaf_rhs: float32 [12288, 128], P(('leaf', 'sep')), may hold values from -6 to 6
- leaf_inverse: float32 [12288, 64], P(('leaf', 'sep')), may hold values from -1 to 1
- leaf_coupling: bfloat16 [2, 8192, 12288], P(None, None, ('leaf', 'sep')), may hold values from -0.21875 to 0.21875
- tile_mask: int32 [2, 128, 192], P(None, None, ('leaf', 'sep')), may hold values 0 or 1
- low_rhs: float32 [16384, 128], P(('leaf', 'sep')), may hold values from -6 to 6
- top_rhs: float32 [8192, 128], P(('leaf', 'sep')), may hold values from -6 to 6
- low_inverse: float32 [16384, 8192], P(('leaf', 'sep')), may hold values from -0.0625 to 0.0625
- top_inverse: float32 [8192, 8192], P(('leaf', 'sep')), may hold values from -0.0625 to 0.0625
- low_coupling: float32 [8192, 16384], P(None, ('leaf', 'sep')), may hold values from -0.0625 to 0.0625
Outputs:
- interior_solution: float32 [12288, 128], P(('leaf', 'sep'))
- top_solution: float32 [8192, 128], P(('leaf', 'sep'))
All inputs are finite; a program needn't handle non-finite values. No bound on the sum of `tile_mask` on one device may be relied on, other than what follows from the above.
Results may differ from a plain program's by a relative error of at most 0.0033.
Values may be sent and summed in bfloat16 or wider, within the bound.
No kernel may reach another device: no remote copies, remote signals or barrier semaphores. Data moves between devices by JAX's collectives and lax.ppermute only.
A program may use at most 192 MiB of HBM per device.

v0:
```python
import functools

import jax
import jax.numpy as jnp
from jax import lax
from jax.experimental import pallas as pl
from jax.experimental.pallas import tpu as pltpu
from jax.sharding import PartitionSpec as P

PRECISE = lax.Precision.HIGHEST
F32 = jnp.float32
BF16 = jnp.bfloat16
I16 = jnp.int16
AXES = ("leaf", "sep")
NEAR = 8
GROUP = 2 * NEAR
BATCHES = ((4, 4), (0, 4))
PAD = 16
VMEM = 24 << 20


def swap(block, offset):
    count = lax.axis_size("leaf") * lax.axis_size("sep")
    return lax.ppermute(block, AXES, [(at, at ^ offset) for at in range(count)])


def encode(value):
    peak = jnp.maximum(jnp.max(jnp.abs(value), axis=0, keepdims=True), 1e-30)
    power = jnp.ceil(jnp.log2(peak))
    part = jnp.ceil(peak * jnp.exp2(14.0 - power))
    scale = 32767.0 / (part * jnp.exp2(power - 14.0))
    code = jnp.floor(value * scale + 0.5).astype(jnp.int32).astype(I16)
    row = lax.broadcasted_iota(jnp.int32, (PAD, value.shape[1]), 0)
    return code, jnp.where(row == 0, power, part).astype(jnp.int32).astype(I16)


def put(ref, coded):
    code, head = coded
    rows = code.shape[0]
    ref[:rows, :] = code
    ref[rows:, :] = head


def decode(block):
    rows = block.shape[0] - PAD
    head = block[rows:, :].astype(jnp.int32).astype(F32)
    scale = head[1:2, :] * jnp.exp2(head[0:1, :] - 14.0) * (1.0 / 32767.0)
    return block[:rows, :].astype(jnp.int32).astype(F32) * scale


def halves(value):
    high = value.astype(BF16)
    return high, (value - high.astype(F32)).astype(BF16)


def dot(left, right):
    return jnp.dot(left, right, preferred_element_type=F32)


def spread_tiles(tiles, level, width, size):
    across = tiles.shape[0]
    flags = tiles[:, level, :].astype(F32).T
    lane = lax.broadcasted_iota(jnp.int32, (flags.shape[0], width), 1) // size
    spread = jnp.zeros((flags.shape[0], width), F32)
    for at in range(across):
        spread = jnp.where(lane == at, flags[:, at : at + 1], spread)
    return spread


def masked(block, spread, chunk, size):
    width = block.shape[1]
    count = block.shape[0] // size
    flags = spread[0, pl.ds(pl.multiple_of(chunk * count, count), count), :]
    parts = []
    for at in range(count):
        row = jnp.broadcast_to(flags[at : at + 1, :], (16, width)).astype(BF16)
        tile = block[at * size : (at + 1) * size, :].reshape(size // 16, 16, width)
        parts.append((tile * row[None]).reshape(size, width))
    return jnp.concatenate(parts, 0)


def triangular(block, row_start, column_start):
    row = lax.broadcasted_iota(jnp.int32, block.shape, 0) + row_start
    column = lax.broadcasted_iota(jnp.int32, block.shape, 1) + column_start
    return jnp.where(row >= column, block, 0.0)


def with_rows(value, chunk, start, rhs):
    count = rhs.shape[0]
    parts = []
    for at in range(value.shape[0] // count):
        here = (start == chunk * value.shape[0] + at * count).astype(F32)
        parts.append(value[at * count : (at + 1) * count, :] + rhs[...] * here)
    return jnp.concatenate(parts, 0) if len(parts) > 1 else parts[0]


def call(kernel, place, steps, ins, outs, scratch, args, flops, moved):
    return pl.pallas_call(
        kernel,
        grid_spec=pltpu.PrefetchScalarGridSpec(
            num_scalar_prefetch=1,
            grid=(steps,),
            in_specs=ins,
            out_specs=[spec for spec, _ in outs],
            scratch_shapes=scratch,
        ),
        out_shape=[shape for _, shape in outs],
        compiler_params=pltpu.CompilerParams(vmem_limit_bytes=VMEM),
        cost_estimate=pl.CostEstimate(flops=flops, bytes_accessed=moved, transcendentals=0),
    )(place, *args)


def whole(shape):
    return pl.BlockSpec(shape, lambda *_: (0,) * len(shape))


def out_whole(shape, dtype):
    return whole(shape), jax.ShapeDtypeStruct(shape, dtype)


def in_steps(count, shape, dtype=None, entries=0):
    spec = pl.BlockSpec((count, *shape), lambda k, p: (k,) + (0,) * len(shape))
    return spec if dtype is None else (spec, jax.ShapeDtypeStruct((entries, *shape), dtype))


def at_rest(array):
    return pltpu.with_memory_space_constraint(array, pltpu.HBM)


def chunk_at(step, place, flip):
    return ((place[1] ^ step) << 1) | (place[0] ^ flip)


def steps_of(first, at, per):
    return first + pl.program_id(0) * per + at


def over(shape, index):
    def spec(first, at, per, flip):
        return pl.BlockSpec(shape, lambda k, p: index(chunk_at(first + k * per + at, p, flip)))

    return spec


def emit(first, per, at, outs, value):
    coded = encode(value)
    for step in range(len(outs) // per):
        where = step * per + at

        @pl.when(pl.program_id(0) == step)
        def _(where=where):
            if first + where == 0:
                outs[where][...] = value
            else:
                put(outs[where], coded)


def reduced(place, kernel, specs, args, shape, scratch, flops, moved, per, received=None):
    coded = (shape[0] + PAD, shape[1])
    if received is None:
        sent = call(
            functools.partial(kernel, 1, 0, per),
            place,
            NEAR // per,
            specs(0, per, 1),
            [in_steps(per, coded, I16, NEAR)],
            scratch,
            args,
            flops // 2,
            moved // 2,
        )
        received = swap(sent[0], 1)
    kept = [None] * NEAR
    for first, count in BATCHES:
        kept[first : first + count] = call(
            functools.partial(kernel, 0, first, per),
            place,
            count // per,
            specs(first, per, 0)
            + [
                pl.BlockSpec(
                    (per, *coded), lambda k, p, first=first: (first // per + k, 0, 0)
                )
            ],
            [
                out_whole(shape, F32) if at == 0 else out_whole(coded, I16)
                for at in range(first, first + count)
            ],
            scratch,
            [*args, received],
            flops // 4,
            moved // 4,
        )
    return kept


def leaf_low_value(size, chunk, place, block, spread, rounded, rhs):
    value = -dot(masked(block[0, 0], spread, chunk, size), rounded[...])
    return with_rows(value, chunk, place[2], rhs)


def leaf_send_kernel(size, per, place, *rest):
    blocks, (leaf_rhs, inverse_t, tiles, rhs) = rest[:per], rest[per : per + 4]
    sent, forward, rounded, spread = rest[per + 4 :]

    @pl.when(pl.program_id(0) == 0)
    def _():
        inverse = inverse_t[...].T
        for at in range(leaf_rhs.shape[0] // size):
            rows = slice(at * size, (at + 1) * size)
            block = triangular(inverse[rows, :], 0, 0)
            value = jnp.dot(block, leaf_rhs[rows, :], precision=PRECISE, preferred_element_type=F32)
            forward[rows, :] = value
            rounded[rows, :] = value.astype(BF16)
        for level in range(spread.shape[0]):
            spread[level] = spread_tiles(tiles, level, spread.shape[2], size)

    for at in range(per):
        chunk = chunk_at(steps_of(0, at, per), place, 1)
        value = leaf_low_value(size, chunk, place, blocks[at], spread, rounded, rhs)
        put(sent.at[at], encode(value))


def leaf_keep_kernel(size, flip, first, per, place, *rest):
    blocks, (spread, rounded, rhs, received) = rest[:per], rest[per : per + 4]
    for at in range(per):
        chunk = chunk_at(steps_of(first, at, per), place, flip)
        value = leaf_low_value(size, chunk, place, blocks[at], spread, rounded, rhs)
        emit(first, per, at, rest[per + 4 :], value + decode(received[at]))


def leaf_top_kernel(size, place, spread, rounded, coupling, part):
    group = coupling.shape[1]
    for at in range(group):
        chunk = pl.program_id(0) * group + at
        part[at] = dot(masked(coupling[0, at], spread, chunk, size), rounded[...])


def sum_kernel(final, waits, place, own, *rest):
    blocks, out = rest[: len(rest) - 1 - waits], rest[-1]
    value = own[...] if own.dtype == F32 else decode(own[...])
    for block in blocks:
        value = value + decode(block[...])
    if final:
        out[...] = value.astype(BF16)
    else:
        put(out, encode(value))


def summed(place, own, received, final, before=()):
    rows, columns = received[0].shape
    return call(
        functools.partial(sum_kernel, final, len(before)),
        place,
        1,
        [whole(own.shape)]
        + [whole(r.shape) for r in received]
        + [pl.BlockSpec(memory_space=pl.ANY) for _ in before],
        [out_whole((rows - PAD if final else rows, columns), BF16 if final else I16)],
        [],
        [own, *received, *before],
        rows * columns * 8,
        rows * columns * 20,
    )[0]


def reduce_and_gather(place, kept, far, final=False, before=()):
    received = [swap(kept[at], at << 1) for at in range(NEAR - 1, 0, -1)]
    coded = summed(place, kept[0], received, final and not far, before)
    if far:
        coded = summed(place, coded, [swap(coded, offset) for offset in far], final)
    mine = [coded] + [None] * (NEAR - 1)
    for at in range(NEAR - 1, 0, -1):
        mine[at] = swap(coded, at << 1)
    mine = jnp.stack(mine)
    return mine, swap(mine, 1)


def factor_kernel(start_at, flip, per, place, *rest):
    factors, stack, rest = rest[:per], rest[per], rest[per + 1 :]
    before, rest = (rest[0], rest[1:]) if flip else (None, rest)
    out, wide, narrow = rest[0], rest[-2], rest[-1]
    depth = factors[0].shape[1]
    columns = narrow.shape[1]

    @pl.when(pl.program_id(0) == 0)
    def _():
        wide[...] = jnp.zeros_like(wide)
        narrow[...] = jnp.zeros_like(narrow)

    @pl.when(pl.program_id(0) >= 0)
    def _():
        highs, lows, uppers, lowers = [], [], [], []
        for at in range(per):
            chunk = chunk_at(steps_of(0, at, per), place, flip)
            high, low = halves(triangular(factors[at][...], place[start_at], chunk * depth))
            upper, lower = halves(decode(stack[at]))
            highs, lows = highs + [high], lows + [low]
            uppers, lowers = uppers + [upper], lowers + [lower]
        upper = jnp.concatenate(uppers, 0)
        both = jnp.concatenate([upper, jnp.concatenate(lowers, 0)], 1)
        wide[...] += dot(jnp.concatenate(highs, 1), both)
        narrow[...] += dot(jnp.concatenate(lows, 1), upper)

    @pl.when(pl.program_id(0) == pl.num_programs(0) - 1)
    def _():
        value = wide[:, :columns] + wide[:, columns:] + narrow[...]
        if flip:
            value = value + before[...]
            rest[1][...] = value.T
        out[...] = value


def factor_apply(place, factor, stacks, start_at):
    count, size = factor.shape
    depth = size // GROUP
    columns = stacks[0].shape[2]
    per = 2
    block = over((count, depth), lambda chunk: (0, chunk))
    result = ()
    for flip in range(2):
        result = call(
            functools.partial(factor_kernel, start_at, flip, per),
            place,
            NEAR // per,
            [block(0, at, per, flip) for at in range(per)]
            + [in_steps(per, stacks[flip].shape[1:])]
            + [whole(r.shape) for r in result],
            [out_whole((count, columns), F32)] + [out_whole((columns, count), F32)] * flip,
            [pltpu.VMEM((count, 2 * columns), F32), pltpu.VMEM((count, columns), F32)],
            [at_rest(factor)] * per + [stacks[flip], *result],
            4 * count * size * columns,
            2 * count * size,
        )
    return result


def coupled_kernel(flip, first, per, place, *rest):
    couplings, parts, rest = rest[:per], rest[per : 2 * per], rest[2 * per :]
    rows, rhs, packed = rest[0], rest[1], rest[-1]
    columns = rows.shape[1]

    @pl.when(pl.program_id(0) == 0)
    def _():
        high, low = halves(rows[...])
        packed[:, :columns] = high
        packed[:, columns:] = low

    for at in range(per):
        chunk = chunk_at(steps_of(first, at, per), place, flip)
        high, low = halves(couplings[at][0])
        product = dot(high, packed[...])
        value = product[:, :columns] + product[:, columns:] + dot(low, packed[:, :columns])
        value = with_rows(-(parts[at][0] + value), chunk, place[3], rhs)
        if flip:
            put(rest[2].at[at], encode(value))
        else:
            emit(first, per, at, rest[3:-1], value + decode(rest[2][at]))


def back_kernel(start_at, flip, first, per, place, *rest):
    factors, vector, rest = rest[:per], rest[per], rest[per + 1 :]
    packed = rest[-1]
    columns = vector.shape[0]

    @pl.when(pl.program_id(0) == 0)
    def _():
        high, low = halves(vector[...])
        packed[:columns, :] = high
        packed[columns:, :] = low

    for at in range(per):
        chunk = chunk_at(steps_of(first, at, per), place, flip)
        depth = factors[at].shape[1]
        high, low = halves(triangular(factors[at][...], place[start_at], chunk * depth))
        product = dot(packed[...], high)
        value = product[:columns, :] + product[columns:, :] + dot(packed[:columns, :], low)
        if flip:
            put(rest[0].at[at], encode(value))
        else:
            emit(first, per, at, rest[1:-1], value + decode(rest[0][at]))


def back_apply(place, factor, vector, start_at):
    count, size = factor.shape
    columns = vector.shape[0]
    chunk = size // GROUP
    block = over((count, chunk), lambda c: (0, c))
    per = 2

    def specs(first, per, flip):
        return [block(first, at, per, flip) for at in range(per)] + [whole(vector.shape)]

    return reduced(
        place,
        functools.partial(back_kernel, start_at),
        specs,
        [at_rest(factor)] * per + [vector],
        (columns, chunk),
        [pltpu.VMEM((2 * columns, count), BF16)],
        8 * count * size * columns,
        4 * count * size,
        per,
    )


def carry_kernel(flip, per, place, *rest):
    couplings, (stack, before, gap, rounded, wide, narrow) = rest[:per], rest[per:]
    columns = before.shape[0]

    @pl.when(pl.program_id(0) == 0)
    def _():
        wide[...] = jnp.zeros_like(wide)
        narrow[...] = jnp.zeros_like(narrow)

    @pl.when(pl.program_id(0) >= 0)
    def _():
        highs, lows, uppers, lowers = [], [], [], []
        for at in range(per):
            high, low = halves(couplings[at][0])
            upper, lower = halves(decode(stack[at]))
            rounded[at] = upper
            highs, lows = highs + [high], lows + [low]
            uppers, lowers = uppers + [upper], lowers + [lower]
        upper = jnp.concatenate(uppers, 1)
        both = jnp.concatenate([upper, jnp.concatenate(lowers, 1)], 0)
        wide[...] += dot(both, jnp.concatenate(highs, 0))
        narrow[...] += dot(upper, jnp.concatenate(lows, 0))

    @pl.when(pl.program_id(0) == pl.num_programs(0) - 1)
    def _():
        gap[...] = before[...] - (wide[:columns, :] + wide[columns:, :] + narrow[...])


def own_kernel(place, mine, other, out):
    chunk = place[3] // out.shape[0]
    here = (chunk % 2 == place[0]).astype(F32)
    out[...] = (decode(mine[0]) * here + decode(other[0]) * (1.0 - here)).T


def leaf_product(size, flip, per, place, blocks, spread, path):
    left, right = [], []
    for at in range(per):
        chunk = chunk_at(steps_of(0, at, per), place, flip)
        left.append(path[at])
        right.append(masked(blocks[at][0, 0], spread, chunk, size))
    return dot(jnp.concatenate(left, 1), jnp.concatenate(right, 0))


def leaf_back_top_kernel(size, per, place, *rest):
    near, far, (spread, mine, other, out) = rest[:per], rest[per : 2 * per], rest[2 * per :]

    @pl.when(pl.program_id(0) == 0)
    def _():
        out[...] = jnp.zeros_like(out)

    @pl.when(pl.program_id(0) >= 0)
    def _():
        out[...] += leaf_product(size, 0, per, place, near, spread, mine)
        out[...] += leaf_product(size, 1, per, place, far, spread, other)


def leaf_back_kernel(size, flip, per, place, *rest):
    blocks, (spread, path, before), rest = rest[:per], rest[per : per + 3], rest[per + 3 :]
    out, total = rest[-2:]

    @pl.when(pl.program_id(0) == 0)
    def _():
        total[...] = before[...]

    @pl.when(pl.program_id(0) >= 0)
    def _():
        total[...] += leaf_product(size, flip, per, place, blocks, spread, path)

    @pl.when(pl.program_id(0) == pl.num_programs(0) - 1)
    def _():
        if not flip:
            out[...] = total[...]
        else:
            forward, inverse_t = rest[:2]
            gap = forward[...] - total[...].T
            inverse = inverse_t[...].T
            for at in range(gap.shape[0] // size):
                rows = slice(at * size, (at + 1) * size)
                block = triangular(inverse[rows, :], 0, 0).T
                out[rows, :] = jnp.dot(
                    block, gap[rows, :], precision=PRECISE, preferred_element_type=F32
                )


def body(
    leaf_rhs,
    leaf_inverse,
    leaf_coupling,
    tile_mask,
    low_rhs,
    top_rhs,
    low_inverse,
    top_inverse,
    low_coupling,
):
    device_total = lax.axis_size("leaf") * lax.axis_size("sep")
    device = lax.axis_index("leaf") * lax.axis_size("sep") + lax.axis_index("sep")
    local_rows, columns = leaf_rhs.shape
    size = leaf_inverse.shape[1]
    levels = leaf_coupling.shape[0]
    sep_size = low_inverse.shape[1]
    low_count = low_inverse.shape[0]
    top_count = top_inverse.shape[0]
    chunk = sep_size // GROUP
    low_far = list(range(GROUP, device_total // 2, GROUP))
    top_far = list(range(GROUP, device_total, GROUP))
    low_start = device % (device_total // 2) * low_count
    top_start = device * top_count
    place = jnp.stack([device % 2, device % GROUP // 2, low_start, top_start]).astype(jnp.int32)

    inverse_t = at_rest(leaf_inverse.T)
    tiles = at_rest(jnp.transpose(tile_mask, (2, 0, 1)))
    coupling = at_rest(leaf_coupling.reshape(levels, GROUP, chunk, local_rows))
    low_blocks = at_rest(low_coupling.reshape(GROUP, chunk, low_count))
    low_rhs, top_rhs = at_rest(low_rhs), at_rest(top_rhs)

    leaf_flops = 2 * sep_size * local_rows * columns
    leaf_moved = 2 * sep_size * local_rows
    leaf_low = over((1, 1, chunk, local_rows), lambda c: (0, c, 0, 0))
    leaf_top = over((1, 1, chunk, local_rows), lambda c: (1, c, 0, 0))
    spread_shape = (levels, sep_size // size, local_rows)

    def spread_of(level):
        return pl.BlockSpec((1, *spread_shape[1:]), lambda k, p: (level, 0, 0))

    per = 4
    coded = (chunk + PAD, columns)
    sent, forward_leaf, rounded_leaf, spread = call(
        functools.partial(leaf_send_kernel, size, per),
        place,
        NEAR // per,
        [leaf_low(0, at, per, 1) for at in range(per)]
        + [whole(a.shape) for a in (leaf_rhs, inverse_t, tiles, low_rhs)],
        [
            in_steps(per, coded, I16, NEAR),
            out_whole(leaf_rhs.shape, F32),
            out_whole(leaf_rhs.shape, BF16),
            out_whole(spread_shape, F32),
        ],
        [],
        [coupling] * per + [at_rest(leaf_rhs), inverse_t, tiles, low_rhs],
        leaf_flops // 2,
        leaf_moved // 2,
    )

    def leaf_specs(first, per, flip):
        return [leaf_low(first, at, per, flip) for at in range(per)] + [
            spread_of(0),
            whole(rounded_leaf.shape),
            whole(low_rhs.shape),
        ]

    kept = reduced(
        place,
        functools.partial(leaf_keep_kernel, size),
        leaf_specs,
        [coupling] * per + [spread, rounded_leaf, low_rhs],
        (chunk, columns),
        [],
        leaf_flops,
        leaf_moved,
        per,
        swap(sent, 1),
    )
    part = call(
        functools.partial(leaf_top_kernel, size),
        place,
        GROUP // per,
        [
            spread_of(1),
            whole(rounded_leaf.shape),
            pl.BlockSpec((1, per, chunk, local_rows), lambda k, p: (1, k, 0, 0)),
        ],
        [in_steps(per, (chunk, columns), F32, GROUP)],
        [],
        [spread, rounded_leaf, coupling],
        leaf_flops,
        leaf_moved,
    )[0]
    first_input = reduce_and_gather(place, kept, low_far, before=[part])
    first_rows, first_columns = factor_apply(place, low_inverse, first_input, 2)

    coupled_flops = 8 * sep_size * low_count * columns
    coupled_moved = 4 * sep_size * low_count
    low_block = over((1, chunk, low_count), lambda c: (c, 0, 0))
    part_block = over((1, chunk, columns), lambda c: (c, 0, 0))
    per = 2

    def coupled_specs(first, per, flip):
        return (
            [low_block(first, at, per, flip) for at in range(per)]
            + [part_block(first, at, per, flip) for at in range(per)]
            + [whole(first_rows.shape), whole(top_rhs.shape)]
        )

    kept = reduced(
        place,
        coupled_kernel,
        coupled_specs,
        [low_blocks] * per + [part] * per + [first_rows, top_rhs],
        (chunk, columns),
        [pltpu.VMEM((low_count, 2 * columns), BF16)],
        coupled_flops,
        coupled_moved,
        per,
    )
    top_input = reduce_and_gather(place, kept, top_far)
    _, forward_columns = factor_apply(place, top_inverse, top_input, 3)

    kept = back_apply(place, top_inverse, forward_columns, 3)
    solution_blocks = reduce_and_gather(place, kept, top_far)
    turned = (columns, chunk)
    gap, rounded = first_columns, []
    for flip in range(2):
        gap, near = call(
            functools.partial(carry_kernel, flip, per),
            place,
            NEAR // per,
            [low_block(0, at, per, flip) for at in range(per)]
            + [in_steps(per, solution_blocks[flip].shape[1:]), whole(gap.shape)],
            [out_whole(gap.shape, F32), in_steps(per, turned, BF16, NEAR)],
            [pltpu.VMEM((2 * columns, low_count), F32), pltpu.VMEM((columns, low_count), F32)],
            [low_blocks] * per + [solution_blocks[flip], gap],
            coupled_flops // 2,
            coupled_moved // 2,
        )
        rounded.append(near)
    top_own = call(
        own_kernel,
        place,
        1,
        [
            pl.BlockSpec(
                (1, *s.shape[1:]), lambda k, p: ((p[3] // chunk // 2) ^ p[1], 0, 0)
            )
            for s in solution_blocks
        ],
        [out_whole((chunk, columns), F32)],
        [],
        list(solution_blocks),
        chunk * columns,
        8 * chunk * columns,
    )[0]
    top_solution = lax.dynamic_slice_in_dim(top_own, top_start % chunk, top_count, 0)
    kept = back_apply(place, low_inverse, gap, 2)
    back_top = call(
        functools.partial(leaf_back_top_kernel, size, per),
        place,
        NEAR // per,
        [leaf_top(0, at, per, flip) for flip in range(2) for at in range(per)]
        + [spread_of(1)]
        + [in_steps(per, turned)] * 2,
        [out_whole((columns, local_rows), F32)],
        [],
        [coupling] * (2 * per) + [spread, *rounded],
        leaf_flops,
        leaf_moved,
    )[0]
    path = reduce_and_gather(place, kept, low_far, True, [back_top, top_own])
    per = 4
    result = back_top
    for flip in range(2):
        last = [forward_leaf, inverse_t] if flip else []
        result = call(
            functools.partial(leaf_back_kernel, size, flip, per),
            place,
            NEAR // per,
            [leaf_low(0, at, per, flip) for at in range(per)]
            + [spread_of(0), in_steps(per, turned), whole(result.shape)]
            + [whole(a.shape) for a in last],
            [out_whole((local_rows, columns) if flip else (columns, local_rows), F32)],
            [pltpu.VMEM((columns, local_rows), F32)],
            [coupling] * per + [spread, path[flip], result, *last],
            leaf_flops // 2,
            leaf_moved // 2,
        )[0]
    return result, top_solution


def solution(mesh):
    return jax.shard_map(
        body,
        mesh=mesh,
        in_specs=(
            P(("leaf", "sep"), None),
            P(("leaf", "sep"), None),
            P(None, None, ("leaf", "sep")),
            P(None, None, ("leaf", "sep")),
            P(("leaf", "sep"), None),
            P(("leaf", "sep"), None),
            P(("leaf", "sep"), None),
            P(("leaf", "sep"), None),
            P(None, ("leaf", "sep")),
        ),
        out_specs=(P(("leaf", "sep"), None), P(("leaf", "sep"), None)),
        check_vma=False,
    )
```

profile of v0, /device:TPU:25, one launch (start us, length us, event | category | flops | bytes accessed | tf_op | source)
XLA Modules:
  0.0 268.7 jit_solution(6874389791501047850)
XLA Ops:
  0.8 4.6 %shard_map.104 = (s16[8,528,128]{2,1,0:T(8,128)(2,1)S(1)}, f32[384,128]{1,0:T(8,128)S(1)}, bf16[384,128]{1,0:T(8,128)(2,1)S(1)}, f32[2,128,384]{2,1,0:T(8,128)S(1)}) custom-call(s32[4]{0:T(128)S(1)} %pad_add_fusion.place, bf16[2,16,512,384]{3,2,1,0:T(8,128)(2,1)} %bitcast.72, bf16[2,16,512,384]{3,2,1,0:T(8,128)(2,1)} %bitcast.73, ...), custom_call_target="tpu_custom_call" | custom-call | flops 402653184 | bytes 3145728 | tf_op jit(solution)/shard_map/pallas_call | solution.py:98
  6.1 2.3 collective-permute-done.rest_7_
  8.4 2.8 %shard_map.106 = (f32[512,128]{1,0:T(8,128)S(1)}, s16[528,128]{1,0:T(8,128)(2,1)S(1)}, s16[528,128]{1,0:T(8,128)(2,1)S(1)}, s16[528,128]{1,0:T(8,128)(2,1)S(1)}) custom-call(s32[4]{0:T(128)S(1)} %pad_add_fusion.place, bf16[2,16,512,384]{3,2,1,0:T(8,128)(2,1)} %bitcast.76, bf16[2,16,512,384]{3,2,1,0:T(8,128)(2,1)} %bitcast.77, ...), custom_call_target="tpu_custom_call" | custom-call | flops 201326592 | bytes 1572864 | tf_op jit(solution)/shard_map/pallas_call | solution.py:98
  13.9 2.9 %shard_map.107 = (s16[528,128]{1,0:T(8,128)(2,1)S(1)}, s16[528,128]{1,0:T(8,128)(2,1)S(1)}, s16[528,128]{1,0:T(8,128)(2,1)S(1)}, s16[528,128]{1,0:T(8,128)(2,1)S(1)}) custom-call(s32[4]{0:T(128)S(1)} %pad_add_fusion.place, bf16[2,16,512,384]{3,2,1,0:T(8,128)(2,1)} %bitcast.80, bf16[2,16,512,384]{3,2,1,0:T(8,128)(2,1)} %bitcast.81, ...), custom_call_target="tpu_custom_call" | custom-call | flops 201326592 | bytes 1572864 | tf_op jit(solution)/shard_map/pallas_call | solution.py:98
  21.6 5.2 %shard_map.105.rest_7_.rest_2_.rest_3_ = f32[16,512,128]{2,1,0:T(8,128)S(1)} custom-call(s32[4]{0:T(128)S(1)} %pad_add_fusion.place, f32[2,128,384]{2,1,0:T(8,128)S(1)} %get-tuple-element.45.spread.rest_4_, bf16[384,128]{1,0:T(8,128)(2,1)S(1)} %get-tuple-element.46.rounded.rest_5_, bf16[2,16,512,384]{3,2,1,0:T(8,128)(2,1)} %bitcast.84), custom_call_target="tpu_custom_call" | custom-call | flops 805306368 | bytes 6291456 | tf_op jit(solution)/shard_map/pallas_call | solution.py:98
  28.4 3.0 %collective-permute-done.4.rest_3_ = s16[528,128]{1,0:T(8,128)(2,1)S(1)} collective-permute-done((s16[528,128]{1,0:T(8,128)(2,1)S(1)}, s16[528,128]{1,0:T(8,128)(2,1)S(1)}, u32[]{:S(2)}, u32[]{:S(2)}) %collective-permute-start.4) | collective-permute-done | bytes 135200 | tf_op jit(solution)/shard_map/ppermute | solution.py:24
  40.7 2.5 collective-permute-done.13
  43.2 3.7 %collective-permute-done.14 = s16[528,128]{1,0:T(8,128)(2,1)S(1)} collective-permute-done((s16[528,128]{1,0:T(8,128)(2,1)S(1)}, s16[528,128]{1,0:T(8,128)(2,1)S(1)}, u32[]{:S(2)}, u32[]{:S(2)}) %collective-permute-start.14) | collective-permute-done | bytes 135200 | tf_op jit(solution)/shard_map/ppermute | solution.py:24
  46.9 3.4 %collective-permute-start.15 = (s16[8,528,128]{2,1,0:T(8,128)(2,1)S(1)}, s16[8,528,128]{2,1,0:T(8,128)(2,1)S(1)}, u32[]{:S(2)}, u32[]{:S(2)}) collective-permute-start(s16[8,528,128]{2,1,0:T(8,128)(2,1)S(1)} %bitcast_dynamic-update-slice_fusion.16.rest_2_), channel_id=1, source_target_pairs={{0,1},{1,0},{2,3},{3,2},{4,5},{5,4},{6,7},{7,6},{8,9},{9,8},{10,11... | collective-permute-start | bytes 3244040 | tf_op jit(solution)/shard_map/ppermute | solution.py:24
  50.3 6.2 %shard_map.109.rest_3_ = f32[512,128]{1,0:T(8,128)S(1)} custom-call(s32[4]{0:T(128)S(1)} %pad_add_fusion.place, f32[512,8192]{1,0:T(8,128)} %rest_1_.19, f32[512,8192]{1,0:T(8,128)} %rest_1_.19, s16[8,528,128]{2,1,0:T(8,128)(2,1)S(1)} %bitcast_dynamic-update-slice_fusion.16.rest_2_), custom_call_target="tpu_custom_call" | custom-call | flops 2147483648 | bytes 8388608 | tf_op jit(solution)/shard_map/pallas_call | solution.py:98
  56.5 6.3 %shard_map.110 = (f32[512,128]{1,0:T(8,128)S(1)}, f32[128,512]{1,0:T(8,128)S(1)}) custom-call(s32[4]{0:T(128)S(1)} %pad_add_fusion.place, f32[512,8192]{1,0:T(8,128)} %rest_1_.19, f32[512,8192]{1,0:T(8,128)} %rest_1_.19, s16[8,528,128]{2,1,0:T(8,128)(2,1)S(1)} %collective-permute-done.15.rest_2_, f32[512,128]{1,0:T(8,128)S(1)} %shard_map.109.rest_3_), custom_call_target="tpu_custom_call" | custom-call | flops 2147483648 | bytes 8388608 | tf_op jit(solution)/shard_map/pallas_call | solution.py:98
  62.8 6.5 %shard_map.111 = s16[8,528,128]{2,1,0:T(8,128)(2,1)S(1)} custom-call(s32[4]{0:T(128)S(1)} %pad_add_fusion.place, f32[16,512,512]{2,1,0:T(8,128)} %bitcast.97, f32[16,512,512]{2,1,0:T(8,128)} %bitcast.98, f32[16,512,128]{2,1,0:T(8,128)S(1)} %shard_map.105.rest_7_.rest_2_.rest_3_, f32[16,512,128]{2,1,0:T(8,128)S(1)} %shard_map.105.rest_7_.rest_2_.rest_3_, ...), custom_call_target="tpu_custom_call" | custom-call | flops 2147483648 | bytes 8388608 | tf_op jit(solution)/shard_map/pallas_call | solution.py:98
  69.5 2.7 collective-permute-done.16.rest_6_
  72.1 4.5 %shard_map.113 = (s16[528,128]{1,0:T(8,128)(2,1)S(1)}, s16[528,128]{1,0:T(8,128)(2,1)S(1)}, s16[528,128]{1,0:T(8,128)(2,1)S(1)}, s16[528,128]{1,0:T(8,128)(2,1)S(1)}) custom-call(s32[4]{0:T(128)S(1)} %pad_add_fusion.place, f32[16,512,512]{2,1,0:T(8,128)} %bitcast.99, f32[16,512,512]{2,1,0:T(8,128)} %bitcast.100, ...), custom_call_target="tpu_custom_call" | custom-call | flops 1073741824 | bytes 4194304 | tf_op jit(solution)/shard_map/pallas_call | solution.py:98
  81.4 4.6 %shard_map.112 = (f32[512,128]{1,0:T(8,128)S(1)}, s16[528,128]{1,0:T(8,128)(2,1)S(1)}, s16[528,128]{1,0:T(8,128)(2,1)S(1)}, s16[528,128]{1,0:T(8,128)(2,1)S(1)}) custom-call(s32[4]{0:T(128)S(1)} %pad_add_fusion.place, f32[16,512,512]{2,1,0:T(8,128)} %bitcast.101, f32[16,512,512]{2,1,0:T(8,128)} %bitcast.102, ...), custom_call_target="tpu_custom_call" | custom-call | flops 1073741824 | bytes 4194304 | tf_op jit(solution)/shard_map/pallas_call | solution.py:98
  92.4 3.2 %collective-permute-done.22.rest_5_ = s16[528,128]{1,0:T(8,128)(2,1)S(1)} collective-permute-done((s16[528,128]{1,0:T(8,128)(2,1)S(1)}, s16[528,128]{1,0:T(8,128)(2,1)S(1)}, u32[]{:S(2)}, u32[]{:S(2)}) %collective-permute-start.22) | collective-permute-done | bytes 135200 | tf_op jit(solution)/shard_map/ppermute | solution.py:24
  96.7 9.2 %collective-permute-done.24.rest_0_ = s16[528,128]{1,0:T(8,128)(2,1)S(1)} collective-permute-done((s16[528,128]{1,0:T(8,128)(2,1)S(1)}, s16[528,128]{1,0:T(8,128)(2,1)S(1)}, u32[]{:S(2)}, u32[]{:S(2)}) %collective-permute-start.24) | collective-permute-done | bytes 135200 | tf_op jit(solution)/shard_map/ppermute | solution.py:24
  107.0 2.3 collective-permute-start.27
  111.2 3.0 %collective-permute-start.31 = (s16[528,128]{1,0:T(8,128)(2,1)S(1)}, s16[528,128]{1,0:T(8,128)(2,1)S(1)}, u32[]{:S(2)}, u32[]{:S(2)}) collective-permute-start(s16[528,128]{1,0:T(8,128)(2,1)S(1)} %shard_map.115), channel_id=1, source_target_pairs={{0,14},{1,15},{2,12},{3,13},{4,10},{5,11},{6,8},{7,9},{8,6},{9,7},... | collective-permute-start | bytes 405512 | tf_op jit(solution)/shard_map/ppermute | solution.py:24
  115.3 2.8 %collective-permute-done.30 = s16[528,128]{1,0:T(8,128)(2,1)S(1)} collective-permute-done((s16[528,128]{1,0:T(8,128)(2,1)S(1)}, s16[528,128]{1,0:T(8,128)(2,1)S(1)}, u32[]{:S(2)}, u32[]{:S(2)}) %collective-permute-start.30) | collective-permute-done | bytes 135200 | tf_op jit(solution)/shard_map/ppermute | solution.py:24
  118.1 2.8 %collective-permute-done.31 = s16[528,128]{1,0:T(8,128)(2,1)S(1)} collective-permute-done((s16[528,128]{1,0:T(8,128)(2,1)S(1)}, s16[528,128]{1,0:T(8,128)(2,1)S(1)}, u32[]{:S(2)}, u32[]{:S(2)}) %collective-permute-start.31) | collective-permute-done | bytes 135200 | tf_op jit(solution)/shard_map/ppermute | solution.py:24
  121.0 3.0 %collective-permute-start.32 = (s16[8,528,128]{2,1,0:T(8,128)(2,1)S(1)}, s16[8,528,128]{2,1,0:T(8,128)(2,1)S(1)}, u32[]{:S(2)}, u32[]{:S(2)}) collective-permute-start(s16[8,528,128]{2,1,0:T(8,128)(2,1)S(1)} %bitcast_dynamic-update-slice_fusion.8.rest_2_), channel_id=1, source_target_pairs={{0,1},{1,0},{2,3},{3,2},{4,5},{5,4},{6,7},{7,6},{8,9},{9,8},{10,11... | collective-permute-start | bytes 3244040 | tf_op jit(solution)/shard_map/ppermute | solution.py:24
  123.9 4.6 %shard_map.116.rest_3_ = f32[256,128]{1,0:T(8,128)S(1)} custom-call(s32[4]{0:T(128)S(1)} %pad_add_fusion.place, f32[256,8192]{1,0:T(8,128)} %rest_1_.16, f32[256,8192]{1,0:T(8,128)} %rest_1_.16, s16[8,528,128]{2,1,0:T(8,128)(2,1)S(1)} %bitcast_dynamic-update-slice_fusion.8.rest_2_), custom_call_target="tpu_custom_call" | custom-call | flops 1073741824 | bytes 4194304 | tf_op jit(solution)/shard_map/pallas_call | solution.py:98
  128.6 5.3 %shard_map.117 = (f32[256,128]{1,0:T(8,128)}, f32[128,256]{1,0:T(8,128)S(1)}) custom-call(s32[4]{0:T(128)S(1)} %pad_add_fusion.place, f32[256,8192]{1,0:T(8,128)} %rest_1_.16, f32[256,8192]{1,0:T(8,128)} %rest_1_.16, s16[8,528,128]{2,1,0:T(8,128)(2,1)S(1)} %collective-permute-done.32.rest_2_, f32[256,128]{1,0:T(8,128)S(1)} %shard_map.116.rest_3_), custom_call_target="tpu_custom_call" | custom-call | flops 1073741824 | bytes 4194304 | tf_op jit(solution)/shard_map/pallas_call | solution.py:98
  133.9 4.7 %shard_map.118 = s16[8,144,512]{2,1,0:T(8,128)(2,1)S(1)} custom-call(s32[4]{0:T(128)S(1)} %pad_add_fusion.place, f32[256,8192]{1,0:T(8,128)} %rest_1_.16, f32[256,8192]{1,0:T(8,128)} %rest_1_.16, f32[128,256]{1,0:T(8,128)S(1)} %get-tuple-element.65.rest_2_), custom_call_target="tpu_custom_call" | custom-call | flops 1073741824 | bytes 4194304 | tf_op jit(solution)/shard_map/pallas_call | solution.py:98
  138.7 2.8 %collective-permute-done.33.rest_3_ = s16[8,144,512]{2,1,0:T(8,128)(2,1)S(1)} collective-permute-done((s16[8,144,512]{2,1,0:T(8,128)(2,1)S(1)}, s16[8,144,512]{2,1,0:T(8,128)(2,1)S(1)}, u32[]{:S(2)}, u32[]{:S(2)}) %collective-permute-start.33) | collective-permute-done | bytes 1179680 | tf_op jit(solution)/shard_map/ppermute | solution.py:24
  141.5 3.5 %shard_map.120 = (s16[144,512]{1,0:T(8,128)(2,1)S(1)}, s16[144,512]{1,0:T(8,128)(2,1)S(1)}, s16[144,512]{1,0:T(8,128)(2,1)S(1)}, s16[144,512]{1,0:T(8,128)(2,1)S(1)}) custom-call(s32[4]{0:T(128)S(1)} %pad_add_fusion.place, f32[256,8192]{1,0:T(8,128)} %rest_1_.16, f32[256,8192]{1,0:T(8,128)} %rest_1_.16, f32[128,256]{1,0:T(8,128)S(1)} %get-tuple-element.65.rest_2_, ...), custom_call_target="tpu_custom_call" | custom-call | flops 536870912 | bytes 2097152 | tf_op jit(solution)/shard_map/pallas_call | solution.py:98
  149.8 3.5 %shard_map.119 = (f32[128,512]{1,0:T(8,128)S(1)}, s16[144,512]{1,0:T(8,128)(2,1)S(1)}, s16[144,512]{1,0:T(8,128)(2,1)S(1)}, s16[144,512]{1,0:T(8,128)(2,1)S(1)}) custom-call(s32[4]{0:T(128)S(1)} %pad_add_fusion.place, f32[256,8192]{1,0:T(8,128)} %rest_1_.16, f32[256,8192]{1,0:T(8,128)} %rest_1_.16, f32[128,256]{1,0:T(8,128)S(1)} %get-tuple-element.65.rest_2_, ...), custom_call_target="tpu_custom_call" | custom-call | flops 536870912 | bytes 2097152 | tf_op jit(solution)/shard_map/pallas_call | solution.py:98
  153.3 2.3 collective-permute-start.38
  156.4 3.2 %collective-permute-done.36.rest_2_ = s16[144,512]{1,0:T(8,128)(2,1)S(1)} collective-permute-done((s16[144,512]{1,0:T(8,128)(2,1)S(1)}, s16[144,512]{1,0:T(8,128)(2,1)S(1)}, u32[]{:S(2)}, u32[]{:S(2)}) %collective-permute-start.36) | collective-permute-done | bytes 147488 | tf_op jit(solution)/shard_map/ppermute | solution.py:24
  162.7 3.3 %collective-permute-done.40.rest_6_ = s16[144,512]{1,0:T(8,128)(2,1)S(1)} collective-permute-done((s16[144,512]{1,0:T(8,128)(2,1)S(1)}, s16[144,512]{1,0:T(8,128)(2,1)S(1)}, u32[]{:S(2)}, u32[]{:S(2)}) %collective-permute-start.40) | collective-permute-done | bytes 147488 | tf_op jit(solution)/shard_map/ppermute | solution.py:24
  167.2 9.8 %collective-permute-done.41.rest_0_ = s16[144,512]{1,0:T(8,128)(2,1)S(1)} collective-permute-done((s16[144,512]{1,0:T(8,128)(2,1)S(1)}, s16[144,512]{1,0:T(8,128)(2,1)S(1)}, u32[]{:S(2)}, u32[]{:S(2)}) %collective-permute-start.41) | collective-permute-done | bytes 147488 | tf_op jit(solution)/shard_map/ppermute | solution.py:24
  187.9 2.6 collective-permute-done.47
  190.6 3.0 %collective-permute-done.48 = s16[144,512]{1,0:T(8,128)(2,1)S(1)} collective-permute-done((s16[144,512]{1,0:T(8,128)(2,1)S(1)}, s16[144,512]{1,0:T(8,128)(2,1)S(1)}, u32[]{:S(2)}, u32[]{:S(2)}) %collective-permute-start.48) | collective-permute-done | bytes 147488 | tf_op jit(solution)/shard_map/ppermute | solution.py:24
  193.6 2.7 collective-permute-start.49
  196.3 6.0 %shard_map.123 = (f32[128,512]{1,0:T(8,128)S(1)}, bf16[8,128,512]{2,1,0:T(8,128)(2,1)S(1)}) custom-call(s32[4]{0:T(128)S(1)} %pad_add_fusion.place, f32[16,512,512]{2,1,0:T(8,128)} %bitcast.103, f32[16,512,512]{2,1,0:T(8,128)} %bitcast.104, s16[8,144,512]{2,1,0:T(8,128)(2,1)S(1)} %bitcast_dynamic-update-slice_fusion.rest_2_.mine, ...), custom_call_target="tpu_custom_call" | custom-call | flops 2147483648 | bytes 8388608 | tf_op jit(solution)/shard_map/pallas_call | solution.py:98
  202.3 6.0 %shard_map.124 = (f32[128,512]{1,0:T(8,128)S(1)}, bf16[8,128,512]{2,1,0:T(8,128)(2,1)S(1)}) custom-call(s32[4]{0:T(128)S(1)} %pad_add_fusion.place, f32[16,512,512]{2,1,0:T(8,128)} %bitcast.105, f32[16,512,512]{2,1,0:T(8,128)} %bitcast.106, s16[8,144,512]{2,1,0:T(8,128)(2,1)S(1)} %collective-permute-done.49.rest_2_.other, ...), custom_call_target="tpu_custom_call" | custom-call | flops 2147483648 | bytes 8388608 | tf_op jit(solution)/shard_map/pallas_call | solution.py:98
  208.3 6.5 %shard_map.125 = s16[8,144,512]{2,1,0:T(8,128)(2,1)S(1)} custom-call(s32[4]{0:T(128)S(1)} %pad_add_fusion.place, f32[512,8192]{1,0:T(8,128)} %rest_1_.19, f32[512,8192]{1,0:T(8,128)} %rest_1_.19, f32[128,512]{1,0:T(8,128)S(1)} %get-tuple-element.76.rest_2_), custom_call_target="tpu_custom_call" | custom-call | flops 2147483648 | bytes 8388608 | tf_op jit(solution)/shard_map/pallas_call | solution.py:98
  214.9 2.8 %collective-permute-done.50.rest_3_ = s16[8,144,512]{2,1,0:T(8,128)(2,1)S(1)} collective-permute-done((s16[8,144,512]{2,1,0:T(8,128)(2,1)S(1)}, s16[8,144,512]{2,1,0:T(8,128)(2,1)S(1)}, u32[]{:S(2)}, u32[]{:S(2)}) %collective-permute-start.50) | collective-permute-done | bytes 1179680 | tf_op jit(solution)/shard_map/ppermute | solution.py:24
  217.7 4.4 %shard_map.127 = (s16[144,512]{1,0:T(8,128)(2,1)S(1)}, s16[144,512]{1,0:T(8,128)(2,1)S(1)}, s16[144,512]{1,0:T(8,128)(2,1)S(1)}, s16[144,512]{1,0:T(8,128)(2,1)S(1)}) custom-call(s32[4]{0:T(128)S(1)} %pad_add_fusion.place, f32[512,8192]{1,0:T(8,128)} %rest_1_.19, f32[512,8192]{1,0:T(8,128)} %rest_1_.19, f32[128,512]{1,0:T(8,128)S(1)} %get-tuple-element.76.rest_2_, ...), custom_call_target="tpu_custom_call" | custom-call | flops 1073741824 | bytes 4194304 | tf_op jit(solution)/shard_map/pallas_call | solution.py:98
  226.9 4.6 %shard_map.126 = (f32[128,512]{1,0:T(8,128)S(1)}, s16[144,512]{1,0:T(8,128)(2,1)S(1)}, s16[144,512]{1,0:T(8,128)(2,1)S(1)}, s16[144,512]{1,0:T(8,128)(2,1)S(1)}) custom-call(s32[4]{0:T(128)S(1)} %pad_add_fusion.place, f32[512,8192]{1,0:T(8,128)} %rest_1_.19, f32[512,8192]{1,0:T(8,128)} %rest_1_.19, f32[128,512]{1,0:T(8,128)S(1)} %get-tuple-element.76.rest_2_, ...), custom_call_target="tpu_custom_call" | custom-call | flops 1073741824 | bytes 4194304 | tf_op jit(solution)/shard_map/pallas_call | solution.py:98
  235.0 4.9 %shard_map.128.rest_7_.rest_6_ = f32[128,384]{1,0:T(8,128)S(1)} custom-call(s32[4]{0:T(128)S(1)} %pad_add_fusion.place, bf16[2,16,512,384]{3,2,1,0:T(8,128)(2,1)} %bitcast.85, bf16[2,16,512,384]{3,2,1,0:T(8,128)(2,1)} %bitcast.86, bf16[2,16,512,384]{3,2,1,0:T(8,128)(2,1)} %bitcast.87, bf16[2,16,512,384]{3,2,1,0:T(8,128)(2,1)} %bitcast.88, ...), custom_call_target="tpu_custom_call" | custom-call | flops 805306368 | bytes 6291456 | tf_op jit(solution)/shard_map/pallas_call | solution.py:98
  248.8 2.5 collective-permute-start.64
  252.7 2.7 %collective-permute-done.63 = bf16[128,512]{1,0:T(8,128)(2,1)S(1)} collective-permute-done((bf16[128,512]{1,0:T(8,128)(2,1)S(1)}, bf16[128,512]{1,0:T(8,128)(2,1)S(1)}, u32[]{:S(2)}, u32[]{:S(2)}) %collective-permute-start.63) | collective-permute-done | bytes 131104 | tf_op jit(solution)/shard_map/ppermute | solution.py:24
  255.4 2.3 collective-permute-done.64
  257.7 3.0 %collective-permute-start.65 = (bf16[8,128,512]{2,1,0:T(8,128)(2,1)S(1)}, bf16[8,128,512]{2,1,0:T(8,128)(2,1)S(1)}, u32[]{:S(2)}, u32[]{:S(2)}) collective-permute-start(bf16[8,128,512]{2,1,0:T(8,128)(2,1)S(1)} %bitcast_dynamic-update-slice_fusion.24.rest_5_), channel_id=1, source_target_pairs={{0,1},{1,0},{2,3},{3,2},{4,5},{5,4},{6,7},{7,6},{8,9},{9,8},{10,11... | collective-permute-start | bytes 3145736 | tf_op jit(solution)/shard_map/ppermute | solution.py:24
  261.4 2.9 %shard_map.131.rest_6_ = f32[128,384]{1,0:T(8,128)S(1)} custom-call(s32[4]{0:T(128)S(1)} %pad_add_fusion.place, bf16[2,16,512,384]{3,2,1,0:T(8,128)(2,1)} %bitcast.89, bf16[2,16,512,384]{3,2,1,0:T(8,128)(2,1)} %bitcast.90, bf16[2,16,512,384]{3,2,1,0:T(8,128)(2,1)} %bitcast.91, bf16[2,16,512,384]{3,2,1,0:T(8,128)(2,1)} %bitcast.92, ...), custom_call_target="tpu_custom_call" | custom-call | flops 402653184 | bytes 3145728 | tf_op jit(solution)/shard_map/pallas_call | solution.py:98
  264.4 4.3 %shard_map.132 = f32[384,128]{1,0:T(8,128)} custom-call(s32[4]{0:T(128)S(1)} %pad_add_fusion.place, bf16[2,16,512,384]{3,2,1,0:T(8,128)(2,1)} %bitcast.93, bf16[2,16,512,384]{3,2,1,0:T(8,128)(2,1)} %bitcast.94, bf16[2,16,512,384]{3,2,1,0:T(8,128)(2,1)} %bitcast.95, bf16[2,16,512,384]{3,2,1,0:T(8,128)(2,1)} %bitcast.96, ...), custom_call_target="tpu_custom_call" | custom-call | flops 402653184 | bytes 3145728 | tf_op jit(solution)/shard_map/pallas_call | solution.py:98
  (147 shorter events, 75.8 us)
Async XLA Ops:
  11.2 9.0 %collective-permute-start.5 = (s16[528,128]{1,0:T(8,128)(2,1)S(1)}, s16[528,128]{1,0:T(8,128)(2,1)S(1)}, u32[]{:S(2)}, u32[]{:S(2)}) collective-permute-start(s16[528,128]{1,0:T(8,128)(2,1)S(1)} %get-tuple-element.53), channel_id=1, source_target_pairs={{0,6},{1,7},{2,4},{3,5},{4,2},{5,3},{6,0},{7,1},{8,14},{9,15},{10,... | collective-permute-start | bytes 405512 | tf_op jit(solution)/shard_map/ppermute | solution.py:24
  13.4 7.1 %collective-permute-start.6 = (s16[528,128]{1,0:T(8,128)(2,1)S(1)}, s16[528,128]{1,0:T(8,128)(2,1)S(1)}, u32[]{:S(2)}, u32[]{:S(2)}) collective-permute-start(s16[528,128]{1,0:T(8,128)(2,1)S(1)} %get-tuple-element.54), channel_id=1, source_target_pairs={{0,4},{1,5},{2,6},{3,7},{4,0},{5,1},{6,2},{7,3},{8,12},{9,13},{10,... | collective-permute-start | bytes 405512 | tf_op jit(solution)/shard_map/ppermute | solution.py:24
  13.7 13.2 %collective-permute-start.7 = (s16[528,128]{1,0:T(8,128)(2,1)S(1)}, s16[528,128]{1,0:T(8,128)(2,1)S(1)}, u32[]{:S(2)}, u32[]{:S(2)}) collective-permute-start(s16[528,128]{1,0:T(8,128)(2,1)S(1)} %get-tuple-element.55), channel_id=1, source_target_pairs={{0,2},{1,3},{2,0},{3,1},{4,6},{5,7},{6,4},{7,5},{8,10},{9,11},{10,... | collective-permute-start | bytes 405512 | tf_op jit(solution)/shard_map/ppermute | solution.py:24
  16.8 10.1 %collective-permute-start.1 = (s16[528,128]{1,0:T(8,128)(2,1)S(1)}, s16[528,128]{1,0:T(8,128)(2,1)S(1)}, u32[]{:S(2)}, u32[]{:S(2)}) collective-permute-start(s16[528,128]{1,0:T(8,128)(2,1)S(1)} %get-tuple-element.49), channel_id=1, source_target_pairs={{0,14},{1,15},{2,12},{3,13},{4,10},{5,11},{6,8},{7,9},{8,6},{9,7},... | collective-permute-start | bytes 405512 | tf_op jit(solution)/shard_map/ppermute | solution.py:24
  18.9 7.9 %collective-permute-start.2 = (s16[528,128]{1,0:T(8,128)(2,1)S(1)}, s16[528,128]{1,0:T(8,128)(2,1)S(1)}, u32[]{:S(2)}, u32[]{:S(2)}) collective-permute-start(s16[528,128]{1,0:T(8,128)(2,1)S(1)} %get-tuple-element.50), channel_id=1, source_target_pairs={{0,12},{1,13},{2,14},{3,15},{4,8},{5,9},{6,10},{7,11},{8,4},{9,5},... | collective-permute-start | bytes 405512 | tf_op jit(solution)/shard_map/ppermute | solution.py:24
  20.2 8.2 %collective-permute-start.3 = (s16[528,128]{1,0:T(8,128)(2,1)S(1)}, s16[528,128]{1,0:T(8,128)(2,1)S(1)}, u32[]{:S(2)}, u32[]{:S(2)}) collective-permute-start(s16[528,128]{1,0:T(8,128)(2,1)S(1)} %get-tuple-element.51), channel_id=1, source_target_pairs={{0,10},{1,11},{2,8},{3,9},{4,14},{5,15},{6,12},{7,13},{8,2},{9,3},... | collective-permute-start | bytes 405512 | tf_op jit(solution)/shard_map/ppermute | solution.py:24
  20.6 10.8 %collective-permute-start.4 = (s16[528,128]{1,0:T(8,128)(2,1)S(1)}, s16[528,128]{1,0:T(8,128)(2,1)S(1)}, u32[]{:S(2)}, u32[]{:S(2)}) collective-permute-start(s16[528,128]{1,0:T(8,128)(2,1)S(1)} %get-tuple-element.52), channel_id=1, source_target_pairs={{0,8},{1,9},{2,10},{3,11},{4,12},{5,13},{6,14},{7,15},{8,0},{9,1},... | collective-permute-start | bytes 405512 | tf_op jit(solution)/shard_map/ppermute | solution.py:24
  32.9 7.1 %collective-permute-start.10 = (s16[528,128]{1,0:T(8,128)(2,1)S(1)}, s16[528,128]{1,0:T(8,128)(2,1)S(1)}, u32[]{:S(2)}, u32[]{:S(2)}) collective-permute-start(s16[528,128]{1,0:T(8,128)(2,1)S(1)} %shard_map.108), channel_id=1, source_target_pairs={{0,6},{1,7},{2,4},{3,5},{4,2},{5,3},{6,0},{7,1},{8,14},{9,15},{10,... | collective-permute-start | bytes 405512 | tf_op jit(solution)/shard_map/ppermute | solution.py:24
  36.5 6.7 %collective-permute-start.13 = (s16[528,128]{1,0:T(8,128)(2,1)S(1)}, s16[528,128]{1,0:T(8,128)(2,1)S(1)}, u32[]{:S(2)}, u32[]{:S(2)}) collective-permute-start(s16[528,128]{1,0:T(8,128)(2,1)S(1)} %shard_map.108), channel_id=1, source_target_pairs={{0,12},{1,13},{2,14},{3,15},{4,8},{5,9},{6,10},{7,11},{8,4},{9,5},... | collective-permute-start | bytes 405512 | tf_op jit(solution)/shard_map/ppermute | solution.py:24
  38.2 8.7 %collective-permute-start.14 = (s16[528,128]{1,0:T(8,128)(2,1)S(1)}, s16[528,128]{1,0:T(8,128)(2,1)S(1)}, u32[]{:S(2)}, u32[]{:S(2)}) collective-permute-start(s16[528,128]{1,0:T(8,128)(2,1)S(1)} %shard_map.108), channel_id=1, source_target_pairs={{0,14},{1,15},{2,12},{3,13},{4,10},{5,11},{6,8},{7,9},{8,6},{9,7},... | collective-permute-start | bytes 405512 | tf_op jit(solution)/shard_map/ppermute | solution.py:24
  46.9 9.6 %collective-permute-start.15 = (s16[8,528,128]{2,1,0:T(8,128)(2,1)S(1)}, s16[8,528,128]{2,1,0:T(8,128)(2,1)S(1)}, u32[]{:S(2)}, u32[]{:S(2)}) collective-permute-start(s16[8,528,128]{2,1,0:T(8,128)(2,1)S(1)} %bitcast_dynamic-update-slice_fusion.16.rest_2_), channel_id=1, source_target_pairs={{0,1},{1,0},{2,3},{3,2},{4,5},{5,4},{6,7},{7,6},{8,9},{9,8},{10,11... | collective-permute-start | bytes 3244040 | tf_op jit(solution)/shard_map/ppermute | solution.py:24
  76.6 11.2 %collective-permute-start.17 = (s16[528,128]{1,0:T(8,128)(2,1)S(1)}, s16[528,128]{1,0:T(8,128)(2,1)S(1)}, u32[]{:S(2)}, u32[]{:S(2)}) collective-permute-start(s16[528,128]{1,0:T(8,128)(2,1)S(1)} %get-tuple-element.58), channel_id=1, source_target_pairs={{0,14},{1,15},{2,12},{3,13},{4,10},{5,11},{6,8},{7,9},{8,6},{9,7},... | collective-permute-start | bytes 405512 | tf_op jit(solution)/shard_map/ppermute | solution.py:24
  78.5 9.8 %collective-permute-start.18 = (s16[528,128]{1,0:T(8,128)(2,1)S(1)}, s16[528,128]{1,0:T(8,128)(2,1)S(1)}, u32[]{:S(2)}, u32[]{:S(2)}) collective-permute-start(s16[528,128]{1,0:T(8,128)(2,1)S(1)} %get-tuple-element.59), channel_id=1, source_target_pairs={{0,12},{1,13},{2,14},{3,15},{4,8},{5,9},{6,10},{7,11},{8,4},{9,5},... | collective-permute-start | bytes 405512 | tf_op jit(solution)/shard_map/ppermute | solution.py:24
  79.7 10.1 %collective-permute-start.19 = (s16[528,128]{1,0:T(8,128)(2,1)S(1)}, s16[528,128]{1,0:T(8,128)(2,1)S(1)}, u32[]{:S(2)}, u32[]{:S(2)}) collective-permute-start(s16[528,128]{1,0:T(8,128)(2,1)S(1)} %get-tuple-element.60), channel_id=1, source_target_pairs={{0,10},{1,11},{2,8},{3,9},{4,14},{5,15},{6,12},{7,13},{8,2},{9,3},... | collective-permute-start | bytes 405512 | tf_op jit(solution)/shard_map/ppermute | solution.py:24
  80.7 11.2 %collective-permute-start.20 = (s16[528,128]{1,0:T(8,128)(2,1)S(1)}, s16[528,128]{1,0:T(8,128)(2,1)S(1)}, u32[]{:S(2)}, u32[]{:S(2)}) collective-permute-start(s16[528,128]{1,0:T(8,128)(2,1)S(1)} %get-tuple-element.61), channel_id=1, source_target_pairs={{0,8},{1,9},{2,10},{3,11},{4,12},{5,13},{6,14},{7,15},{8,0},{9,1},... | collective-permute-start | bytes 405512 | tf_op jit(solution)/shard_map/ppermute | solution.py:24
  86.0 6.4 %collective-permute-start.21 = (s16[528,128]{1,0:T(8,128)(2,1)S(1)}, s16[528,128]{1,0:T(8,128)(2,1)S(1)}, u32[]{:S(2)}, u32[]{:S(2)}) collective-permute-start(s16[528,128]{1,0:T(8,128)(2,1)S(1)} %get-tuple-element.62), channel_id=1, source_target_pairs={{0,6},{1,7},{2,4},{3,5},{4,2},{5,3},{6,0},{7,1},{8,14},{9,15},{10,... | collective-permute-start | bytes 405512 | tf_op jit(solution)/shard_map/ppermute | solution.py:24
  87.8 7.8 %collective-permute-start.22 = (s16[528,128]{1,0:T(8,128)(2,1)S(1)}, s16[528,128]{1,0:T(8,128)(2,1)S(1)}, u32[]{:S(2)}, u32[]{:S(2)}) collective-permute-start(s16[528,128]{1,0:T(8,128)(2,1)S(1)} %get-tuple-element.63), channel_id=1, source_target_pairs={{0,4},{1,5},{2,6},{3,7},{4,0},{5,1},{6,2},{7,3},{8,12},{9,13},{10,... | collective-permute-start | bytes 405512 | tf_op jit(solution)/shard_map/ppermute | solution.py:24
  88.2 7.3 %collective-permute-start.23 = (s16[528,128]{1,0:T(8,128)(2,1)S(1)}, s16[528,128]{1,0:T(8,128)(2,1)S(1)}, u32[]{:S(2)}, u32[]{:S(2)}) collective-permute-start(s16[528,128]{1,0:T(8,128)(2,1)S(1)} %get-tuple-element.64), channel_id=1, source_target_pairs={{0,2},{1,3},{2,0},{3,1},{4,6},{5,7},{6,4},{7,5},{8,10},{9,11},{10,... | collective-permute-start | bytes 405512 | tf_op jit(solution)/shard_map/ppermute | solution.py:24
  96.6 9.3 %collective-permute-start.24 = (s16[528,128]{1,0:T(8,128)(2,1)S(1)}, s16[528,128]{1,0:T(8,128)(2,1)S(1)}, u32[]{:S(2)}, u32[]{:S(2)}) collective-permute-start(s16[528,128]{1,0:T(8,128)(2,1)S(1)} %shard_map.114.own), channel_id=1, source_target_pairs={{0,16},{1,17},{2,18},{3,19},{4,20},{5,21},{6,22},{7,23},{8,24},{9,... | collective-permute-start | bytes 405512 | tf_op jit(solution)/shard_map/ppermute | solution.py:24
  107.0 7.7 %collective-permute-start.27 = (s16[528,128]{1,0:T(8,128)(2,1)S(1)}, s16[528,128]{1,0:T(8,128)(2,1)S(1)}, u32[]{:S(2)}, u32[]{:S(2)}) collective-permute-start(s16[528,128]{1,0:T(8,128)(2,1)S(1)} %shard_map.115), channel_id=1, source_target_pairs={{0,6},{1,7},{2,4},{3,5},{4,2},{5,3},{6,0},{7,1},{8,14},{9,15},{10,... | collective-permute-start | bytes 405512 | tf_op jit(solution)/shard_map/ppermute | solution.py:24
  111.2 6.9 %collective-permute-start.30 = (s16[528,128]{1,0:T(8,128)(2,1)S(1)}, s16[528,128]{1,0:T(8,128)(2,1)S(1)}, u32[]{:S(2)}, u32[]{:S(2)}) collective-permute-start(s16[528,128]{1,0:T(8,128)(2,1)S(1)} %shard_map.115), channel_id=1, source_target_pairs={{0,12},{1,13},{2,14},{3,15},{4,8},{5,9},{6,10},{7,11},{8,4},{9,5},... | collective-permute-start | bytes 405512 | tf_op jit(solution)/shard_map/ppermute | solution.py:24
  111.2 9.7 %collective-permute-start.31 = (s16[528,128]{1,0:T(8,128)(2,1)S(1)}, s16[528,128]{1,0:T(8,128)(2,1)S(1)}, u32[]{:S(2)}, u32[]{:S(2)}) collective-permute-start(s16[528,128]{1,0:T(8,128)(2,1)S(1)} %shard_map.115), channel_id=1, source_target_pairs={{0,14},{1,15},{2,12},{3,13},{4,10},{5,11},{6,8},{7,9},{8,6},{9,7},... | collective-permute-start | bytes 405512 | tf_op jit(solution)/shard_map/ppermute | solution.py:24
  121.0 7.6 %collective-permute-start.32 = (s16[8,528,128]{2,1,0:T(8,128)(2,1)S(1)}, s16[8,528,128]{2,1,0:T(8,128)(2,1)S(1)}, u32[]{:S(2)}, u32[]{:S(2)}) collective-permute-start(s16[8,528,128]{2,1,0:T(8,128)(2,1)S(1)} %bitcast_dynamic-update-slice_fusion.8.rest_2_), channel_id=1, source_target_pairs={{0,1},{1,0},{2,3},{3,2},{4,5},{5,4},{6,7},{7,6},{8,9},{9,8},{10,11... | collective-permute-start | bytes 3244040 | tf_op jit(solution)/shard_map/ppermute | solution.py:24
  145.0 10.6 %collective-permute-start.34 = (s16[144,512]{1,0:T(8,128)(2,1)S(1)}, s16[144,512]{1,0:T(8,128)(2,1)S(1)}, u32[]{:S(2)}, u32[]{:S(2)}) collective-permute-start(s16[144,512]{1,0:T(8,128)(2,1)S(1)} %get-tuple-element.67), channel_id=1, source_target_pairs={{0,14},{1,15},{2,12},{3,13},{4,10},{5,11},{6,8},{7,9},{8,6},{9,7},... | collective-permute-start | bytes 442376 | tf_op jit(solution)/shard_map/ppermute | solution.py:24
  147.1 8.6 %collective-permute-start.35 = (s16[144,512]{1,0:T(8,128)(2,1)S(1)}, s16[144,512]{1,0:T(8,128)(2,1)S(1)}, u32[]{:S(2)}, u32[]{:S(2)}) collective-permute-start(s16[144,512]{1,0:T(8,128)(2,1)S(1)} %get-tuple-element.68), channel_id=1, source_target_pairs={{0,12},{1,13},{2,14},{3,15},{4,8},{5,9},{6,10},{7,11},{8,4},{9,5},... | collective-permute-start | bytes 442376 | tf_op jit(solution)/shard_map/ppermute | solution.py:24
  148.2 11.3 %collective-permute-start.36 = (s16[144,512]{1,0:T(8,128)(2,1)S(1)}, s16[144,512]{1,0:T(8,128)(2,1)S(1)}, u32[]{:S(2)}, u32[]{:S(2)}) collective-permute-start(s16[144,512]{1,0:T(8,128)(2,1)S(1)} %get-tuple-element.69), channel_id=1, source_target_pairs={{0,10},{1,11},{2,8},{3,9},{4,14},{5,15},{6,12},{7,13},{8,2},{9,3},... | collective-permute-start | bytes 442376 | tf_op jit(solution)/shard_map/ppermute | solution.py:24
  149.0 12.8 %collective-permute-start.37 = (s16[144,512]{1,0:T(8,128)(2,1)S(1)}, s16[144,512]{1,0:T(8,128)(2,1)S(1)}, u32[]{:S(2)}, u32[]{:S(2)}) collective-permute-start(s16[144,512]{1,0:T(8,128)(2,1)S(1)} %get-tuple-element.70), channel_id=1, source_target_pairs={{0,8},{1,9},{2,10},{3,11},{4,12},{5,13},{6,14},{7,15},{8,0},{9,1},... | collective-permute-start | bytes 442376 | tf_op jit(solution)/shard_map/ppermute | solution.py:24
  153.3 9.4 %collective-permute-start.38 = (s16[144,512]{1,0:T(8,128)(2,1)S(1)}, s16[144,512]{1,0:T(8,128)(2,1)S(1)}, u32[]{:S(2)}, u32[]{:S(2)}) collective-permute-start(s16[144,512]{1,0:T(8,128)(2,1)S(1)} %get-tuple-element.71), channel_id=1, source_target_pairs={{0,6},{1,7},{2,4},{3,5},{4,2},{5,3},{6,0},{7,1},{8,14},{9,15},{10,... | collective-permute-start | bytes 442376 | tf_op jit(solution)/shard_map/ppermute | solution.py:24
  155.6 7.1 %collective-permute-start.39 = (s16[144,512]{1,0:T(8,128)(2,1)S(1)}, s16[144,512]{1,0:T(8,128)(2,1)S(1)}, u32[]{:S(2)}, u32[]{:S(2)}) collective-permute-start(s16[144,512]{1,0:T(8,128)(2,1)S(1)} %get-tuple-element.72), channel_id=1, source_target_pairs={{0,4},{1,5},{2,6},{3,7},{4,0},{5,1},{6,2},{7,3},{8,12},{9,13},{10,... | collective-permute-start | bytes 442376 | tf_op jit(solution)/shard_map/ppermute | solution.py:24
  155.7 10.4 %collective-permute-start.40 = (s16[144,512]{1,0:T(8,128)(2,1)S(1)}, s16[144,512]{1,0:T(8,128)(2,1)S(1)}, u32[]{:S(2)}, u32[]{:S(2)}) collective-permute-start(s16[144,512]{1,0:T(8,128)(2,1)S(1)} %get-tuple-element.73), channel_id=1, source_target_pairs={{0,2},{1,3},{2,0},{3,1},{4,6},{5,7},{6,4},{7,5},{8,10},{9,11},{10,... | collective-permute-start | bytes 442376 | tf_op jit(solution)/shard_map/ppermute | solution.py:24
  167.1 9.9 %collective-permute-start.41 = (s16[144,512]{1,0:T(8,128)(2,1)S(1)}, s16[144,512]{1,0:T(8,128)(2,1)S(1)}, u32[]{:S(2)}, u32[]{:S(2)}) collective-permute-start(s16[144,512]{1,0:T(8,128)(2,1)S(1)} %shard_map.121.own), channel_id=1, source_target_pairs={{0,16},{1,17},{2,18},{3,19},{4,20},{5,21},{6,22},{7,23},{8,24},{9,... | collective-permute-start | bytes 442376 | tf_op jit(solution)/shard_map/ppermute | solution.py:24
  178.4 8.6 %collective-permute-start.44 = (s16[144,512]{1,0:T(8,128)(2,1)S(1)}, s16[144,512]{1,0:T(8,128)(2,1)S(1)}, u32[]{:S(2)}, u32[]{:S(2)}) collective-permute-start(s16[144,512]{1,0:T(8,128)(2,1)S(1)} %shard_map.122), channel_id=1, source_target_pairs={{0,6},{1,7},{2,4},{3,5},{4,2},{5,3},{6,0},{7,1},{8,14},{9,15},{10,... | collective-permute-start | bytes 442376 | tf_op jit(solution)/shard_map/ppermute | solution.py:24
  180.4 6.6 %collective-permute-start.45 = (s16[144,512]{1,0:T(8,128)(2,1)S(1)}, s16[144,512]{1,0:T(8,128)(2,1)S(1)}, u32[]{:S(2)}, u32[]{:S(2)}) collective-permute-start(s16[144,512]{1,0:T(8,128)(2,1)S(1)} %shard_map.122), channel_id=1, source_target_pairs={{0,8},{1,9},{2,10},{3,11},{4,12},{5,13},{6,14},{7,15},{8,0},{9,1},... | collective-permute-start | bytes 442376 | tf_op jit(solution)/shard_map/ppermute | solution.py:24
  180.4 7.5 %collective-permute-start.46 = (s16[144,512]{1,0:T(8,128)(2,1)S(1)}, s16[144,512]{1,0:T(8,128)(2,1)S(1)}, u32[]{:S(2)}, u32[]{:S(2)}) collective-permute-start(s16[144,512]{1,0:T(8,128)(2,1)S(1)} %shard_map.122), channel_id=1, source_target_pairs={{0,10},{1,11},{2,8},{3,9},{4,14},{5,15},{6,12},{7,13},{8,2},{9,3},... | collective-permute-start | bytes 442376 | tf_op jit(solution)/shard_map/ppermute | solution.py:24
  182.6 8.0 %collective-permute-start.47 = (s16[144,512]{1,0:T(8,128)(2,1)S(1)}, s16[144,512]{1,0:T(8,128)(2,1)S(1)}, u32[]{:S(2)}, u32[]{:S(2)}) collective-permute-start(s16[144,512]{1,0:T(8,128)(2,1)S(1)} %shard_map.122), channel_id=1, source_target_pairs={{0,12},{1,13},{2,14},{3,15},{4,8},{5,9},{6,10},{7,11},{8,4},{9,5},... | collective-permute-start | bytes 442376 | tf_op jit(solution)/shard_map/ppermute | solution.py:24
  183.4 10.2 %collective-permute-start.48 = (s16[144,512]{1,0:T(8,128)(2,1)S(1)}, s16[144,512]{1,0:T(8,128)(2,1)S(1)}, u32[]{:S(2)}, u32[]{:S(2)}) collective-permute-start(s16[144,512]{1,0:T(8,128)(2,1)S(1)} %shard_map.122), channel_id=1, source_target_pairs={{0,14},{1,15},{2,12},{3,13},{4,10},{5,11},{6,8},{7,9},{8,6},{9,7},... | collective-permute-start | bytes 442376 | tf_op jit(solution)/shard_map/ppermute | solution.py:24
  193.6 8.7 %collective-permute-start.49 = (s16[8,144,512]{2,1,0:T(8,128)(2,1)S(1)}, s16[8,144,512]{2,1,0:T(8,128)(2,1)S(1)}, u32[]{:S(2)}, u32[]{:S(2)}) collective-permute-start(s16[8,144,512]{2,1,0:T(8,128)(2,1)S(1)} %bitcast_dynamic-update-slice_fusion.rest_2_.mine), channel_id=1, source_target_pairs={{0,1},{1,0},{2,3},{3,2},{4,5},{5,4},{6,7},{7,6},{8,9},{9,8},{10,11... | collective-permute-start | bytes 3538952 | tf_op jit(solution)/shard_map/ppermute | solution.py:24
  222.1 11.5 %collective-permute-start.51 = (s16[144,512]{1,0:T(8,128)(2,1)S(1)}, s16[144,512]{1,0:T(8,128)(2,1)S(1)}, u32[]{:S(2)}, u32[]{:S(2)}) collective-permute-start(s16[144,512]{1,0:T(8,128)(2,1)S(1)} %get-tuple-element.78), channel_id=1, source_target_pairs={{0,14},{1,15},{2,12},{3,13},{4,10},{5,11},{6,8},{7,9},{8,6},{9,7},... | collective-permute-start | bytes 442376 | tf_op jit(solution)/shard_map/ppermute | solution.py:24
  223.8 9.8 %collective-permute-start.52 = (s16[144,512]{1,0:T(8,128)(2,1)S(1)}, s16[144,512]{1,0:T(8,128)(2,1)S(1)}, u32[]{:S(2)}, u32[]{:S(2)}) collective-permute-start(s16[144,512]{1,0:T(8,128)(2,1)S(1)} %get-tuple-element.79), channel_id=1, source_target_pairs={{0,12},{1,13},{2,14},{3,15},{4,8},{5,9},{6,10},{7,11},{8,4},{9,5},... | collective-permute-start | bytes 442376 | tf_op jit(solution)/shard_map/ppermute | solution.py:24
  225.2 14.8 %collective-permute-start.53 = (s16[144,512]{1,0:T(8,128)(2,1)S(1)}, s16[144,512]{1,0:T(8,128)(2,1)S(1)}, u32[]{:S(2)}, u32[]{:S(2)}) collective-permute-start(s16[144,512]{1,0:T(8,128)(2,1)S(1)} %get-tuple-element.80), channel_id=1, source_target_pairs={{0,10},{1,11},{2,8},{3,9},{4,14},{5,15},{6,12},{7,13},{8,2},{9,3},... | collective-permute-start | bytes 442376 | tf_op jit(solution)/shard_map/ppermute | solution.py:24
  225.7 14.2 %collective-permute-start.54 = (s16[144,512]{1,0:T(8,128)(2,1)S(1)}, s16[144,512]{1,0:T(8,128)(2,1)S(1)}, u32[]{:S(2)}, u32[]{:S(2)}) collective-permute-start(s16[144,512]{1,0:T(8,128)(2,1)S(1)} %get-tuple-element.81), channel_id=1, source_target_pairs={{0,8},{1,9},{2,10},{3,11},{4,12},{5,13},{6,14},{7,15},{8,0},{9,1},... | collective-permute-start | bytes 442376 | tf_op jit(solution)/shard_map/ppermute | solution.py:24
  231.5 8.5 %collective-permute-start.55 = (s16[144,512]{1,0:T(8,128)(2,1)S(1)}, s16[144,512]{1,0:T(8,128)(2,1)S(1)}, u32[]{:S(2)}, u32[]{:S(2)}) collective-permute-start(s16[144,512]{1,0:T(8,128)(2,1)S(1)} %get-tuple-element.82), channel_id=1, source_target_pairs={{0,6},{1,7},{2,4},{3,5},{4,2},{5,3},{6,0},{7,1},{8,14},{9,15},{10,... | collective-permute-start | bytes 442376 | tf_op jit(solution)/shard_map/ppermute | solution.py:24
  233.6 8.2 %collective-permute-start.56 = (s16[144,512]{1,0:T(8,128)(2,1)S(1)}, s16[144,512]{1,0:T(8,128)(2,1)S(1)}, u32[]{:S(2)}, u32[]{:S(2)}) collective-permute-start(s16[144,512]{1,0:T(8,128)(2,1)S(1)} %get-tuple-element.83), channel_id=1, source_target_pairs={{0,4},{1,5},{2,6},{3,7},{4,0},{5,1},{6,2},{7,3},{8,12},{9,13},{10,... | collective-permute-start | bytes 442376 | tf_op jit(solution)/shard_map/ppermute | solution.py:24
  233.7 9.1 %collective-permute-start.57 = (s16[144,512]{1,0:T(8,128)(2,1)S(1)}, s16[144,512]{1,0:T(8,128)(2,1)S(1)}, u32[]{:S(2)}, u32[]{:S(2)}) collective-permute-start(s16[144,512]{1,0:T(8,128)(2,1)S(1)} %get-tuple-element.84), channel_id=1, source_target_pairs={{0,2},{1,3},{2,0},{3,1},{4,6},{5,7},{6,4},{7,5},{8,10},{9,11},{10,... | collective-permute-start | bytes 442376 | tf_op jit(solution)/shard_map/ppermute | solution.py:24
  244.3 7.7 %collective-permute-start.60 = (bf16[128,512]{1,0:T(8,128)(2,1)S(1)}, bf16[128,512]{1,0:T(8,128)(2,1)S(1)}, u32[]{:S(2)}, u32[]{:S(2)}) collective-permute-start(bf16[128,512]{1,0:T(8,128)(2,1)S(1)} %shard_map.130), channel_id=1, source_target_pairs={{0,6},{1,7},{2,4},{3,5},{4,2},{5,3},{6,0},{7,1},{8,14},{9,15},{10,... | collective-permute-start | bytes 393224 | tf_op jit(solution)/shard_map/ppermute | solution.py:24
  248.1 7.2 %collective-permute-start.63 = (bf16[128,512]{1,0:T(8,128)(2,1)S(1)}, bf16[128,512]{1,0:T(8,128)(2,1)S(1)}, u32[]{:S(2)}, u32[]{:S(2)}) collective-permute-start(bf16[128,512]{1,0:T(8,128)(2,1)S(1)} %shard_map.130), channel_id=1, source_target_pairs={{0,12},{1,13},{2,14},{3,15},{4,8},{5,9},{6,10},{7,11},{8,4},{9,5},... | collective-permute-start | bytes 393224 | tf_op jit(solution)/shard_map/ppermute | solution.py:24
  248.8 9.0 %collective-permute-start.64 = (bf16[128,512]{1,0:T(8,128)(2,1)S(1)}, bf16[128,512]{1,0:T(8,128)(2,1)S(1)}, u32[]{:S(2)}, u32[]{:S(2)}) collective-permute-start(bf16[128,512]{1,0:T(8,128)(2,1)S(1)} %shard_map.130), channel_id=1, source_target_pairs={{0,14},{1,15},{2,12},{3,13},{4,10},{5,11},{6,8},{7,9},{8,6},{9,7},... | collective-permute-start | bytes 393224 | tf_op jit(solution)/shard_map/ppermute | solution.py:24
  257.7 6.6 %collective-permute-start.65 = (bf16[8,128,512]{2,1,0:T(8,128)(2,1)S(1)}, bf16[8,128,512]{2,1,0:T(8,128)(2,1)S(1)}, u32[]{:S(2)}, u32[]{:S(2)}) collective-permute-start(bf16[8,128,512]{2,1,0:T(8,128)(2,1)S(1)} %bitcast_dynamic-update-slice_fusion.24.rest_5_), channel_id=1, source_target_pairs={{0,1},{1,0},{2,3},{3,2},{4,5},{5,4},{6,7},{7,6},{8,9},{9,8},{10,11... | collective-permute-start | bytes 3145736 | tf_op jit(solution)/shard_map/ppermute | solution.py:24
  (18 other events, 83.4 us)
where the time goes:
time: 271 us; the launch traced here: 269 us
  Pallas kernels  111 us (41%)
  waiting for transfers between devices  84.4 us (31%)
  starting transfers between devices  71 us (26%)
    pallas_call x29, Pallas kernels, call(): pl.pallas_call(kernel, grid_spec=pltpu.PrefetchScalarGridSpec(num_scalar_...  111 us
    ppermute x66, waiting for transfers between devices, swap(): return lax.ppermute(block, AXES, [(at, at ^ offset) for at in range(count)])  84.4 us
    ppermute x66, starting transfers between devices, swap(): return lax.ppermute(block, AXES, [(at, at ^ offset) for at in range(count)])  71 us
  transfers between devices with their start and end apart: 66, of which 39 were waited for; matrix products, arithmetic and copies ran while one was open for 0% of the time, Pallas kernels for 17%

commit v1 on v0

--- a/solution.py
+++ b/solution.py
@@ -135,11 +135,26 @@
     return first + pl.program_id(0) * per + at
 
 
+def arrival(entry):
+    return (NEAR - entry) & (NEAR - 1)
+
+
 def over(shape, index):
     def spec(first, at, per, flip):
         return pl.BlockSpec(shape, lambda k, p: index(chunk_at(first + k * per + at, p, flip)))
 
     return spec
+
+
+def over_arrived(shape, index):
+    def spec(at, per, flip):
+        return pl.BlockSpec(shape, lambda k, p: index(chunk_at(arrival(k * per + at), p, flip)))
+
+    return spec
+
+
+def arrived(at, per, place, flip):
+    return chunk_at(arrival(pl.program_id(0) * per + at), place, flip)
 
 
 def emit(first, per, at, outs, value):
@@ -155,7 +170,7 @@
                 put(outs[where], coded)
 
 
-def reduced(place, kernel, specs, args, shape, scratch, flops, moved, per, received=None):
+def reduced(place, kernel, specs, args, shape, scratch, flops, moved, per, received=None, batches=BATCHES):
     coded = (shape[0] + PAD, shape[1])
     if received is None:
         sent = call(
@@ -171,7 +186,7 @@
         )
         received = swap(sent[0], 1)
     kept = [None] * NEAR
-    for first, count in BATCHES:
+    for first, count in batches:
         kept[first : first + count] = call(
             functools.partial(kernel, 0, first, per),
             place,
@@ -188,8 +203,8 @@
             ],
             scratch,
             [*args, received],
-            flops // 4,
-            moved // 4,
+            flops * count // GROUP,
+            moved * count // GROUP,
         )
     return kept
 
@@ -215,18 +230,22 @@
         for level in range(spread.shape[0]):
             spread[level] = spread_tiles(tiles, level, spread.shape[2], size)
 
+    values = []
     for at in range(per):
         chunk = chunk_at(steps_of(0, at, per), place, 1)
-        value = leaf_low_value(size, chunk, place, blocks[at], spread, rounded, rhs)
-        put(sent.at[at], encode(value))
+        values.append(leaf_low_value(size, chunk, place, blocks[at], spread, rounded, rhs))
+    for at in range(per):
+        put(sent.at[at], encode(values[at]))
 
 
 def leaf_keep_kernel(size, flip, first, per, place, *rest):
     blocks, (spread, rounded, rhs, received) = rest[:per], rest[per : per + 4]
+    values = []
     for at in range(per):
         chunk = chunk_at(steps_of(first, at, per), place, flip)
-        value = leaf_low_value(size, chunk, place, blocks[at], spread, rounded, rhs)
-        emit(first, per, at, rest[per + 4 :], value + decode(received[at]))
+        values.append(leaf_low_value(size, chunk, place, blocks[at], spread, rounded, rhs))
+    for at in range(per):
+        emit(first, per, at, rest[per + 4 :], values[at] + decode(received[at]))
 
 
 def leaf_top_kernel(size, place, spread, rounded, coupling, part):
@@ -269,9 +288,7 @@
     coded = summed(place, kept[0], received, final and not far, before)
     if far:
         coded = summed(place, coded, [swap(coded, offset) for offset in far], final)
-    mine = [coded] + [None] * (NEAR - 1)
-    for at in range(NEAR - 1, 0, -1):
-        mine[at] = swap(coded, at << 1)
+    mine = [coded] + [swap(coded, arrival(entry) << 1) for entry in range(1, NEAR)]
     mine = jnp.stack(mine)
     return mine, swap(mine, 1)
 
@@ -288,12 +305,18 @@
         wide[...] = jnp.zeros_like(wide)
         narrow[...] = jnp.zeros_like(narrow)
 
-    @pl.when(pl.program_id(0) >= 0)
-    def _():
+    start = place[start_at]
+    rows = factors[0].shape[0]
+    chunks = [arrived(at, per, place, flip) for at in range(per)]
+    below = functools.reduce(
+        jnp.logical_and, [(chunk + 1) * depth <= start + 1 for chunk in chunks]
+    )
+
+    def add(wanted, cut):
         highs, lows, uppers, lowers = [], [], [], []
-        for at in range(per):
-            chunk = chunk_at(steps_of(0, at, per), place, flip)
-            high, low = halves(triangular(factors[at][...], place[start_at], chunk * depth))
+        for at in wanted:
+            block = factors[at][...]
+            high, low = halves(triangular(block, start, chunks[at] * depth) if cut else block)
             upper, lower = halves(decode(stack[at]))
             highs, lows = highs + [high], lows + [low]
             uppers, lowers = uppers + [upper], lowers + [lower]
@@ -302,6 +325,16 @@
         wide[...] += dot(jnp.concatenate(highs, 1), both)
         narrow[...] += dot(jnp.concatenate(lows, 1), upper)
 
+    @pl.when(below)
+    def _():
+        add(range(per), False)
+
+    for at in range(per):
+
+        @pl.when(jnp.logical_not(below) & (chunks[at] * depth < start + rows))
+        def _(at=at):
+            add([at], True)
+
     @pl.when(pl.program_id(0) == pl.num_programs(0) - 1)
     def _():
         value = wide[:, :columns] + wide[:, columns:] + narrow[...]
@@ -316,14 +349,14 @@
     depth = size // GROUP
     columns = stacks[0].shape[2]
     per = 2
-    block = over((count, depth), lambda chunk: (0, chunk))
+    block = over_arrived((count, depth), lambda chunk: (0, chunk))
     result = ()
     for flip in range(2):
         result = call(
             functools.partial(factor_kernel, start_at, flip, per),
             place,
             NEAR // per,
-            [block(0, at, per, flip) for at in range(per)]
+            [block(at, per, flip) for at in range(per)]
             + [in_steps(per, stacks[flip].shape[1:])]
             + [whole(r.shape) for r in result],
             [out_whole((count, columns), F32)] + [out_whole((columns, count), F32)] * flip,
@@ -346,16 +379,18 @@
         packed[:, :columns] = high
         packed[:, columns:] = low
 
+    values = []
     for at in range(per):
         chunk = chunk_at(steps_of(first, at, per), place, flip)
         high, low = halves(couplings[at][0])
         product = dot(high, packed[...])
         value = product[:, :columns] + product[:, columns:] + dot(low, packed[:, :columns])
-        value = with_rows(-(parts[at][0] + value), chunk, place[3], rhs)
+        values.append(with_rows(-(parts[at][0] + value), chunk, place[3], rhs))
+    for at in range(per):
         if flip:
-            put(rest[2].at[at], encode(value))
+            put(rest[2].at[at], encode(values[at]))
         else:
-            emit(first, per, at, rest[3:-1], value + decode(rest[2][at]))
+            emit(first, per, at, rest[3:-1], values[at] + decode(rest[2][at]))
 
 
 def back_kernel(start_at, flip, first, per, place, *rest):
@@ -369,16 +404,43 @@
         packed[:columns, :] = high
         packed[columns:, :] = low
 
-    for at in range(per):
-        chunk = chunk_at(steps_of(first, at, per), place, flip)
-        depth = factors[at].shape[1]
-        high, low = halves(triangular(factors[at][...], place[start_at], chunk * depth))
-        product = dot(packed[...], high)
-        value = product[:columns, :] + product[columns:, :] + dot(packed[:columns, :], low)
-        if flip:
-            put(rest[0].at[at], encode(value))
-        else:
-            emit(first, per, at, rest[1:-1], value + decode(rest[0][at]))
+    rows, depth = factors[0].shape
+    start = place[start_at]
+    chunks = [chunk_at(steps_of(first, at, per), place, flip) for at in range(per)]
+    below = functools.reduce(
+        jnp.logical_and, [(chunk + 1) * depth <= start + 1 for chunk in chunks]
+    )
+    above = functools.reduce(jnp.logical_and, [chunk * depth >= start + rows for chunk in chunks])
+
+    def finish(values):
+        for at in range(per):
+            if flip:
+                put(rest[0].at[at], encode(values[at]))
+            else:
+                emit(first, per, at, rest[1:-1], values[at] + decode(rest[0][at]))
+
+    def products(cut):
+        values = []
+        for at in range(per):
+            block = factors[at][...]
+            high, low = halves(triangular(block, start, chunks[at] * depth) if cut else block)
+            product = dot(packed[...], high)
+            values.append(
+                product[:columns, :] + product[columns:, :] + dot(packed[:columns, :], low)
+            )
+        return values
+
+    @pl.when(below)
+    def _():
+        finish(products(False))
+
+    @pl.when(above)
+    def _():
+        finish([jnp.zeros((columns, depth), F32)] * per)
+
+    @pl.when(jnp.logical_not(below | above))
+    def _():
+        finish(products(True))
 
 
 def back_apply(place, factor, vector, start_at):
@@ -441,7 +503,7 @@
 def leaf_product(size, flip, per, place, blocks, spread, path):
     left, right = [], []
     for at in range(per):
-        chunk = chunk_at(steps_of(0, at, per), place, flip)
+        chunk = arrived(at, per, place, flip)
         left.append(path[at])
         right.append(masked(blocks[at][0, 0], spread, chunk, size))
     return dot(jnp.concatenate(left, 1), jnp.concatenate(right, 0))
@@ -523,7 +585,8 @@
     leaf_flops = 2 * sep_size * local_rows * columns
     leaf_moved = 2 * sep_size * local_rows
     leaf_low = over((1, 1, chunk, local_rows), lambda c: (0, c, 0, 0))
-    leaf_top = over((1, 1, chunk, local_rows), lambda c: (1, c, 0, 0))
+    leaf_top = over_arrived((1, 1, chunk, local_rows), lambda c: (1, c, 0, 0))
+    leaf_arrived = over_arrived((1, 1, chunk, local_rows), lambda c: (0, c, 0, 0))
     spread_shape = (levels, sep_size // size, local_rows)
 
     def spread_of(level):
@@ -567,6 +630,7 @@
         leaf_moved,
         per,
         swap(sent, 1),
+        ((0, NEAR),),
     )
     part = call(
         functools.partial(leaf_top_kernel, size),
@@ -589,6 +653,7 @@
     coupled_flops = 8 * sep_size * low_count * columns
     coupled_moved = 4 * sep_size * low_count
     low_block = over((1, chunk, low_count), lambda c: (c, 0, 0))
+    low_arrived = over_arrived((1, chunk, low_count), lambda c: (c, 0, 0))
     part_block = over((1, chunk, columns), lambda c: (c, 0, 0))
     per = 2
 
@@ -622,7 +687,7 @@
             functools.partial(carry_kernel, flip, per),
             place,
             NEAR // per,
-            [low_block(0, at, per, flip) for at in range(per)]
+            [low_arrived(at, per, flip) for at in range(per)]
             + [in_steps(per, solution_blocks[flip].shape[1:]), whole(gap.shape)],
             [out_whole(gap.shape, F32), in_steps(per, turned, BF16, NEAR)],
             [pltpu.VMEM((2 * columns, low_count), F32), pltpu.VMEM((columns, low_count), F32)],
@@ -637,7 +702,7 @@
         1,
         [
             pl.BlockSpec(
-                (1, *s.shape[1:]), lambda k, p: ((p[3] // chunk // 2) ^ p[1], 0, 0)
+                (1, *s.shape[1:]), lambda k, p: (arrival((p[3] // chunk // 2) ^ p[1]), 0, 0)
             )
             for s in solution_blocks
         ],
@@ -653,7 +718,7 @@
         functools.partial(leaf_back_top_kernel, size, per),
         place,
         NEAR // per,
-        [leaf_top(0, at, per, flip) for flip in range(2) for at in range(per)]
+        [leaf_top(at, per, flip) for flip in range(2) for at in range(per)]
         + [spread_of(1)]
         + [in_steps(per, turned)] * 2,
         [out_whole((columns, local_rows), F32)],
@@ -671,7 +736,7 @@
             functools.partial(leaf_back_kernel, size, flip, per),
             place,
             NEAR // per,
-            [leaf_low(0, at, per, flip) for at in range(per)]
+            [leaf_arrived(at, per, flip) for at in range(per)]
             + [spread_of(0), in_steps(per, turned), whole(result.shape)]
             + [whole(a.shape) for a in last],
             [out_whole((local_rows, columns) if flip else (columns, local_rows), F32)],

time: 271 us -> 264 us (0.974)
  Pallas kernels: 111 us -> 104 us
  waiting for transfers between devices: 84.4 us -> 87.6 us
    pallas_call x29 -> x28, Pallas kernels: 111 us -> 104 us  [call(): pl.pallas_call(kernel, grid_spec=pltpu.PrefetchScalarGridSpec(num_scalar_...]
    ppermute x66, waiting for transfers between devices: 84.4 us -> 87.6 us  [swap(): return lax.ppermute(block, AXES, [(at, at ^ offset) for at in range(count)])]
  transfers between devices with their start and end apart: 66 -> 66, of which waited for: 39 -> 39; matrix products, arithmetic and copies ran while one was open for 0% -> 0% of each run, Pallas kernels for 17% -> 15%
where the time goes in v1:
time: 264 us
  Pallas kernels  104 us (39%)
  waiting for transfers between devices  87.6 us (33%)
  starting transfers between devices  69.3 us (26%)
    pallas_call x28, Pallas kernels, call(): pl.pallas_call(kernel, grid_spec=pltpu.PrefetchScalarGridSpec(num_scalar_...  104 us
    ppermute x66, waiting for transfers between devices, swap(): return lax.ppermute(block, AXES, [(at, at ^ offset) for at in range(count)])  87.6 us
    ppermute x66, starting transfers between devices, swap(): return lax.ppermute(block, AXES, [(at, at ^ offset) for at in range(count)])  69.3 us
  transfers between devices with their start and end apart: 66, of which 39 were waited for; matrix products, arithmetic and copies ran while one was open for 0% of the time, Pallas kernels for 15%

profile of v1, /device:TPU:25, one launch (start us, length us, event | category | flops | bytes accessed | tf_op | source)
XLA Modules:
  0.0 263.5 jit_solution(9683277919681853569)
XLA Ops:
  0.8 4.6 %shard_map.104 = (s16[8,528,128]{2,1,0:T(8,128)(2,1)S(1)}, f32[384,128]{1,0:T(8,128)S(1)}, bf16[384,128]{1,0:T(8,128)(2,1)S(1)}, f32[2,128,384]{2,1,0:T(8,128)S(1)}) custom-call(s32[4]{0:T(128)S(1)} %pad_add_fusion.place, bf16[2,16,512,384]{3,2,1,0:T(8,128)(2,1)} %bitcast.72, bf16[2,16,512,384]{3,2,1,0:T(8,128)(2,1)} %bitcast.73, ...), custom_call_target="tpu_custom_call" | custom-call | flops 402653184 | bytes 3145728 | tf_op jit(solution)/shard_map/pallas_call | solution.py:98
  6.1 2.3 collective-permute-done.rest_7_
  8.4 4.5 %shard_map.106 = (f32[512,128]{1,0:T(8,128)S(1)}, s16[528,128]{1,0:T(8,128)(2,1)S(1)}, s16[528,128]{1,0:T(8,128)(2,1)S(1)}, s16[528,128]{1,0:T(8,128)(2,1)S(1)},...) custom-call(s32[4]{0:T(128)S(1)} %pad_add_fusion.place, ...), custom_call_target="tpu_custom_call" | custom-call | flops 402653184 | bytes 3145728 | tf_op jit(solution)/shard_map/pallas_call | solution.py:98
  20.8 2.7 %collective-permute-done.2.rest_1_ = s16[528,128]{1,0:T(8,128)(2,1)S(1)} collective-permute-done((s16[528,128]{1,0:T(8,128)(2,1)S(1)}, s16[528,128]{1,0:T(8,128)(2,1)S(1)}, u32[]{:S(2)}, u32[]{:S(2)}) %collective-permute-start.2) | collective-permute-done | bytes 135200 | tf_op jit(solution)/shard_map/ppermute | solution.py:24
  24.1 5.2 %shard_map.105.rest_7_.rest_2_.rest_3_ = f32[16,512,128]{2,1,0:T(8,128)S(1)} custom-call(s32[4]{0:T(128)S(1)} %pad_add_fusion.place, f32[2,128,384]{2,1,0:T(8,128)S(1)} %get-tuple-element.45.spread.rest_4_, bf16[384,128]{1,0:T(8,128)(2,1)S(1)} %get-tuple-element.46.rounded.rest_5_, bf16[2,16,512,384]{3,2,1,0:T(8,128)(2,1)} %bitcast.80), custom_call_target="tpu_custom_call" | custom-call | flops 805306368 | bytes 6291456 | tf_op jit(solution)/shard_map/pallas_call | solution.py:98
  38.9 2.5 collective-permute-done.10
  41.4 2.5 collective-permute-done.11
  46.9 2.6 %collective-permute-start.15 = (s16[8,528,128]{2,1,0:T(8,128)(2,1)S(1)}, s16[8,528,128]{2,1,0:T(8,128)(2,1)S(1)}, u32[]{:S(2)}, u32[]{:S(2)}) collective-permute-start(s16[8,528,128]{2,1,0:T(8,128)(2,1)S(1)} %bitcast_dynamic-update-slice_fusion.16.rest_2_), channel_id=1, source_target_pairs={{0,1},{1,0},{2,3},{3,2},{4,5},{5,4},{6,7},{7,6},{8,9},{9,8},{10,11... | collective-permute-start | bytes 3244040 | tf_op jit(solution)/shard_map/ppermute | solution.py:24
  49.5 5.7 %shard_map.108.rest_3_ = f32[512,128]{1,0:T(8,128)S(1)} custom-call(s32[4]{0:T(128)S(1)} %pad_add_fusion.place, f32[512,8192]{1,0:T(8,128)} %rest_1_.19, f32[512,8192]{1,0:T(8,128)} %rest_1_.19, s16[8,528,128]{2,1,0:T(8,128)(2,1)S(1)} %bitcast_dynamic-update-slice_fusion.16.rest_2_), custom_call_target="tpu_custom_call" | custom-call | flops 2147483648 | bytes 8388608 | tf_op jit(solution)/shard_map/pallas_call | solution.py:98
  55.2 5.6 %shard_map.109 = (f32[512,128]{1,0:T(8,128)S(1)}, f32[128,512]{1,0:T(8,128)S(1)}) custom-call(s32[4]{0:T(128)S(1)} %pad_add_fusion.place, f32[512,8192]{1,0:T(8,128)} %rest_1_.19, f32[512,8192]{1,0:T(8,128)} %rest_1_.19, s16[8,528,128]{2,1,0:T(8,128)(2,1)S(1)} %collective-permute-done.15.rest_2_, f32[512,128]{1,0:T(8,128)S(1)} %shard_map.108.rest_3_), custom_call_target="tpu_custom_call" | custom-call | flops 2147483648 | bytes 8388608 | tf_op jit(solution)/shard_map/pallas_call | solution.py:98
  60.9 6.5 %shard_map.110 = s16[8,528,128]{2,1,0:T(8,128)(2,1)S(1)} custom-call(s32[4]{0:T(128)S(1)} %pad_add_fusion.place, f32[16,512,512]{2,1,0:T(8,128)} %bitcast.93, f32[16,512,512]{2,1,0:T(8,128)} %bitcast.94, f32[16,512,128]{2,1,0:T(8,128)S(1)} %shard_map.105.rest_7_.rest_2_.rest_3_, f32[16,512,128]{2,1,0:T(8,128)S(1)} %shard_map.105.rest_7_.rest_2_.rest_3_, ...), custom_call_target="tpu_custom_call" | custom-call | flops 2147483648 | bytes 8388608 | tf_op jit(solution)/shard_map/pallas_call | solution.py:98
  67.5 2.7 %collective-permute-done.16.rest_6_ = s16[8,528,128]{2,1,0:T(8,128)(2,1)S(1)} collective-permute-done((s16[8,528,128]{2,1,0:T(8,128)(2,1)S(1)}, s16[8,528,128]{2,1,0:T(8,128)(2,1)S(1)}, u32[]{:S(2)}, u32[]{:S(2)}) %collective-permute-start.16) | collective-permute-done | bytes 1081376 | tf_op jit(solution)/shard_map/ppermute | solution.py:24
  70.1 4.0 %shard_map.112 = (s16[528,128]{1,0:T(8,128)(2,1)S(1)}, s16[528,128]{1,0:T(8,128)(2,1)S(1)}, s16[528,128]{1,0:T(8,128)(2,1)S(1)}, s16[528,128]{1,0:T(8,128)(2,1)S(1)}) custom-call(s32[4]{0:T(128)S(1)} %pad_add_fusion.place, f32[16,512,512]{2,1,0:T(8,128)} %bitcast.95, f32[16,512,512]{2,1,0:T(8,128)} %bitcast.96, ...), custom_call_target="tpu_custom_call" | custom-call | flops 1073741824 | bytes 4194304 | tf_op jit(solution)/shard_map/pallas_call | solution.py:98
  79.0 4.2 %shard_map.111 = (f32[512,128]{1,0:T(8,128)S(1)}, s16[528,128]{1,0:T(8,128)(2,1)S(1)}, s16[528,128]{1,0:T(8,128)(2,1)S(1)}, s16[528,128]{1,0:T(8,128)(2,1)S(1)}) custom-call(s32[4]{0:T(128)S(1)} %pad_add_fusion.place, f32[16,512,512]{2,1,0:T(8,128)} %bitcast.97, f32[16,512,512]{2,1,0:T(8,128)} %bitcast.98, ...), custom_call_target="tpu_custom_call" | custom-call | flops 1073741824 | bytes 4194304 | tf_op jit(solution)/shard_map/pallas_call | solution.py:98
  83.2 3.2 %collective-permute-start.21 = (s16[528,128]{1,0:T(8,128)(2,1)S(1)}, s16[528,128]{1,0:T(8,128)(2,1)S(1)}, u32[]{:S(2)}, u32[]{:S(2)}) collective-permute-start(s16[528,128]{1,0:T(8,128)(2,1)S(1)} %get-tuple-element.62), channel_id=1, source_target_pairs={{0,6},{1,7},{2,4},{3,5},{4,2},{5,3},{6,0},{7,1},{8,14},{9,15},{10,... | collective-permute-start | bytes 405512 | tf_op jit(solution)/shard_map/ppermute | solution.py:24
  91.0 3.2 %collective-permute-done.22.rest_5_ = s16[528,128]{1,0:T(8,128)(2,1)S(1)} collective-permute-done((s16[528,128]{1,0:T(8,128)(2,1)S(1)}, s16[528,128]{1,0:T(8,128)(2,1)S(1)}, u32[]{:S(2)}, u32[]{:S(2)}) %collective-permute-start.22) | collective-permute-done | bytes 135200 | tf_op jit(solution)/shard_map/ppermute | solution.py:24
  95.9 8.3 %collective-permute-done.24.rest_0_ = s16[528,128]{1,0:T(8,128)(2,1)S(1)} collective-permute-done((s16[528,128]{1,0:T(8,128)(2,1)S(1)}, s16[528,128]{1,0:T(8,128)(2,1)S(1)}, u32[]{:S(2)}, u32[]{:S(2)}) %collective-permute-start.24) | collective-permute-done | bytes 135200 | tf_op jit(solution)/shard_map/ppermute | solution.py:24
  105.0 2.3 collective-permute-start.26
  107.3 2.4 collective-permute-start.28
  111.7 2.8 %collective-permute-done.26 = s16[528,128]{1,0:T(8,128)(2,1)S(1)} collective-permute-done((s16[528,128]{1,0:T(8,128)(2,1)S(1)}, s16[528,128]{1,0:T(8,128)(2,1)S(1)}, u32[]{:S(2)}, u32[]{:S(2)}) %collective-permute-start.26) | collective-permute-done | bytes 135200 | tf_op jit(solution)/shard_map/ppermute | solution.py:24
  116.9 3.1 %collective-permute-done.30 = s16[528,128]{1,0:T(8,128)(2,1)S(1)} collective-permute-done((s16[528,128]{1,0:T(8,128)(2,1)S(1)}, s16[528,128]{1,0:T(8,128)(2,1)S(1)}, u32[]{:S(2)}, u32[]{:S(2)}) %collective-permute-start.30) | collective-permute-done | bytes 135200 | tf_op jit(solution)/shard_map/ppermute | solution.py:24
  120.0 2.2 collective-permute-start.32
  122.3 4.4 %shard_map.115.rest_3_ = f32[256,128]{1,0:T(8,128)S(1)} custom-call(s32[4]{0:T(128)S(1)} %pad_add_fusion.place, f32[256,8192]{1,0:T(8,128)} %rest_1_.16, f32[256,8192]{1,0:T(8,128)} %rest_1_.16, s16[8,528,128]{2,1,0:T(8,128)(2,1)S(1)} %bitcast_dynamic-update-slice_fusion.8.rest_2_), custom_call_target="tpu_custom_call" | custom-call | flops 1073741824 | bytes 4194304 | tf_op jit(solution)/shard_map/pallas_call | solution.py:98
  126.7 5.5 %shard_map.116 = (f32[256,128]{1,0:T(8,128)}, f32[128,256]{1,0:T(8,128)S(1)}) custom-call(s32[4]{0:T(128)S(1)} %pad_add_fusion.place, f32[256,8192]{1,0:T(8,128)} %rest_1_.16, f32[256,8192]{1,0:T(8,128)} %rest_1_.16, s16[8,528,128]{2,1,0:T(8,128)(2,1)S(1)} %collective-permute-done.32.rest_2_, f32[256,128]{1,0:T(8,128)S(1)} %shard_map.115.rest_3_), custom_call_target="tpu_custom_call" | custom-call | flops 1073741824 | bytes 4194304 | tf_op jit(solution)/shard_map/pallas_call | solution.py:98
  132.2 4.6 %shard_map.117 = s16[8,144,512]{2,1,0:T(8,128)(2,1)S(1)} custom-call(s32[4]{0:T(128)S(1)} %pad_add_fusion.place, f32[256,8192]{1,0:T(8,128)} %rest_1_.16, f32[256,8192]{1,0:T(8,128)} %rest_1_.16, f32[128,256]{1,0:T(8,128)S(1)} %get-tuple-element.65.rest_2_), custom_call_target="tpu_custom_call" | custom-call | flops 1073741824 | bytes 4194304 | tf_op jit(solution)/shard_map/pallas_call | solution.py:98
  136.9 2.8 %collective-permute-done.33.rest_3_ = s16[8,144,512]{2,1,0:T(8,128)(2,1)S(1)} collective-permute-done((s16[8,144,512]{2,1,0:T(8,128)(2,1)S(1)}, s16[8,144,512]{2,1,0:T(8,128)(2,1)S(1)}, u32[]{:S(2)}, u32[]{:S(2)}) %collective-permute-start.33) | collective-permute-done | bytes 1179680 | tf_op jit(solution)/shard_map/ppermute | solution.py:24
  139.8 2.9 %shard_map.119 = (s16[144,512]{1,0:T(8,128)(2,1)S(1)}, s16[144,512]{1,0:T(8,128)(2,1)S(1)}, s16[144,512]{1,0:T(8,128)(2,1)S(1)}, s16[144,512]{1,0:T(8,128)(2,1)S(1)}) custom-call(s32[4]{0:T(128)S(1)} %pad_add_fusion.place, f32[256,8192]{1,0:T(8,128)} %rest_1_.16, f32[256,8192]{1,0:T(8,128)} %rest_1_.16, f32[128,256]{1,0:T(8,128)S(1)} %get-tuple-element.65.rest_2_, ...), custom_call_target="tpu_custom_call" | custom-call | flops 536870912 | bytes 2097152 | tf_op jit(solution)/shard_map/pallas_call | solution.py:98
  142.8 2.4 collective-permute-start.35
  147.5 2.7 %shard_map.118 = (f32[128,512]{1,0:T(8,128)S(1)}, s16[144,512]{1,0:T(8,128)(2,1)S(1)}, s16[144,512]{1,0:T(8,128)(2,1)S(1)}, s16[144,512]{1,0:T(8,128)(2,1)S(1)}) custom-call(s32[4]{0:T(128)S(1)} %pad_add_fusion.place, f32[256,8192]{1,0:T(8,128)} %rest_1_.16, f32[256,8192]{1,0:T(8,128)} %rest_1_.16, f32[128,256]{1,0:T(8,128)S(1)} %get-tuple-element.65.rest_2_, ...), custom_call_target="tpu_custom_call" | custom-call | flops 536870912 | bytes 2097152 | tf_op jit(solution)/shard_map/pallas_call | solution.py:98
  153.4 2.7 %collective-permute-done.36.rest_2_ = s16[144,512]{1,0:T(8,128)(2,1)S(1)} collective-permute-done((s16[144,512]{1,0:T(8,128)(2,1)S(1)}, s16[144,512]{1,0:T(8,128)(2,1)S(1)}, u32[]{:S(2)}, u32[]{:S(2)}) %collective-permute-start.36) | collective-permute-done | bytes 147488 | tf_op jit(solution)/shard_map/ppermute | solution.py:24
  156.0 3.1 %collective-permute-done.37.rest_3_ = s16[144,512]{1,0:T(8,128)(2,1)S(1)} collective-permute-done((s16[144,512]{1,0:T(8,128)(2,1)S(1)}, s16[144,512]{1,0:T(8,128)(2,1)S(1)}, u32[]{:S(2)}, u32[]{:S(2)}) %collective-permute-start.37) | collective-permute-done | bytes 147488 | tf_op jit(solution)/shard_map/ppermute | solution.py:24
  159.6 3.2 %collective-permute-done.40.rest_6_ = s16[144,512]{1,0:T(8,128)(2,1)S(1)} collective-permute-done((s16[144,512]{1,0:T(8,128)(2,1)S(1)}, s16[144,512]{1,0:T(8,128)(2,1)S(1)}, u32[]{:S(2)}, u32[]{:S(2)}) %collective-permute-start.40) | collective-permute-done | bytes 147488 | tf_op jit(solution)/shard_map/ppermute | solution.py:24
  163.9 8.7 %collective-permute-done.41.rest_0_ = s16[144,512]{1,0:T(8,128)(2,1)S(1)} collective-permute-done((s16[144,512]{1,0:T(8,128)(2,1)S(1)}, s16[144,512]{1,0:T(8,128)(2,1)S(1)}, u32[]{:S(2)}, u32[]{:S(2)}) %collective-permute-start.41) | collective-permute-done | bytes 147488 | tf_op jit(solution)/shard_map/ppermute | solution.py:24
  173.4 2.5 collective-permute-start.43
  181.2 2.6 collective-permute-done.43
  186.8 2.6 collective-permute-done.45
  192.5 6.0 %shard_map.122 = (f32[128,512]{1,0:T(8,128)S(1)}, bf16[8,128,512]{2,1,0:T(8,128)(2,1)S(1)}) custom-call(s32[4]{0:T(128)S(1)} %pad_add_fusion.place, f32[16,512,512]{2,1,0:T(8,128)} %bitcast.99, f32[16,512,512]{2,1,0:T(8,128)} %bitcast.100, s16[8,144,512]{2,1,0:T(8,128)(2,1)S(1)} %bitcast_dynamic-update-slice_fusion.rest_2_.mine, ...), custom_call_target="tpu_custom_call" | custom-call | flops 2147483648 | bytes 8388608 | tf_op jit(solution)/shard_map/pallas_call | solution.py:98
  198.5 6.0 %shard_map.123 = (f32[128,512]{1,0:T(8,128)S(1)}, bf16[8,128,512]{2,1,0:T(8,128)(2,1)S(1)}) custom-call(s32[4]{0:T(128)S(1)} %pad_add_fusion.place, f32[16,512,512]{2,1,0:T(8,128)} %bitcast.101, f32[16,512,512]{2,1,0:T(8,128)} %bitcast.102, s16[8,144,512]{2,1,0:T(8,128)(2,1)S(1)} %collective-permute-done.49.rest_2_.other, ...), custom_call_target="tpu_custom_call" | custom-call | flops 2147483648 | bytes 8388608 | tf_op jit(solution)/shard_map/pallas_call | solution.py:98
  204.6 6.3 %shard_map.124 = s16[8,144,512]{2,1,0:T(8,128)(2,1)S(1)} custom-call(s32[4]{0:T(128)S(1)} %pad_add_fusion.place, f32[512,8192]{1,0:T(8,128)} %rest_1_.19, f32[512,8192]{1,0:T(8,128)} %rest_1_.19, f32[128,512]{1,0:T(8,128)S(1)} %get-tuple-element.76.rest_2_), custom_call_target="tpu_custom_call" | custom-call | flops 2147483648 | bytes 8388608 | tf_op jit(solution)/shard_map/pallas_call | solution.py:98
  211.0 2.8 %collective-permute-done.50.rest_3_ = s16[8,144,512]{2,1,0:T(8,128)(2,1)S(1)} collective-permute-done((s16[8,144,512]{2,1,0:T(8,128)(2,1)S(1)}, s16[8,144,512]{2,1,0:T(8,128)(2,1)S(1)}, u32[]{:S(2)}, u32[]{:S(2)}) %collective-permute-start.50) | collective-permute-done | bytes 1179680 | tf_op jit(solution)/shard_map/ppermute | solution.py:24
  213.8 3.8 %shard_map.126 = (s16[144,512]{1,0:T(8,128)(2,1)S(1)}, s16[144,512]{1,0:T(8,128)(2,1)S(1)}, s16[144,512]{1,0:T(8,128)(2,1)S(1)}, s16[144,512]{1,0:T(8,128)(2,1)S(1)}) custom-call(s32[4]{0:T(128)S(1)} %pad_add_fusion.place, f32[512,8192]{1,0:T(8,128)} %rest_1_.19, f32[512,8192]{1,0:T(8,128)} %rest_1_.19, f32[128,512]{1,0:T(8,128)S(1)} %get-tuple-element.76.rest_2_, ...), custom_call_target="tpu_custom_call" | custom-call | flops 1073741824 | bytes 4194304 | tf_op jit(solution)/shard_map/pallas_call | solution.py:98
  222.4 3.4 %shard_map.125 = (f32[128,512]{1,0:T(8,128)S(1)}, s16[144,512]{1,0:T(8,128)(2,1)S(1)}, s16[144,512]{1,0:T(8,128)(2,1)S(1)}, s16[144,512]{1,0:T(8,128)(2,1)S(1)}) custom-call(s32[4]{0:T(128)S(1)} %pad_add_fusion.place, f32[512,8192]{1,0:T(8,128)} %rest_1_.19, f32[512,8192]{1,0:T(8,128)} %rest_1_.19, f32[128,512]{1,0:T(8,128)S(1)} %get-tuple-element.76.rest_2_, ...), custom_call_target="tpu_custom_call" | custom-call | flops 1073741824 | bytes 4194304 | tf_op jit(solution)/shard_map/pallas_call | solution.py:98
  229.3 4.9 %shard_map.127.rest_7_.rest_6_ = f32[128,384]{1,0:T(8,128)S(1)} custom-call(s32[4]{0:T(128)S(1)} %pad_add_fusion.place, bf16[2,16,512,384]{3,2,1,0:T(8,128)(2,1)} %bitcast.81, bf16[2,16,512,384]{3,2,1,0:T(8,128)(2,1)} %bitcast.82, bf16[2,16,512,384]{3,2,1,0:T(8,128)(2,1)} %bitcast.83, bf16[2,16,512,384]{3,2,1,0:T(8,128)(2,1)} %bitcast.84, ...), custom_call_target="tpu_custom_call" | custom-call | flops 805306368 | bytes 6291456 | tf_op jit(solution)/shard_map/pallas_call | solution.py:98
  234.8 2.6 collective-permute-done.57.rest_6_
  238.4 3.1 %collective-permute-start.59 = (bf16[128,512]{1,0:T(8,128)(2,1)S(1)}, bf16[128,512]{1,0:T(8,128)(2,1)S(1)}, u32[]{:S(2)}, u32[]{:S(2)}) collective-permute-start(bf16[128,512]{1,0:T(8,128)(2,1)S(1)} %shard_map.129), channel_id=1, source_target_pairs={{0,12},{1,13},{2,14},{3,15},{4,8},{5,9},{6,10},{7,11},{8,4},{9,5},... | collective-permute-start | bytes 393224 | tf_op jit(solution)/shard_map/ppermute | solution.py:24
  251.6 2.4 collective-permute-done.63
  256.3 3.0 %shard_map.130.rest_6_ = f32[128,384]{1,0:T(8,128)S(1)} custom-call(s32[4]{0:T(128)S(1)} %pad_add_fusion.place, bf16[2,16,512,384]{3,2,1,0:T(8,128)(2,1)} %bitcast.85, bf16[2,16,512,384]{3,2,1,0:T(8,128)(2,1)} %bitcast.86, bf16[2,16,512,384]{3,2,1,0:T(8,128)(2,1)} %bitcast.87, bf16[2,16,512,384]{3,2,1,0:T(8,128)(2,1)} %bitcast.88, ...), custom_call_target="tpu_custom_call" | custom-call | flops 402653184 | bytes 3145728 | tf_op jit(solution)/shard_map/pallas_call | solution.py:98
  259.3 4.3 %shard_map.131 = f32[384,128]{1,0:T(8,128)} custom-call(s32[4]{0:T(128)S(1)} %pad_add_fusion.place, bf16[2,16,512,384]{3,2,1,0:T(8,128)(2,1)} %bitcast.89, bf16[2,16,512,384]{3,2,1,0:T(8,128)(2,1)} %bitcast.90, bf16[2,16,512,384]{3,2,1,0:T(8,128)(2,1)} %bitcast.91, bf16[2,16,512,384]{3,2,1,0:T(8,128)(2,1)} %bitcast.92, ...), custom_call_target="tpu_custom_call" | custom-call | flops 402653184 | bytes 3145728 | tf_op jit(solution)/shard_map/pallas_call | solution.py:98
  (146 shorter events, 79.5 us)
Async XLA Ops:
  15.0 8.5 %collective-permute-start.2 = (s16[528,128]{1,0:T(8,128)(2,1)S(1)}, s16[528,128]{1,0:T(8,128)(2,1)S(1)}, u32[]{:S(2)}, u32[]{:S(2)}) collective-permute-start(s16[528,128]{1,0:T(8,128)(2,1)S(1)} %get-tuple-element.50), channel_id=1, source_target_pairs={{0,12},{1,13},{2,14},{3,15},{4,8},{5,9},{6,10},{7,11},{8,4},{9,5},... | collective-permute-start | bytes 405512 | tf_op jit(solution)/shard_map/ppermute | solution.py:24
  16.2 13.1 %collective-permute-start.3 = (s16[528,128]{1,0:T(8,128)(2,1)S(1)}, s16[528,128]{1,0:T(8,128)(2,1)S(1)}, u32[]{:S(2)}, u32[]{:S(2)}) collective-permute-start(s16[528,128]{1,0:T(8,128)(2,1)S(1)} %get-tuple-element.51), channel_id=1, source_target_pairs={{0,10},{1,11},{2,8},{3,9},{4,14},{5,15},{6,12},{7,13},{8,2},{9,3},... | collective-permute-start | bytes 405512 | tf_op jit(solution)/shard_map/ppermute | solution.py:24
  16.4 13.0 %collective-permute-start.4 = (s16[528,128]{1,0:T(8,128)(2,1)S(1)}, s16[528,128]{1,0:T(8,128)(2,1)S(1)}, u32[]{:S(2)}, u32[]{:S(2)}) collective-permute-start(s16[528,128]{1,0:T(8,128)(2,1)S(1)} %get-tuple-element.52), channel_id=1, source_target_pairs={{0,8},{1,9},{2,10},{3,11},{4,12},{5,13},{6,14},{7,15},{8,0},{9,1},... | collective-permute-start | bytes 405512 | tf_op jit(solution)/shard_map/ppermute | solution.py:24
  17.7 11.7 %collective-permute-start.5 = (s16[528,128]{1,0:T(8,128)(2,1)S(1)}, s16[528,128]{1,0:T(8,128)(2,1)S(1)}, u32[]{:S(2)}, u32[]{:S(2)}) collective-permute-start(s16[528,128]{1,0:T(8,128)(2,1)S(1)} %get-tuple-element.53), channel_id=1, source_target_pairs={{0,6},{1,7},{2,4},{3,5},{4,2},{5,3},{6,0},{7,1},{8,14},{9,15},{10,... | collective-permute-start | bytes 405512 | tf_op jit(solution)/shard_map/ppermute | solution.py:24
  19.8 9.5 %collective-permute-start.6 = (s16[528,128]{1,0:T(8,128)(2,1)S(1)}, s16[528,128]{1,0:T(8,128)(2,1)S(1)}, u32[]{:S(2)}, u32[]{:S(2)}) collective-permute-start(s16[528,128]{1,0:T(8,128)(2,1)S(1)} %get-tuple-element.54), channel_id=1, source_target_pairs={{0,4},{1,5},{2,6},{3,7},{4,0},{5,1},{6,2},{7,3},{8,12},{9,13},{10,... | collective-permute-start | bytes 405512 | tf_op jit(solution)/shard_map/ppermute | solution.py:24
  33.8 7.6 %collective-permute-start.10 = (s16[528,128]{1,0:T(8,128)(2,1)S(1)}, s16[528,128]{1,0:T(8,128)(2,1)S(1)}, u32[]{:S(2)}, u32[]{:S(2)}) collective-permute-start(s16[528,128]{1,0:T(8,128)(2,1)S(1)} %shard_map.107), channel_id=1, source_target_pairs={{0,10},{1,11},{2,8},{3,9},{4,14},{5,15},{6,12},{7,13},{8,2},{9,3},... | collective-permute-start | bytes 405512 | tf_op jit(solution)/shard_map/ppermute | solution.py:24
  34.4 9.4 %collective-permute-start.11 = (s16[528,128]{1,0:T(8,128)(2,1)S(1)}, s16[528,128]{1,0:T(8,128)(2,1)S(1)}, u32[]{:S(2)}, u32[]{:S(2)}) collective-permute-start(s16[528,128]{1,0:T(8,128)(2,1)S(1)} %shard_map.107), channel_id=1, source_target_pairs={{0,8},{1,9},{2,10},{3,11},{4,12},{5,13},{6,14},{7,15},{8,0},{9,1},... | collective-permute-start | bytes 405512 | tf_op jit(solution)/shard_map/ppermute | solution.py:24
  35.2 8.6 %collective-permute-start.12 = (s16[528,128]{1,0:T(8,128)(2,1)S(1)}, s16[528,128]{1,0:T(8,128)(2,1)S(1)}, u32[]{:S(2)}, u32[]{:S(2)}) collective-permute-start(s16[528,128]{1,0:T(8,128)(2,1)S(1)} %shard_map.107), channel_id=1, source_target_pairs={{0,6},{1,7},{2,4},{3,5},{4,2},{5,3},{6,0},{7,1},{8,14},{9,15},{10,... | collective-permute-start | bytes 405512 | tf_op jit(solution)/shard_map/ppermute | solution.py:24
  37.0 8.9 %collective-permute-start.13 = (s16[528,128]{1,0:T(8,128)(2,1)S(1)}, s16[528,128]{1,0:T(8,128)(2,1)S(1)}, u32[]{:S(2)}, u32[]{:S(2)}) collective-permute-start(s16[528,128]{1,0:T(8,128)(2,1)S(1)} %shard_map.107), channel_id=1, source_target_pairs={{0,4},{1,5},{2,6},{3,7},{4,0},{5,1},{6,2},{7,3},{8,12},{9,13},{10,... | collective-permute-start | bytes 405512 | tf_op jit(solution)/shard_map/ppermute | solution.py:24
  37.8 9.1 %collective-permute-start.14 = (s16[528,128]{1,0:T(8,128)(2,1)S(1)}, s16[528,128]{1,0:T(8,128)(2,1)S(1)}, u32[]{:S(2)}, u32[]{:S(2)}) collective-permute-start(s16[528,128]{1,0:T(8,128)(2,1)S(1)} %shard_map.107), channel_id=1, source_target_pairs={{0,2},{1,3},{2,0},{3,1},{4,6},{5,7},{6,4},{7,5},{8,10},{9,11},{10,... | collective-permute-start | bytes 405512 | tf_op jit(solution)/shard_map/ppermute | solution.py:24
  46.9 8.3 %collective-permute-start.15 = (s16[8,528,128]{2,1,0:T(8,128)(2,1)S(1)}, s16[8,528,128]{2,1,0:T(8,128)(2,1)S(1)}, u32[]{:S(2)}, u32[]{:S(2)}) collective-permute-start(s16[8,528,128]{2,1,0:T(8,128)(2,1)S(1)} %bitcast_dynamic-update-slice_fusion.16.rest_2_), channel_id=1, source_target_pairs={{0,1},{1,0},{2,3},{3,2},{4,5},{5,4},{6,7},{7,6},{8,9},{9,8},{10,11... | collective-permute-start | bytes 3244040 | tf_op jit(solution)/shard_map/ppermute | solution.py:24
  74.2 12.3 %collective-permute-start.17 = (s16[528,128]{1,0:T(8,128)(2,1)S(1)}, s16[528,128]{1,0:T(8,128)(2,1)S(1)}, u32[]{:S(2)}, u32[]{:S(2)}) collective-permute-start(s16[528,128]{1,0:T(8,128)(2,1)S(1)} %get-tuple-element.58), channel_id=1, source_target_pairs={{0,14},{1,15},{2,12},{3,13},{4,10},{5,11},{6,8},{7,9},{8,6},{9,7},... | collective-permute-start | bytes 405512 | tf_op jit(solution)/shard_map/ppermute | solution.py:24
  76.0 10.5 %collective-permute-start.18 = (s16[528,128]{1,0:T(8,128)(2,1)S(1)}, s16[528,128]{1,0:T(8,128)(2,1)S(1)}, u32[]{:S(2)}, u32[]{:S(2)}) collective-permute-start(s16[528,128]{1,0:T(8,128)(2,1)S(1)} %get-tuple-element.59), channel_id=1, source_target_pairs={{0,12},{1,13},{2,14},{3,15},{4,8},{5,9},{6,10},{7,11},{8,4},{9,5},... | collective-permute-start | bytes 405512 | tf_op jit(solution)/shard_map/ppermute | solution.py:24
  78.0 10.8 %collective-permute-start.19 = (s16[528,128]{1,0:T(8,128)(2,1)S(1)}, s16[528,128]{1,0:T(8,128)(2,1)S(1)}, u32[]{:S(2)}, u32[]{:S(2)}) collective-permute-start(s16[528,128]{1,0:T(8,128)(2,1)S(1)} %get-tuple-element.60), channel_id=1, source_target_pairs={{0,10},{1,11},{2,8},{3,9},{4,14},{5,15},{6,12},{7,13},{8,2},{9,3},... | collective-permute-start | bytes 405512 | tf_op jit(solution)/shard_map/ppermute | solution.py:24
  78.7 12.2 %collective-permute-start.20 = (s16[528,128]{1,0:T(8,128)(2,1)S(1)}, s16[528,128]{1,0:T(8,128)(2,1)S(1)}, u32[]{:S(2)}, u32[]{:S(2)}) collective-permute-start(s16[528,128]{1,0:T(8,128)(2,1)S(1)} %get-tuple-element.61), channel_id=1, source_target_pairs={{0,8},{1,9},{2,10},{3,11},{4,12},{5,13},{6,14},{7,15},{8,0},{9,1},... | collective-permute-start | bytes 405512 | tf_op jit(solution)/shard_map/ppermute | solution.py:24
  83.2 7.8 %collective-permute-start.21 = (s16[528,128]{1,0:T(8,128)(2,1)S(1)}, s16[528,128]{1,0:T(8,128)(2,1)S(1)}, u32[]{:S(2)}, u32[]{:S(2)}) collective-permute-start(s16[528,128]{1,0:T(8,128)(2,1)S(1)} %get-tuple-element.62), channel_id=1, source_target_pairs={{0,6},{1,7},{2,4},{3,5},{4,2},{5,3},{6,0},{7,1},{8,14},{9,15},{10,... | collective-permute-start | bytes 405512 | tf_op jit(solution)/shard_map/ppermute | solution.py:24
  86.4 7.8 %collective-permute-start.22 = (s16[528,128]{1,0:T(8,128)(2,1)S(1)}, s16[528,128]{1,0:T(8,128)(2,1)S(1)}, u32[]{:S(2)}, u32[]{:S(2)}) collective-permute-start(s16[528,128]{1,0:T(8,128)(2,1)S(1)} %get-tuple-element.63), channel_id=1, source_target_pairs={{0,4},{1,5},{2,6},{3,7},{4,0},{5,1},{6,2},{7,3},{8,12},{9,13},{10,... | collective-permute-start | bytes 405512 | tf_op jit(solution)/shard_map/ppermute | solution.py:24
  86.5 8.3 %collective-permute-start.23 = (s16[528,128]{1,0:T(8,128)(2,1)S(1)}, s16[528,128]{1,0:T(8,128)(2,1)S(1)}, u32[]{:S(2)}, u32[]{:S(2)}) collective-permute-start(s16[528,128]{1,0:T(8,128)(2,1)S(1)} %get-tuple-element.64), channel_id=1, source_target_pairs={{0,2},{1,3},{2,0},{3,1},{4,6},{5,7},{6,4},{7,5},{8,10},{9,11},{10,... | collective-permute-start | bytes 405512 | tf_op jit(solution)/shard_map/ppermute | solution.py:24
  95.8 8.4 %collective-permute-start.24 = (s16[528,128]{1,0:T(8,128)(2,1)S(1)}, s16[528,128]{1,0:T(8,128)(2,1)S(1)}, u32[]{:S(2)}, u32[]{:S(2)}) collective-permute-start(s16[528,128]{1,0:T(8,128)(2,1)S(1)} %shard_map.113.own), channel_id=1, source_target_pairs={{0,16},{1,17},{2,18},{3,19},{4,20},{5,21},{6,22},{7,23},{8,24},{9,... | collective-permute-start | bytes 405512 | tf_op jit(solution)/shard_map/ppermute | solution.py:24
  105.0 9.5 %collective-permute-start.26 = (s16[528,128]{1,0:T(8,128)(2,1)S(1)}, s16[528,128]{1,0:T(8,128)(2,1)S(1)}, u32[]{:S(2)}, u32[]{:S(2)}) collective-permute-start(s16[528,128]{1,0:T(8,128)(2,1)S(1)} %shard_map.114), channel_id=1, source_target_pairs={{0,12},{1,13},{2,14},{3,15},{4,8},{5,9},{6,10},{7,11},{8,4},{9,5},... | collective-permute-start | bytes 405512 | tf_op jit(solution)/shard_map/ppermute | solution.py:24
  107.3 8.2 %collective-permute-start.27 = (s16[528,128]{1,0:T(8,128)(2,1)S(1)}, s16[528,128]{1,0:T(8,128)(2,1)S(1)}, u32[]{:S(2)}, u32[]{:S(2)}) collective-permute-start(s16[528,128]{1,0:T(8,128)(2,1)S(1)} %shard_map.114), channel_id=1, source_target_pairs={{0,10},{1,11},{2,8},{3,9},{4,14},{5,15},{6,12},{7,13},{8,2},{9,3},... | collective-permute-start | bytes 405512 | tf_op jit(solution)/shard_map/ppermute | solution.py:24
  107.3 9.5 %collective-permute-start.28 = (s16[528,128]{1,0:T(8,128)(2,1)S(1)}, s16[528,128]{1,0:T(8,128)(2,1)S(1)}, u32[]{:S(2)}, u32[]{:S(2)}) collective-permute-start(s16[528,128]{1,0:T(8,128)(2,1)S(1)} %shard_map.114), channel_id=1, source_target_pairs={{0,8},{1,9},{2,10},{3,11},{4,12},{5,13},{6,14},{7,15},{8,0},{9,1},... | collective-permute-start | bytes 405512 | tf_op jit(solution)/shard_map/ppermute | solution.py:24
  111.7 8.3 %collective-permute-start.30 = (s16[528,128]{1,0:T(8,128)(2,1)S(1)}, s16[528,128]{1,0:T(8,128)(2,1)S(1)}, u32[]{:S(2)}, u32[]{:S(2)}) collective-permute-start(s16[528,128]{1,0:T(8,128)(2,1)S(1)} %shard_map.114), channel_id=1, source_target_pairs={{0,4},{1,5},{2,6},{3,7},{4,0},{5,1},{6,2},{7,3},{8,12},{9,13},{10,... | collective-permute-start | bytes 405512 | tf_op jit(solution)/shard_map/ppermute | solution.py:24
  142.7 8.7 %collective-permute-start.34 = (s16[144,512]{1,0:T(8,128)(2,1)S(1)}, s16[144,512]{1,0:T(8,128)(2,1)S(1)}, u32[]{:S(2)}, u32[]{:S(2)}) collective-permute-start(s16[144,512]{1,0:T(8,128)(2,1)S(1)} %get-tuple-element.67), channel_id=1, source_target_pairs={{0,14},{1,15},{2,12},{3,13},{4,10},{5,11},{6,8},{7,9},{8,6},{9,7},... | collective-permute-start | bytes 442376 | tf_op jit(solution)/shard_map/ppermute | solution.py:24
  142.8 10.2 %collective-permute-start.35 = (s16[144,512]{1,0:T(8,128)(2,1)S(1)}, s16[144,512]{1,0:T(8,128)(2,1)S(1)}, u32[]{:S(2)}, u32[]{:S(2)}) collective-permute-start(s16[144,512]{1,0:T(8,128)(2,1)S(1)} %get-tuple-element.68), channel_id=1, source_target_pairs={{0,12},{1,13},{2,14},{3,15},{4,8},{5,9},{6,10},{7,11},{8,4},{9,5},... | collective-permute-start | bytes 442376 | tf_op jit(solution)/shard_map/ppermute | solution.py:24
  145.2 10.8 %collective-permute-start.36 = (s16[144,512]{1,0:T(8,128)(2,1)S(1)}, s16[144,512]{1,0:T(8,128)(2,1)S(1)}, u32[]{:S(2)}, u32[]{:S(2)}) collective-permute-start(s16[144,512]{1,0:T(8,128)(2,1)S(1)} %get-tuple-element.69), channel_id=1, source_target_pairs={{0,10},{1,11},{2,8},{3,9},{4,14},{5,15},{6,12},{7,13},{8,2},{9,3},... | collective-permute-start | bytes 442376 | tf_op jit(solution)/shard_map/ppermute | solution.py:24
  145.8 13.3 %collective-permute-start.37 = (s16[144,512]{1,0:T(8,128)(2,1)S(1)}, s16[144,512]{1,0:T(8,128)(2,1)S(1)}, u32[]{:S(2)}, u32[]{:S(2)}) collective-permute-start(s16[144,512]{1,0:T(8,128)(2,1)S(1)} %get-tuple-element.70), channel_id=1, source_target_pairs={{0,8},{1,9},{2,10},{3,11},{4,12},{5,13},{6,14},{7,15},{8,0},{9,1},... | collective-permute-start | bytes 442376 | tf_op jit(solution)/shard_map/ppermute | solution.py:24
  150.2 9.4 %collective-permute-start.38 = (s16[144,512]{1,0:T(8,128)(2,1)S(1)}, s16[144,512]{1,0:T(8,128)(2,1)S(1)}, u32[]{:S(2)}, u32[]{:S(2)}) collective-permute-start(s16[144,512]{1,0:T(8,128)(2,1)S(1)} %get-tuple-element.71), channel_id=1, source_target_pairs={{0,6},{1,7},{2,4},{3,5},{4,2},{5,3},{6,0},{7,1},{8,14},{9,15},{10,... | collective-permute-start | bytes 442376 | tf_op jit(solution)/shard_map/ppermute | solution.py:24
  151.4 8.1 %collective-permute-start.39 = (s16[144,512]{1,0:T(8,128)(2,1)S(1)}, s16[144,512]{1,0:T(8,128)(2,1)S(1)}, u32[]{:S(2)}, u32[]{:S(2)}) collective-permute-start(s16[144,512]{1,0:T(8,128)(2,1)S(1)} %get-tuple-element.72), channel_id=1, source_target_pairs={{0,4},{1,5},{2,6},{3,7},{4,0},{5,1},{6,2},{7,3},{8,12},{9,13},{10,... | collective-permute-start | bytes 442376 | tf_op jit(solution)/shard_map/ppermute | solution.py:24
  153.0 9.8 %collective-permute-start.40 = (s16[144,512]{1,0:T(8,128)(2,1)S(1)}, s16[144,512]{1,0:T(8,128)(2,1)S(1)}, u32[]{:S(2)}, u32[]{:S(2)}) collective-permute-start(s16[144,512]{1,0:T(8,128)(2,1)S(1)} %get-tuple-element.73), channel_id=1, source_target_pairs={{0,2},{1,3},{2,0},{3,1},{4,6},{5,7},{6,4},{7,5},{8,10},{9,11},{10,... | collective-permute-start | bytes 442376 | tf_op jit(solution)/shard_map/ppermute | solution.py:24
  163.8 8.8 %collective-permute-start.41 = (s16[144,512]{1,0:T(8,128)(2,1)S(1)}, s16[144,512]{1,0:T(8,128)(2,1)S(1)}, u32[]{:S(2)}, u32[]{:S(2)}) collective-permute-start(s16[144,512]{1,0:T(8,128)(2,1)S(1)} %shard_map.120.own), channel_id=1, source_target_pairs={{0,16},{1,17},{2,18},{3,19},{4,20},{5,21},{6,22},{7,23},{8,24},{9,... | collective-permute-start | bytes 442376 | tf_op jit(solution)/shard_map/ppermute | solution.py:24
  173.4 10.4 %collective-permute-start.43 = (s16[144,512]{1,0:T(8,128)(2,1)S(1)}, s16[144,512]{1,0:T(8,128)(2,1)S(1)}, u32[]{:S(2)}, u32[]{:S(2)}) collective-permute-start(s16[144,512]{1,0:T(8,128)(2,1)S(1)} %shard_map.121), channel_id=1, source_target_pairs={{0,12},{1,13},{2,14},{3,15},{4,8},{5,9},{6,10},{7,11},{8,4},{9,5},... | collective-permute-start | bytes 442376 | tf_op jit(solution)/shard_map/ppermute | solution.py:24
  175.9 10.8 %collective-permute-start.44 = (s16[144,512]{1,0:T(8,128)(2,1)S(1)}, s16[144,512]{1,0:T(8,128)(2,1)S(1)}, u32[]{:S(2)}, u32[]{:S(2)}) collective-permute-start(s16[144,512]{1,0:T(8,128)(2,1)S(1)} %shard_map.121), channel_id=1, source_target_pairs={{0,10},{1,11},{2,8},{3,9},{4,14},{5,15},{6,12},{7,13},{8,2},{9,3},... | collective-permute-start | bytes 442376 | tf_op jit(solution)/shard_map/ppermute | solution.py:24
  176.5 12.9 %collective-permute-start.45 = (s16[144,512]{1,0:T(8,128)(2,1)S(1)}, s16[144,512]{1,0:T(8,128)(2,1)S(1)}, u32[]{:S(2)}, u32[]{:S(2)}) collective-permute-start(s16[144,512]{1,0:T(8,128)(2,1)S(1)} %shard_map.121), channel_id=1, source_target_pairs={{0,8},{1,9},{2,10},{3,11},{4,12},{5,13},{6,14},{7,15},{8,0},{9,1},... | collective-permute-start | bytes 442376 | tf_op jit(solution)/shard_map/ppermute | solution.py:24
  178.1 11.2 %collective-permute-start.46 = (s16[144,512]{1,0:T(8,128)(2,1)S(1)}, s16[144,512]{1,0:T(8,128)(2,1)S(1)}, u32[]{:S(2)}, u32[]{:S(2)}) collective-permute-start(s16[144,512]{1,0:T(8,128)(2,1)S(1)} %shard_map.121), channel_id=1, source_target_pairs={{0,6},{1,7},{2,4},{3,5},{4,2},{5,3},{6,0},{7,1},{8,14},{9,15},{10,... | collective-permute-start | bytes 442376 | tf_op jit(solution)/shard_map/ppermute | solution.py:24
  180.2 10.2 %collective-permute-start.47 = (s16[144,512]{1,0:T(8,128)(2,1)S(1)}, s16[144,512]{1,0:T(8,128)(2,1)S(1)}, u32[]{:S(2)}, u32[]{:S(2)}) collective-permute-start(s16[144,512]{1,0:T(8,128)(2,1)S(1)} %shard_map.121), channel_id=1, source_target_pairs={{0,4},{1,5},{2,6},{3,7},{4,0},{5,1},{6,2},{7,3},{8,12},{9,13},{10,... | collective-permute-start | bytes 442376 | tf_op jit(solution)/shard_map/ppermute | solution.py:24
  190.9 7.6 %collective-permute-start.49 = (s16[8,144,512]{2,1,0:T(8,128)(2,1)S(1)}, s16[8,144,512]{2,1,0:T(8,128)(2,1)S(1)}, u32[]{:S(2)}, u32[]{:S(2)}) collective-permute-start(s16[8,144,512]{2,1,0:T(8,128)(2,1)S(1)} %bitcast_dynamic-update-slice_fusion.rest_2_.mine), channel_id=1, source_target_pairs={{0,1},{1,0},{2,3},{3,2},{4,5},{5,4},{6,7},{7,6},{8,9},{9,8},{10,11... | collective-permute-start | bytes 3538952 | tf_op jit(solution)/shard_map/ppermute | solution.py:24
  217.6 9.6 %collective-permute-start.51 = (s16[144,512]{1,0:T(8,128)(2,1)S(1)}, s16[144,512]{1,0:T(8,128)(2,1)S(1)}, u32[]{:S(2)}, u32[]{:S(2)}) collective-permute-start(s16[144,512]{1,0:T(8,128)(2,1)S(1)} %get-tuple-element.78), channel_id=1, source_target_pairs={{0,14},{1,15},{2,12},{3,13},{4,10},{5,11},{6,8},{7,9},{8,6},{9,7},... | collective-permute-start | bytes 442376 | tf_op jit(solution)/shard_map/ppermute | solution.py:24
  217.7 10.2 %collective-permute-start.52 = (s16[144,512]{1,0:T(8,128)(2,1)S(1)}, s16[144,512]{1,0:T(8,128)(2,1)S(1)}, u32[]{:S(2)}, u32[]{:S(2)}) collective-permute-start(s16[144,512]{1,0:T(8,128)(2,1)S(1)} %get-tuple-element.79), channel_id=1, source_target_pairs={{0,12},{1,13},{2,14},{3,15},{4,8},{5,9},{6,10},{7,11},{8,4},{9,5},... | collective-permute-start | bytes 442376 | tf_op jit(solution)/shard_map/ppermute | solution.py:24
  219.8 14.4 %collective-permute-start.53 = (s16[144,512]{1,0:T(8,128)(2,1)S(1)}, s16[144,512]{1,0:T(8,128)(2,1)S(1)}, u32[]{:S(2)}, u32[]{:S(2)}) collective-permute-start(s16[144,512]{1,0:T(8,128)(2,1)S(1)} %get-tuple-element.80), channel_id=1, source_target_pairs={{0,10},{1,11},{2,8},{3,9},{4,14},{5,15},{6,12},{7,13},{8,2},{9,3},... | collective-permute-start | bytes 442376 | tf_op jit(solution)/shard_map/ppermute | solution.py:24
  220.4 13.9 %collective-permute-start.54 = (s16[144,512]{1,0:T(8,128)(2,1)S(1)}, s16[144,512]{1,0:T(8,128)(2,1)S(1)}, u32[]{:S(2)}, u32[]{:S(2)}) collective-permute-start(s16[144,512]{1,0:T(8,128)(2,1)S(1)} %get-tuple-element.81), channel_id=1, source_target_pairs={{0,8},{1,9},{2,10},{3,11},{4,12},{5,13},{6,14},{7,15},{8,0},{9,1},... | collective-permute-start | bytes 442376 | tf_op jit(solution)/shard_map/ppermute | solution.py:24
  225.9 8.9 %collective-permute-start.55 = (s16[144,512]{1,0:T(8,128)(2,1)S(1)}, s16[144,512]{1,0:T(8,128)(2,1)S(1)}, u32[]{:S(2)}, u32[]{:S(2)}) collective-permute-start(s16[144,512]{1,0:T(8,128)(2,1)S(1)} %get-tuple-element.82), channel_id=1, source_target_pairs={{0,6},{1,7},{2,4},{3,5},{4,2},{5,3},{6,0},{7,1},{8,14},{9,15},{10,... | collective-permute-start | bytes 442376 | tf_op jit(solution)/shard_map/ppermute | solution.py:24
  227.9 9.4 %collective-permute-start.57 = (s16[144,512]{1,0:T(8,128)(2,1)S(1)}, s16[144,512]{1,0:T(8,128)(2,1)S(1)}, u32[]{:S(2)}, u32[]{:S(2)}) collective-permute-start(s16[144,512]{1,0:T(8,128)(2,1)S(1)} %get-tuple-element.84), channel_id=1, source_target_pairs={{0,2},{1,3},{2,0},{3,1},{4,6},{5,7},{6,4},{7,5},{8,10},{9,11},{10,... | collective-permute-start | bytes 442376 | tf_op jit(solution)/shard_map/ppermute | solution.py:24
  238.4 9.6 %collective-permute-start.59 = (bf16[128,512]{1,0:T(8,128)(2,1)S(1)}, bf16[128,512]{1,0:T(8,128)(2,1)S(1)}, u32[]{:S(2)}, u32[]{:S(2)}) collective-permute-start(bf16[128,512]{1,0:T(8,128)(2,1)S(1)} %shard_map.129), channel_id=1, source_target_pairs={{0,12},{1,13},{2,14},{3,15},{4,8},{5,9},{6,10},{7,11},{8,4},{9,5},... | collective-permute-start | bytes 393224 | tf_op jit(solution)/shard_map/ppermute | solution.py:24
  241.5 8.5 %collective-permute-start.60 = (bf16[128,512]{1,0:T(8,128)(2,1)S(1)}, bf16[128,512]{1,0:T(8,128)(2,1)S(1)}, u32[]{:S(2)}, u32[]{:S(2)}) collective-permute-start(bf16[128,512]{1,0:T(8,128)(2,1)S(1)} %shard_map.129), channel_id=1, source_target_pairs={{0,10},{1,11},{2,8},{3,9},{4,14},{5,15},{6,12},{7,13},{8,2},{9,3},... | collective-permute-start | bytes 393224 | tf_op jit(solution)/shard_map/ppermute | solution.py:24
  241.5 10.0 %collective-permute-start.61 = (bf16[128,512]{1,0:T(8,128)(2,1)S(1)}, bf16[128,512]{1,0:T(8,128)(2,1)S(1)}, u32[]{:S(2)}, u32[]{:S(2)}) collective-permute-start(bf16[128,512]{1,0:T(8,128)(2,1)S(1)} %shard_map.129), channel_id=1, source_target_pairs={{0,8},{1,9},{2,10},{3,11},{4,12},{5,13},{6,14},{7,15},{8,0},{9,1},... | collective-permute-start | bytes 393224 | tf_op jit(solution)/shard_map/ppermute | solution.py:24
  243.0 8.6 %collective-permute-start.62 = (bf16[128,512]{1,0:T(8,128)(2,1)S(1)}, bf16[128,512]{1,0:T(8,128)(2,1)S(1)}, u32[]{:S(2)}, u32[]{:S(2)}) collective-permute-start(bf16[128,512]{1,0:T(8,128)(2,1)S(1)} %shard_map.129), channel_id=1, source_target_pairs={{0,6},{1,7},{2,4},{3,5},{4,2},{5,3},{6,0},{7,1},{8,14},{9,15},{10,... | collective-permute-start | bytes 393224 | tf_op jit(solution)/shard_map/ppermute | solution.py:24
  244.4 9.5 %collective-permute-start.63 = (bf16[128,512]{1,0:T(8,128)(2,1)S(1)}, bf16[128,512]{1,0:T(8,128)(2,1)S(1)}, u32[]{:S(2)}, u32[]{:S(2)}) collective-permute-start(bf16[128,512]{1,0:T(8,128)(2,1)S(1)} %shard_map.129), channel_id=1, source_target_pairs={{0,4},{1,5},{2,6},{3,7},{4,0},{5,1},{6,2},{7,3},{8,12},{9,13},{10,... | collective-permute-start | bytes 393224 | tf_op jit(solution)/shard_map/ppermute | solution.py:24
  (18 other events, 101.8 us)

commit v2 on v1

--- a/solution.py
+++ b/solution.py
@@ -16,7 +16,7 @@
 GROUP = 2 * NEAR
 BATCHES = ((4, 4), (0, 4))
 PAD = 16
-VMEM = 24 << 20
+VMEM = 12 << 20
 
 
 def swap(block, offset):
@@ -361,7 +361,7 @@
             + [whole(r.shape) for r in result],
             [out_whole((count, columns), F32)] + [out_whole((columns, count), F32)] * flip,
             [pltpu.VMEM((count, 2 * columns), F32), pltpu.VMEM((count, columns), F32)],
-            [at_rest(factor)] * per + [stacks[flip], *result],
+            [factor] * per + [stacks[flip], *result],
             4 * count * size * columns,
             2 * count * size,
         )
@@ -457,7 +457,7 @@
         place,
         functools.partial(back_kernel, start_at),
         specs,
-        [at_rest(factor)] * per + [vector],
+        [factor] * per + [vector],
         (columns, chunk),
         [pltpu.VMEM((2 * columns, count), BF16)],
         8 * count * size * columns,
@@ -579,7 +579,7 @@
     inverse_t = at_rest(leaf_inverse.T)
     tiles = at_rest(jnp.transpose(tile_mask, (2, 0, 1)))
     coupling = at_rest(leaf_coupling.reshape(levels, GROUP, chunk, local_rows))
-    low_blocks = at_rest(low_coupling.reshape(GROUP, chunk, low_count))
+    low_blocks = low_coupling.reshape(GROUP, chunk, low_count)
     low_rhs, top_rhs = at_rest(low_rhs), at_rest(top_rhs)
 
     leaf_flops = 2 * sep_size * local_rows * columns

time: 264 us -> 243 us (0.920)
  Pallas kernels: 104 us -> 80.8 us
  starting transfers between devices: 69.3 us -> 75 us
  waiting for transfers between devices: 87.6 us -> 84.3 us
    pallas_call x28, Pallas kernels: 104 us -> 80.8 us  [call(): pl.pallas_call(kernel, grid_spec=pltpu.PrefetchScalarGridSpec(num_scalar_...]
    ppermute x66, starting transfers between devices: 69.3 us -> 75 us  [swap(): return lax.ppermute(block, AXES, [(at, at ^ offset) for at in range(count)])]
    ppermute x66, waiting for transfers between devices: 87.6 us -> 84.3 us  [swap(): return lax.ppermute(block, AXES, [(at, at ^ offset) for at in range(count)])]
  transfers between devices with their start and end apart: 66 -> 66, of which waited for: 39 -> 36; matrix products, arithmetic and copies ran while one was open for 0% -> 0% of each run, Pallas kernels for 15% -> 13%
where the time goes in v2:
time: 243 us
  waiting for transfers between devices  84.3 us (35%)
  Pallas kernels  80.8 us (33%)
  starting transfers between devices  75 us (31%)
    ppermute x66, waiting for transfers between devices, swap(): return lax.ppermute(block, AXES, [(at, at ^ offset) for at in range(count)])  84.3 us
    pallas_call x28, Pallas kernels, call(): pl.pallas_call(kernel, grid_spec=pltpu.PrefetchScalarGridSpec(num_scalar_...  80.8 us
    ppermute x66, starting transfers between devices, swap(): return lax.ppermute(block, AXES, [(at, at ^ offset) for at in range(count)])  75 us
  transfers between devices with their start and end apart: 66, of which 36 were waited for; matrix products, arithmetic and copies ran while one was open for 0% of the time, Pallas kernels for 13%

profile of v2, /device:TPU:25, one launch (start us, length us, event | category | flops | bytes accessed | tf_op | source)
XLA Modules:
  0.0 242.9 jit_solution(15801659956034434382)
XLA Ops:
  0.8 4.6 %shard_map.104 = (s16[8,528,128]{2,1,0:T(8,128)(2,1)S(1)}, f32[384,128]{1,0:T(8,128)S(1)}, bf16[384,128]{1,0:T(8,128)(2,1)S(1)}, f32[2,128,384]{2,1,0:T(8,128)S(1)}) custom-call(s32[4]{0:T(128)S(1)} %pad_add_fusion.place, bf16[2,16,512,384]{3,2,1,0:T(8,128)(2,1)} %bitcast.92, bf16[2,16,512,384]{3,2,1,0:T(8,128)(2,1)} %bitcast.93, ...), custom_call_target="tpu_custom_call" | custom-call | flops 402653184 | bytes 3145728 | tf_op jit(solution)/shard_map/pallas_call | solution.py:98
  6.1 2.3 collective-permute-done.rest_7_
  8.4 4.7 %shard_map.106 = (f32[512,128]{1,0:T(8,128)S(1)}, s16[528,128]{1,0:T(8,128)(2,1)S(1)}, s16[528,128]{1,0:T(8,128)(2,1)S(1)}, s16[528,128]{1,0:T(8,128)(2,1)S(1)},...) custom-call(s32[4]{0:T(128)S(1)} %pad_add_fusion.place, ...), custom_call_target="tpu_custom_call" | custom-call | flops 402653184 | bytes 3145728 | tf_op jit(solution)/shard_map/pallas_call | solution.py:98
  17.9 2.2 collective-permute-start.5
  21.1 2.7 %collective-permute-done.2.rest_1_ = s16[528,128]{1,0:T(8,128)(2,1)S(1)} collective-permute-done((s16[528,128]{1,0:T(8,128)(2,1)S(1)}, s16[528,128]{1,0:T(8,128)(2,1)S(1)}, u32[]{:S(2)}, u32[]{:S(2)}) %collective-permute-start.2) | collective-permute-done | bytes 135200 | tf_op jit(solution)/shard_map/ppermute | solution.py:24
  24.4 5.3 %shard_map.105.rest_7_.rest_2_.rest_3_ = f32[16,512,128]{2,1,0:T(8,128)S(1)} custom-call(s32[4]{0:T(128)S(1)} %pad_add_fusion.place, f32[2,128,384]{2,1,0:T(8,128)S(1)} %get-tuple-element.45.spread.rest_4_, bf16[384,128]{1,0:T(8,128)(2,1)S(1)} %get-tuple-element.46.rounded.rest_5_, bf16[2,16,512,384]{3,2,1,0:T(8,128)(2,1)} %bitcast.100), custom_call_target="tpu_custom_call" | custom-call | flops 805306368 | bytes 6291456 | tf_op jit(solution)/shard_map/pallas_call | solution.py:98
  39.1 2.6 %collective-permute-done.10 = s16[528,128]{1,0:T(8,128)(2,1)S(1)} collective-permute-done((s16[528,128]{1,0:T(8,128)(2,1)S(1)}, s16[528,128]{1,0:T(8,128)(2,1)S(1)}, u32[]{:S(2)}, u32[]{:S(2)}) %collective-permute-start.10) | collective-permute-done | bytes 135200 | tf_op jit(solution)/shard_map/ppermute | solution.py:24
  41.7 2.4 %collective-permute-done.11 = s16[528,128]{1,0:T(8,128)(2,1)S(1)} collective-permute-done((s16[528,128]{1,0:T(8,128)(2,1)S(1)}, s16[528,128]{1,0:T(8,128)(2,1)S(1)}, u32[]{:S(2)}, u32[]{:S(2)}) %collective-permute-start.11) | collective-permute-done | bytes 135200 | tf_op jit(solution)/shard_map/ppermute | solution.py:24
  47.3 2.6 %collective-permute-start.15 = (s16[8,528,128]{2,1,0:T(8,128)(2,1)S(1)}, s16[8,528,128]{2,1,0:T(8,128)(2,1)S(1)}, u32[]{:S(2)}, u32[]{:S(2)}) collective-permute-start(s16[8,528,128]{2,1,0:T(8,128)(2,1)S(1)} %bitcast_dynamic-update-slice_fusion.16.rest_2_), channel_id=1, source_target_pairs={{0,1},{1,0},{2,3},{3,2},{4,5},{5,4},{6,7},{7,6},{8,9},{9,8},{10,11... | collective-permute-start | bytes 3244040 | tf_op jit(solution)/shard_map/ppermute | solution.py:24
  49.9 3.6 %shard_map.108.rest_3_ = f32[512,128]{1,0:T(8,128)S(1)} custom-call(s32[4]{0:T(128)S(1)} %pad_add_fusion.place, f32[512,8192]{1,0:T(8,128)S(1)} %bitcast.85, f32[512,8192]{1,0:T(8,128)S(1)} %bitcast.85, s16[8,528,128]{2,1,0:T(8,128)(2,1)S(1)} %bitcast_dynamic-update-slice_fusion.16.rest_2_), custom_call_target="tpu_custom_call" | custom-call | flops 2147483648 | bytes 8388608 | tf_op jit(solution)/shard_map/pallas_call | solution.py:98
  53.6 3.5 %shard_map.109 = (f32[512,128]{1,0:T(8,128)S(1)}, f32[128,512]{1,0:T(8,128)S(1)}) custom-call(s32[4]{0:T(128)S(1)} %pad_add_fusion.place, f32[512,8192]{1,0:T(8,128)S(1)} %bitcast.87, f32[512,8192]{1,0:T(8,128)S(1)} %bitcast.87, s16[8,528,128]{2,1,0:T(8,128)(2,1)S(1)} %collective-permute-done.15.rest_2_, f32[512,128]{1,0:T(8,128)S(1)} %shard_map.108.rest_3_), custom_call_target="tpu_custom_call" | custom-call | flops 2147483648 | bytes 8388608 | tf_op jit(solution)/shard_map/pallas_call | solution.py:98
  57.2 5.0 %shard_map.110 = s16[8,528,128]{2,1,0:T(8,128)(2,1)S(1)} custom-call(s32[4]{0:T(128)S(1)} %pad_add_fusion.place, f32[16,512,512]{2,1,0:T(8,128)S(1)} %bitcast.74, f32[16,512,512]{2,1,0:T(8,128)S(1)} %bitcast.75, f32[16,512,128]{2,1,0:T(8,128)S(1)} %shard_map.105.rest_7_.rest_2_.rest_3_, f32[16,512,128]{2,1,0:T(8,128)S(1)} %shard_map.105.rest_7_.rest_2_.rest_3_, ...), custom_call_target="tpu_custom_call" | custom-call | flops 2147483648 | bytes 8388608 | tf_op jit(solution)/shard_map/pallas_call | solution.py:98
  62.2 2.3 collective-permute-start.16
  64.5 2.3 collective-permute-done.16.rest_6_
  66.8 3.4 %shard_map.112 = (s16[528,128]{1,0:T(8,128)(2,1)S(1)}, s16[528,128]{1,0:T(8,128)(2,1)S(1)}, s16[528,128]{1,0:T(8,128)(2,1)S(1)}, s16[528,128]{1,0:T(8,128)(2,1)S(1)}) custom-call(s32[4]{0:T(128)S(1)} %pad_add_fusion.place, f32[16,512,512]{2,1,0:T(8,128)S(1)} %bitcast.76, f32[16,512,512]{2,1,0:T(8,128)S(1)} %bitcast.77, ...), custom_call_target="tpu_custom_call" | custom-call | flops 1073741824 | bytes 4194304 | tf_op jit(solution)/shard_map/pallas_call | solution.py:98
  75.0 3.9 %shard_map.111 = (f32[512,128]{1,0:T(8,128)S(1)}, s16[528,128]{1,0:T(8,128)(2,1)S(1)}, s16[528,128]{1,0:T(8,128)(2,1)S(1)}, s16[528,128]{1,0:T(8,128)(2,1)S(1)}) custom-call(s32[4]{0:T(128)S(1)} %pad_add_fusion.place, f32[16,512,512]{2,1,0:T(8,128)S(1)} %bitcast.78, f32[16,512,512]{2,1,0:T(8,128)S(1)} %bitcast.79, ...), custom_call_target="tpu_custom_call" | custom-call | flops 1073741824 | bytes 4194304 | tf_op jit(solution)/shard_map/pallas_call | solution.py:98
  83.2 2.6 %collective-permute-done.20.rest_3_ = s16[528,128]{1,0:T(8,128)(2,1)S(1)} collective-permute-done((s16[528,128]{1,0:T(8,128)(2,1)S(1)}, s16[528,128]{1,0:T(8,128)(2,1)S(1)}, u32[]{:S(2)}, u32[]{:S(2)}) %collective-permute-start.20) | collective-permute-done | bytes 135200 | tf_op jit(solution)/shard_map/ppermute | solution.py:24
  86.0 2.2 collective-permute-done.22.rest_5_
  90.4 8.2 %collective-permute-done.24.rest_0_ = s16[528,128]{1,0:T(8,128)(2,1)S(1)} collective-permute-done((s16[528,128]{1,0:T(8,128)(2,1)S(1)}, s16[528,128]{1,0:T(8,128)(2,1)S(1)}, u32[]{:S(2)}, u32[]{:S(2)}) %collective-permute-start.24) | collective-permute-done | bytes 135200 | tf_op jit(solution)/shard_map/ppermute | solution.py:24
  99.4 2.9 %collective-permute-start.26 = (s16[528,128]{1,0:T(8,128)(2,1)S(1)}, s16[528,128]{1,0:T(8,128)(2,1)S(1)}, u32[]{:S(2)}, u32[]{:S(2)}) collective-permute-start(s16[528,128]{1,0:T(8,128)(2,1)S(1)} %shard_map.114), channel_id=1, source_target_pairs={{0,12},{1,13},{2,14},{3,15},{4,8},{5,9},{6,10},{7,11},{8,4},{9,5},... | collective-permute-start | bytes 405512 | tf_op jit(solution)/shard_map/ppermute | solution.py:24
  108.7 2.4 collective-permute-done.27
  112.4 2.4 %collective-permute-done.30 = s16[528,128]{1,0:T(8,128)(2,1)S(1)} collective-permute-done((s16[528,128]{1,0:T(8,128)(2,1)S(1)}, s16[528,128]{1,0:T(8,128)(2,1)S(1)}, u32[]{:S(2)}, u32[]{:S(2)}) %collective-permute-start.30) | collective-permute-done | bytes 135200 | tf_op jit(solution)/shard_map/ppermute | solution.py:24
  116.9 2.7 %shard_map.115.rest_3_ = f32[256,128]{1,0:T(8,128)S(1)} custom-call(s32[4]{0:T(128)S(1)} %pad_add_fusion.place, f32[256,8192]{1,0:T(8,128)S(1)} %bitcast.91, f32[256,8192]{1,0:T(8,128)S(1)} %bitcast.91, s16[8,528,128]{2,1,0:T(8,128)(2,1)S(1)} %bitcast_dynamic-update-slice_fusion.8.rest_2_), custom_call_target="tpu_custom_call" | custom-call | flops 1073741824 | bytes 4194304 | tf_op jit(solution)/shard_map/pallas_call | solution.py:98
  119.5 3.7 %shard_map.116 = (f32[256,128]{1,0:T(8,128)}, f32[128,256]{1,0:T(8,128)S(1)}) custom-call(s32[4]{0:T(128)S(1)} %pad_add_fusion.place, f32[256,8192]{1,0:T(8,128)S(1)} %bitcast.91, f32[256,8192]{1,0:T(8,128)S(1)} %bitcast.91, s16[8,528,128]{2,1,0:T(8,128)(2,1)S(1)} %collective-permute-done.32.rest_2_, f32[256,128]{1,0:T(8,128)S(1)} %shard_map.115.rest_3_), custom_call_target="tpu_custom_call" | custom-call | flops 1073741824 | bytes 4194304 | tf_op jit(solution)/shard_map/pallas_call | solution.py:98
  123.3 3.0 %shard_map.117 = s16[8,144,512]{2,1,0:T(8,128)(2,1)S(1)} custom-call(s32[4]{0:T(128)S(1)} %pad_add_fusion.place, f32[256,8192]{1,0:T(8,128)S(1)} %bitcast.91, f32[256,8192]{1,0:T(8,128)S(1)} %bitcast.91, f32[128,256]{1,0:T(8,128)S(1)} %get-tuple-element.65.rest_2_), custom_call_target="tpu_custom_call" | custom-call | flops 1073741824 | bytes 4194304 | tf_op jit(solution)/shard_map/pallas_call | solution.py:98
  126.4 2.8 %collective-permute-done.33.rest_3_ = s16[8,144,512]{2,1,0:T(8,128)(2,1)S(1)} collective-permute-done((s16[8,144,512]{2,1,0:T(8,128)(2,1)S(1)}, s16[8,144,512]{2,1,0:T(8,128)(2,1)S(1)}, u32[]{:S(2)}, u32[]{:S(2)}) %collective-permute-start.33) | collective-permute-done | bytes 1179680 | tf_op jit(solution)/shard_map/ppermute | solution.py:24
  131.2 2.9 %collective-permute-start.35 = (s16[144,512]{1,0:T(8,128)(2,1)S(1)}, s16[144,512]{1,0:T(8,128)(2,1)S(1)}, u32[]{:S(2)}, u32[]{:S(2)}) collective-permute-start(s16[144,512]{1,0:T(8,128)(2,1)S(1)} %get-tuple-element.68), channel_id=1, source_target_pairs={{0,12},{1,13},{2,14},{3,15},{4,8},{5,9},{6,10},{7,11},{8,4},{9,5},... | collective-permute-start | bytes 442376 | tf_op jit(solution)/shard_map/ppermute | solution.py:24
  142.3 2.6 %collective-permute-done.36.rest_2_ = s16[144,512]{1,0:T(8,128)(2,1)S(1)} collective-permute-done((s16[144,512]{1,0:T(8,128)(2,1)S(1)}, s16[144,512]{1,0:T(8,128)(2,1)S(1)}, u32[]{:S(2)}, u32[]{:S(2)}) %collective-permute-start.36) | collective-permute-done | bytes 147488 | tf_op jit(solution)/shard_map/ppermute | solution.py:24
  144.8 2.6 %collective-permute-done.37.rest_3_ = s16[144,512]{1,0:T(8,128)(2,1)S(1)} collective-permute-done((s16[144,512]{1,0:T(8,128)(2,1)S(1)}, s16[144,512]{1,0:T(8,128)(2,1)S(1)}, u32[]{:S(2)}, u32[]{:S(2)}) %collective-permute-start.37) | collective-permute-done | bytes 147488 | tf_op jit(solution)/shard_map/ppermute | solution.py:24
  150.7 9.5 %collective-permute-done.41.rest_0_ = s16[144,512]{1,0:T(8,128)(2,1)S(1)} collective-permute-done((s16[144,512]{1,0:T(8,128)(2,1)S(1)}, s16[144,512]{1,0:T(8,128)(2,1)S(1)}, u32[]{:S(2)}, u32[]{:S(2)}) %collective-permute-start.41) | collective-permute-done | bytes 147488 | tf_op jit(solution)/shard_map/ppermute | solution.py:24
  160.9 3.3 %collective-permute-start.43 = (s16[144,512]{1,0:T(8,128)(2,1)S(1)}, s16[144,512]{1,0:T(8,128)(2,1)S(1)}, u32[]{:S(2)}, u32[]{:S(2)}) collective-permute-start(s16[144,512]{1,0:T(8,128)(2,1)S(1)} %shard_map.121), channel_id=1, source_target_pairs={{0,12},{1,13},{2,14},{3,15},{4,8},{5,9},{6,10},{7,11},{8,4},{9,5},... | collective-permute-start | bytes 442376 | tf_op jit(solution)/shard_map/ppermute | solution.py:24
  168.1 3.9 %collective-permute-done.43 = s16[144,512]{1,0:T(8,128)(2,1)S(1)} collective-permute-done((s16[144,512]{1,0:T(8,128)(2,1)S(1)}, s16[144,512]{1,0:T(8,128)(2,1)S(1)}, u32[]{:S(2)}, u32[]{:S(2)}) %collective-permute-start.43) | collective-permute-done | bytes 147488 | tf_op jit(solution)/shard_map/ppermute | solution.py:24
  172.1 4.7 %collective-permute-done.45 = s16[144,512]{1,0:T(8,128)(2,1)S(1)} collective-permute-done((s16[144,512]{1,0:T(8,128)(2,1)S(1)}, s16[144,512]{1,0:T(8,128)(2,1)S(1)}, u32[]{:S(2)}, u32[]{:S(2)}) %collective-permute-start.45) | collective-permute-done | bytes 147488 | tf_op jit(solution)/shard_map/ppermute | solution.py:24
  179.9 3.7 %shard_map.122 = (f32[128,512]{1,0:T(8,128)S(1)}, bf16[8,128,512]{2,1,0:T(8,128)(2,1)S(1)}) custom-call(s32[4]{0:T(128)S(1)} %pad_add_fusion.place, f32[16,512,512]{2,1,0:T(8,128)S(1)} %bitcast.80, f32[16,512,512]{2,1,0:T(8,128)S(1)} %bitcast.81, s16[8,144,512]{2,1,0:T(8,128)(2,1)S(1)} %bitcast_dynamic-update-slice_fusion.rest_2_.mine, ...), custom_call_target="tpu_custom_call" | custom-call | flops 2147483648 | bytes 8388608 | tf_op jit(solution)/shard_map/pallas_call | solution.py:98
  183.6 3.4 %shard_map.123 = (f32[128,512]{1,0:T(8,128)S(1)}, bf16[8,128,512]{2,1,0:T(8,128)(2,1)S(1)}) custom-call(s32[4]{0:T(128)S(1)} %pad_add_fusion.place, f32[16,512,512]{2,1,0:T(8,128)S(1)} %bitcast.82, f32[16,512,512]{2,1,0:T(8,128)S(1)} %bitcast.83, s16[8,144,512]{2,1,0:T(8,128)(2,1)S(1)} %collective-permute-done.49.rest_2_.other, ...), custom_call_target="tpu_custom_call" | custom-call | flops 2147483648 | bytes 8388608 | tf_op jit(solution)/shard_map/pallas_call | solution.py:98
  187.0 3.7 %shard_map.124 = s16[8,144,512]{2,1,0:T(8,128)(2,1)S(1)} custom-call(s32[4]{0:T(128)S(1)} %pad_add_fusion.place, f32[512,8192]{1,0:T(8,128)S(1)} %bitcast.89, f32[512,8192]{1,0:T(8,128)S(1)} %bitcast.89, f32[128,512]{1,0:T(8,128)S(1)} %get-tuple-element.76.rest_2_), custom_call_target="tpu_custom_call" | custom-call | flops 2147483648 | bytes 8388608 | tf_op jit(solution)/shard_map/pallas_call | solution.py:98
  190.8 2.8 %collective-permute-done.50.rest_3_ = s16[8,144,512]{2,1,0:T(8,128)(2,1)S(1)} collective-permute-done((s16[8,144,512]{2,1,0:T(8,128)(2,1)S(1)}, s16[8,144,512]{2,1,0:T(8,128)(2,1)S(1)}, u32[]{:S(2)}, u32[]{:S(2)}) %collective-permute-start.50) | collective-permute-done | bytes 1179680 | tf_op jit(solution)/shard_map/ppermute | solution.py:24
  193.6 2.6 %shard_map.126 = (s16[144,512]{1,0:T(8,128)(2,1)S(1)}, s16[144,512]{1,0:T(8,128)(2,1)S(1)}, s16[144,512]{1,0:T(8,128)(2,1)S(1)}, s16[144,512]{1,0:T(8,128)(2,1)S(1)}) custom-call(s32[4]{0:T(128)S(1)} %pad_add_fusion.place, f32[512,8192]{1,0:T(8,128)S(1)} %bitcast.89, f32[512,8192]{1,0:T(8,128)S(1)} %bitcast.89, f32[128,512]{1,0:T(8,128)S(1)} %get-tuple-element.76.rest_2_, ...), custom_call_target="tpu_custom_call" | custom-call | flops 1073741824 | bytes 4194304 | tf_op jit(solution)/shard_map/pallas_call | solution.py:98
  196.3 2.9 %collective-permute-start.52 = (s16[144,512]{1,0:T(8,128)(2,1)S(1)}, s16[144,512]{1,0:T(8,128)(2,1)S(1)}, u32[]{:S(2)}, u32[]{:S(2)}) collective-permute-start(s16[144,512]{1,0:T(8,128)(2,1)S(1)} %get-tuple-element.79), channel_id=1, source_target_pairs={{0,12},{1,13},{2,14},{3,15},{4,8},{5,9},{6,10},{7,11},{8,4},{9,5},... | collective-permute-start | bytes 442376 | tf_op jit(solution)/shard_map/ppermute | solution.py:24
  201.1 2.2 shard_map.125
  203.2 2.8 %collective-permute-start.55 = (s16[144,512]{1,0:T(8,128)(2,1)S(1)}, s16[144,512]{1,0:T(8,128)(2,1)S(1)}, u32[]{:S(2)}, u32[]{:S(2)}) collective-permute-start(s16[144,512]{1,0:T(8,128)(2,1)S(1)} %get-tuple-element.82), channel_id=1, source_target_pairs={{0,6},{1,7},{2,4},{3,5},{4,2},{5,3},{6,0},{7,1},{8,14},{9,15},{10,... | collective-permute-start | bytes 442376 | tf_op jit(solution)/shard_map/ppermute | solution.py:24
  208.1 4.9 %shard_map.127.rest_7_.rest_6_ = f32[128,384]{1,0:T(8,128)S(1)} custom-call(s32[4]{0:T(128)S(1)} %pad_add_fusion.place, bf16[2,16,512,384]{3,2,1,0:T(8,128)(2,1)} %bitcast.101, bf16[2,16,512,384]{3,2,1,0:T(8,128)(2,1)} %bitcast.102, bf16[2,16,512,384]{3,2,1,0:T(8,128)(2,1)} %bitcast.103, bf16[2,16,512,384]{3,2,1,0:T(8,128)(2,1)} %bitcast.104, ...), custom_call_target="tpu_custom_call" | custom-call | flops 805306368 | bytes 6291456 | tf_op jit(solution)/shard_map/pallas_call | solution.py:98
  213.1 2.3 collective-permute-done.57.rest_6_
  217.3 3.3 %collective-permute-start.59 = (bf16[128,512]{1,0:T(8,128)(2,1)S(1)}, bf16[128,512]{1,0:T(8,128)(2,1)S(1)}, u32[]{:S(2)}, u32[]{:S(2)}) collective-permute-start(bf16[128,512]{1,0:T(8,128)(2,1)S(1)} %shard_map.129), channel_id=1, source_target_pairs={{0,12},{1,13},{2,14},{3,15},{4,8},{5,9},{6,10},{7,11},{8,4},{9,5},... | collective-permute-start | bytes 393224 | tf_op jit(solution)/shard_map/ppermute | solution.py:24
  222.2 2.4 collective-permute-start.63
  229.5 3.5 %collective-permute-done.63 = bf16[128,512]{1,0:T(8,128)(2,1)S(1)} collective-permute-done((bf16[128,512]{1,0:T(8,128)(2,1)S(1)}, bf16[128,512]{1,0:T(8,128)(2,1)S(1)}, u32[]{:S(2)}, u32[]{:S(2)}) %collective-permute-start.63) | collective-permute-done | bytes 131104 | tf_op jit(solution)/shard_map/ppermute | solution.py:24
  235.4 3.0 %shard_map.130.rest_6_ = f32[128,384]{1,0:T(8,128)S(1)} custom-call(s32[4]{0:T(128)S(1)} %pad_add_fusion.place, bf16[2,16,512,384]{3,2,1,0:T(8,128)(2,1)} %bitcast.105, bf16[2,16,512,384]{3,2,1,0:T(8,128)(2,1)} %bitcast.106, bf16[2,16,512,384]{3,2,1,0:T(8,128)(2,1)} %bitcast.107, bf16[2,16,512,384]{3,2,1,0:T(8,128)(2,1)} %bitcast.108, ...), custom_call_target="tpu_custom_call" | custom-call | flops 402653184 | bytes 3145728 | tf_op jit(solution)/shard_map/pallas_call | solution.py:98
  238.3 4.6 %shard_map.131 = f32[384,128]{1,0:T(8,128)} custom-call(s32[4]{0:T(128)S(1)} %pad_add_fusion.place, bf16[2,16,512,384]{3,2,1,0:T(8,128)(2,1)} %bitcast.109, bf16[2,16,512,384]{3,2,1,0:T(8,128)(2,1)} %bitcast.110, bf16[2,16,512,384]{3,2,1,0:T(8,128)(2,1)} %bitcast.111, bf16[2,16,512,384]{3,2,1,0:T(8,128)(2,1)} %bitcast.112, ...), custom_call_target="tpu_custom_call" | custom-call | flops 402653184 | bytes 3145728 | tf_op jit(solution)/shard_map/pallas_call | solution.py:98
  (187 shorter events, 77.8 us)
Async XLA Ops:
  13.1 7.0 %collective-permute-start.1 = (s16[528,128]{1,0:T(8,128)(2,1)S(1)}, s16[528,128]{1,0:T(8,128)(2,1)S(1)}, u32[]{:S(2)}, u32[]{:S(2)}) collective-permute-start(s16[528,128]{1,0:T(8,128)(2,1)S(1)} %get-tuple-element.49), channel_id=1, source_target_pairs={{0,14},{1,15},{2,12},{3,13},{4,10},{5,11},{6,8},{7,9},{8,6},{9,7},... | collective-permute-start | bytes 405512 | tf_op jit(solution)/shard_map/ppermute | solution.py:24
  15.3 8.5 %collective-permute-start.2 = (s16[528,128]{1,0:T(8,128)(2,1)S(1)}, s16[528,128]{1,0:T(8,128)(2,1)S(1)}, u32[]{:S(2)}, u32[]{:S(2)}) collective-permute-start(s16[528,128]{1,0:T(8,128)(2,1)S(1)} %get-tuple-element.50), channel_id=1, source_target_pairs={{0,12},{1,13},{2,14},{3,15},{4,8},{5,9},{6,10},{7,11},{8,4},{9,5},... | collective-permute-start | bytes 405512 | tf_op jit(solution)/shard_map/ppermute | solution.py:24
  16.5 13.2 %collective-permute-start.3 = (s16[528,128]{1,0:T(8,128)(2,1)S(1)}, s16[528,128]{1,0:T(8,128)(2,1)S(1)}, u32[]{:S(2)}, u32[]{:S(2)}) collective-permute-start(s16[528,128]{1,0:T(8,128)(2,1)S(1)} %get-tuple-element.51), channel_id=1, source_target_pairs={{0,10},{1,11},{2,8},{3,9},{4,14},{5,15},{6,12},{7,13},{8,2},{9,3},... | collective-permute-start | bytes 405512 | tf_op jit(solution)/shard_map/ppermute | solution.py:24
  16.6 13.1 %collective-permute-start.4 = (s16[528,128]{1,0:T(8,128)(2,1)S(1)}, s16[528,128]{1,0:T(8,128)(2,1)S(1)}, u32[]{:S(2)}, u32[]{:S(2)}) collective-permute-start(s16[528,128]{1,0:T(8,128)(2,1)S(1)} %get-tuple-element.52), channel_id=1, source_target_pairs={{0,8},{1,9},{2,10},{3,11},{4,12},{5,13},{6,14},{7,15},{8,0},{9,1},... | collective-permute-start | bytes 405512 | tf_op jit(solution)/shard_map/ppermute | solution.py:24
  17.9 11.8 %collective-permute-start.5 = (s16[528,128]{1,0:T(8,128)(2,1)S(1)}, s16[528,128]{1,0:T(8,128)(2,1)S(1)}, u32[]{:S(2)}, u32[]{:S(2)}) collective-permute-start(s16[528,128]{1,0:T(8,128)(2,1)S(1)} %get-tuple-element.53), channel_id=1, source_target_pairs={{0,6},{1,7},{2,4},{3,5},{4,2},{5,3},{6,0},{7,1},{8,14},{9,15},{10,... | collective-permute-start | bytes 405512 | tf_op jit(solution)/shard_map/ppermute | solution.py:24
  20.1 9.6 %collective-permute-start.6 = (s16[528,128]{1,0:T(8,128)(2,1)S(1)}, s16[528,128]{1,0:T(8,128)(2,1)S(1)}, u32[]{:S(2)}, u32[]{:S(2)}) collective-permute-start(s16[528,128]{1,0:T(8,128)(2,1)S(1)} %get-tuple-element.54), channel_id=1, source_target_pairs={{0,4},{1,5},{2,6},{3,7},{4,0},{5,1},{6,2},{7,3},{8,12},{9,13},{10,... | collective-permute-start | bytes 405512 | tf_op jit(solution)/shard_map/ppermute | solution.py:24
  34.0 7.7 %collective-permute-start.10 = (s16[528,128]{1,0:T(8,128)(2,1)S(1)}, s16[528,128]{1,0:T(8,128)(2,1)S(1)}, u32[]{:S(2)}, u32[]{:S(2)}) collective-permute-start(s16[528,128]{1,0:T(8,128)(2,1)S(1)} %shard_map.107), channel_id=1, source_target_pairs={{0,10},{1,11},{2,8},{3,9},{4,14},{5,15},{6,12},{7,13},{8,2},{9,3},... | collective-permute-start | bytes 405512 | tf_op jit(solution)/shard_map/ppermute | solution.py:24
  34.7 9.5 %collective-permute-start.11 = (s16[528,128]{1,0:T(8,128)(2,1)S(1)}, s16[528,128]{1,0:T(8,128)(2,1)S(1)}, u32[]{:S(2)}, u32[]{:S(2)}) collective-permute-start(s16[528,128]{1,0:T(8,128)(2,1)S(1)} %shard_map.107), channel_id=1, source_target_pairs={{0,8},{1,9},{2,10},{3,11},{4,12},{5,13},{6,14},{7,15},{8,0},{9,1},... | collective-permute-start | bytes 405512 | tf_op jit(solution)/shard_map/ppermute | solution.py:24
  35.6 8.6 %collective-permute-start.12 = (s16[528,128]{1,0:T(8,128)(2,1)S(1)}, s16[528,128]{1,0:T(8,128)(2,1)S(1)}, u32[]{:S(2)}, u32[]{:S(2)}) collective-permute-start(s16[528,128]{1,0:T(8,128)(2,1)S(1)} %shard_map.107), channel_id=1, source_target_pairs={{0,6},{1,7},{2,4},{3,5},{4,2},{5,3},{6,0},{7,1},{8,14},{9,15},{10,... | collective-permute-start | bytes 405512 | tf_op jit(solution)/shard_map/ppermute | solution.py:24
  37.3 9.0 %collective-permute-start.13 = (s16[528,128]{1,0:T(8,128)(2,1)S(1)}, s16[528,128]{1,0:T(8,128)(2,1)S(1)}, u32[]{:S(2)}, u32[]{:S(2)}) collective-permute-start(s16[528,128]{1,0:T(8,128)(2,1)S(1)} %shard_map.107), channel_id=1, source_target_pairs={{0,4},{1,5},{2,6},{3,7},{4,0},{5,1},{6,2},{7,3},{8,12},{9,13},{10,... | collective-permute-start | bytes 405512 | tf_op jit(solution)/shard_map/ppermute | solution.py:24
  38.2 9.0 %collective-permute-start.14 = (s16[528,128]{1,0:T(8,128)(2,1)S(1)}, s16[528,128]{1,0:T(8,128)(2,1)S(1)}, u32[]{:S(2)}, u32[]{:S(2)}) collective-permute-start(s16[528,128]{1,0:T(8,128)(2,1)S(1)} %shard_map.107), channel_id=1, source_target_pairs={{0,2},{1,3},{2,0},{3,1},{4,6},{5,7},{6,4},{7,5},{8,10},{9,11},{10,... | collective-permute-start | bytes 405512 | tf_op jit(solution)/shard_map/ppermute | solution.py:24
  70.2 10.5 %collective-permute-start.17 = (s16[528,128]{1,0:T(8,128)(2,1)S(1)}, s16[528,128]{1,0:T(8,128)(2,1)S(1)}, u32[]{:S(2)}, u32[]{:S(2)}) collective-permute-start(s16[528,128]{1,0:T(8,128)(2,1)S(1)} %get-tuple-element.58), channel_id=1, source_target_pairs={{0,14},{1,15},{2,12},{3,13},{4,10},{5,11},{6,8},{7,9},{8,6},{9,7},... | collective-permute-start | bytes 405512 | tf_op jit(solution)/shard_map/ppermute | solution.py:24
  71.8 9.2 %collective-permute-start.18 = (s16[528,128]{1,0:T(8,128)(2,1)S(1)}, s16[528,128]{1,0:T(8,128)(2,1)S(1)}, u32[]{:S(2)}, u32[]{:S(2)}) collective-permute-start(s16[528,128]{1,0:T(8,128)(2,1)S(1)} %get-tuple-element.59), channel_id=1, source_target_pairs={{0,12},{1,13},{2,14},{3,15},{4,8},{5,9},{6,10},{7,11},{8,4},{9,5},... | collective-permute-start | bytes 405512 | tf_op jit(solution)/shard_map/ppermute | solution.py:24
  73.0 10.2 %collective-permute-start.19 = (s16[528,128]{1,0:T(8,128)(2,1)S(1)}, s16[528,128]{1,0:T(8,128)(2,1)S(1)}, u32[]{:S(2)}, u32[]{:S(2)}) collective-permute-start(s16[528,128]{1,0:T(8,128)(2,1)S(1)} %get-tuple-element.60), channel_id=1, source_target_pairs={{0,10},{1,11},{2,8},{3,9},{4,14},{5,15},{6,12},{7,13},{8,2},{9,3},... | collective-permute-start | bytes 405512 | tf_op jit(solution)/shard_map/ppermute | solution.py:24
  73.6 12.1 %collective-permute-start.20 = (s16[528,128]{1,0:T(8,128)(2,1)S(1)}, s16[528,128]{1,0:T(8,128)(2,1)S(1)}, u32[]{:S(2)}, u32[]{:S(2)}) collective-permute-start(s16[528,128]{1,0:T(8,128)(2,1)S(1)} %get-tuple-element.61), channel_id=1, source_target_pairs={{0,8},{1,9},{2,10},{3,11},{4,12},{5,13},{6,14},{7,15},{8,0},{9,1},... | collective-permute-start | bytes 405512 | tf_op jit(solution)/shard_map/ppermute | solution.py:24
  78.9 7.1 %collective-permute-start.21 = (s16[528,128]{1,0:T(8,128)(2,1)S(1)}, s16[528,128]{1,0:T(8,128)(2,1)S(1)}, u32[]{:S(2)}, u32[]{:S(2)}) collective-permute-start(s16[528,128]{1,0:T(8,128)(2,1)S(1)} %get-tuple-element.62), channel_id=1, source_target_pairs={{0,6},{1,7},{2,4},{3,5},{4,2},{5,3},{6,0},{7,1},{8,14},{9,15},{10,... | collective-permute-start | bytes 405512 | tf_op jit(solution)/shard_map/ppermute | solution.py:24
  80.7 7.5 %collective-permute-start.22 = (s16[528,128]{1,0:T(8,128)(2,1)S(1)}, s16[528,128]{1,0:T(8,128)(2,1)S(1)}, u32[]{:S(2)}, u32[]{:S(2)}) collective-permute-start(s16[528,128]{1,0:T(8,128)(2,1)S(1)} %get-tuple-element.63), channel_id=1, source_target_pairs={{0,4},{1,5},{2,6},{3,7},{4,0},{5,1},{6,2},{7,3},{8,12},{9,13},{10,... | collective-permute-start | bytes 405512 | tf_op jit(solution)/shard_map/ppermute | solution.py:24
  80.9 8.3 %collective-permute-start.23 = (s16[528,128]{1,0:T(8,128)(2,1)S(1)}, s16[528,128]{1,0:T(8,128)(2,1)S(1)}, u32[]{:S(2)}, u32[]{:S(2)}) collective-permute-start(s16[528,128]{1,0:T(8,128)(2,1)S(1)} %get-tuple-element.64), channel_id=1, source_target_pairs={{0,2},{1,3},{2,0},{3,1},{4,6},{5,7},{6,4},{7,5},{8,10},{9,11},{10,... | collective-permute-start | bytes 405512 | tf_op jit(solution)/shard_map/ppermute | solution.py:24
  90.2 8.4 %collective-permute-start.24 = (s16[528,128]{1,0:T(8,128)(2,1)S(1)}, s16[528,128]{1,0:T(8,128)(2,1)S(1)}, u32[]{:S(2)}, u32[]{:S(2)}) collective-permute-start(s16[528,128]{1,0:T(8,128)(2,1)S(1)} %shard_map.113.own), channel_id=1, source_target_pairs={{0,16},{1,17},{2,18},{3,19},{4,20},{5,21},{6,22},{7,23},{8,24},{9,... | collective-permute-start | bytes 405512 | tf_op jit(solution)/shard_map/ppermute | solution.py:24
  99.4 8.7 %collective-permute-start.26 = (s16[528,128]{1,0:T(8,128)(2,1)S(1)}, s16[528,128]{1,0:T(8,128)(2,1)S(1)}, u32[]{:S(2)}, u32[]{:S(2)}) collective-permute-start(s16[528,128]{1,0:T(8,128)(2,1)S(1)} %shard_map.114), channel_id=1, source_target_pairs={{0,12},{1,13},{2,14},{3,15},{4,8},{5,9},{6,10},{7,11},{8,4},{9,5},... | collective-permute-start | bytes 405512 | tf_op jit(solution)/shard_map/ppermute | solution.py:24
  102.2 8.9 %collective-permute-start.27 = (s16[528,128]{1,0:T(8,128)(2,1)S(1)}, s16[528,128]{1,0:T(8,128)(2,1)S(1)}, u32[]{:S(2)}, u32[]{:S(2)}) collective-permute-start(s16[528,128]{1,0:T(8,128)(2,1)S(1)} %shard_map.114), channel_id=1, source_target_pairs={{0,10},{1,11},{2,8},{3,9},{4,14},{5,15},{6,12},{7,13},{8,2},{9,3},... | collective-permute-start | bytes 405512 | tf_op jit(solution)/shard_map/ppermute | solution.py:24
  102.2 10.1 %collective-permute-start.28 = (s16[528,128]{1,0:T(8,128)(2,1)S(1)}, s16[528,128]{1,0:T(8,128)(2,1)S(1)}, u32[]{:S(2)}, u32[]{:S(2)}) collective-permute-start(s16[528,128]{1,0:T(8,128)(2,1)S(1)} %shard_map.114), channel_id=1, source_target_pairs={{0,8},{1,9},{2,10},{3,11},{4,12},{5,13},{6,14},{7,15},{8,0},{9,1},... | collective-permute-start | bytes 405512 | tf_op jit(solution)/shard_map/ppermute | solution.py:24
  104.1 8.3 %collective-permute-start.29 = (s16[528,128]{1,0:T(8,128)(2,1)S(1)}, s16[528,128]{1,0:T(8,128)(2,1)S(1)}, u32[]{:S(2)}, u32[]{:S(2)}) collective-permute-start(s16[528,128]{1,0:T(8,128)(2,1)S(1)} %shard_map.114), channel_id=1, source_target_pairs={{0,6},{1,7},{2,4},{3,5},{4,2},{5,3},{6,0},{7,1},{8,14},{9,15},{10,... | collective-permute-start | bytes 405512 | tf_op jit(solution)/shard_map/ppermute | solution.py:24
  105.4 9.4 %collective-permute-start.30 = (s16[528,128]{1,0:T(8,128)(2,1)S(1)}, s16[528,128]{1,0:T(8,128)(2,1)S(1)}, u32[]{:S(2)}, u32[]{:S(2)}) collective-permute-start(s16[528,128]{1,0:T(8,128)(2,1)S(1)} %shard_map.114), channel_id=1, source_target_pairs={{0,4},{1,5},{2,6},{3,7},{4,0},{5,1},{6,2},{7,3},{8,12},{9,13},{10,... | collective-permute-start | bytes 405512 | tf_op jit(solution)/shard_map/ppermute | solution.py:24
  131.1 8.2 %collective-permute-start.34 = (s16[144,512]{1,0:T(8,128)(2,1)S(1)}, s16[144,512]{1,0:T(8,128)(2,1)S(1)}, u32[]{:S(2)}, u32[]{:S(2)}) collective-permute-start(s16[144,512]{1,0:T(8,128)(2,1)S(1)} %get-tuple-element.67), channel_id=1, source_target_pairs={{0,14},{1,15},{2,12},{3,13},{4,10},{5,11},{6,8},{7,9},{8,6},{9,7},... | collective-permute-start | bytes 442376 | tf_op jit(solution)/shard_map/ppermute | solution.py:24
  131.2 10.2 %collective-permute-start.35 = (s16[144,512]{1,0:T(8,128)(2,1)S(1)}, s16[144,512]{1,0:T(8,128)(2,1)S(1)}, u32[]{:S(2)}, u32[]{:S(2)}) collective-permute-start(s16[144,512]{1,0:T(8,128)(2,1)S(1)} %get-tuple-element.68), channel_id=1, source_target_pairs={{0,12},{1,13},{2,14},{3,15},{4,8},{5,9},{6,10},{7,11},{8,4},{9,5},... | collective-permute-start | bytes 442376 | tf_op jit(solution)/shard_map/ppermute | solution.py:24
  134.1 10.7 %collective-permute-start.36 = (s16[144,512]{1,0:T(8,128)(2,1)S(1)}, s16[144,512]{1,0:T(8,128)(2,1)S(1)}, u32[]{:S(2)}, u32[]{:S(2)}) collective-permute-start(s16[144,512]{1,0:T(8,128)(2,1)S(1)} %get-tuple-element.69), channel_id=1, source_target_pairs={{0,10},{1,11},{2,8},{3,9},{4,14},{5,15},{6,12},{7,13},{8,2},{9,3},... | collective-permute-start | bytes 442376 | tf_op jit(solution)/shard_map/ppermute | solution.py:24
  134.1 13.3 %collective-permute-start.37 = (s16[144,512]{1,0:T(8,128)(2,1)S(1)}, s16[144,512]{1,0:T(8,128)(2,1)S(1)}, u32[]{:S(2)}, u32[]{:S(2)}) collective-permute-start(s16[144,512]{1,0:T(8,128)(2,1)S(1)} %get-tuple-element.70), channel_id=1, source_target_pairs={{0,8},{1,9},{2,10},{3,11},{4,12},{5,13},{6,14},{7,15},{8,0},{9,1},... | collective-permute-start | bytes 442376 | tf_op jit(solution)/shard_map/ppermute | solution.py:24
  137.6 9.8 %collective-permute-start.38 = (s16[144,512]{1,0:T(8,128)(2,1)S(1)}, s16[144,512]{1,0:T(8,128)(2,1)S(1)}, u32[]{:S(2)}, u32[]{:S(2)}) collective-permute-start(s16[144,512]{1,0:T(8,128)(2,1)S(1)} %get-tuple-element.71), channel_id=1, source_target_pairs={{0,6},{1,7},{2,4},{3,5},{4,2},{5,3},{6,0},{7,1},{8,14},{9,15},{10,... | collective-permute-start | bytes 442376 | tf_op jit(solution)/shard_map/ppermute | solution.py:24
  139.3 8.1 %collective-permute-start.39 = (s16[144,512]{1,0:T(8,128)(2,1)S(1)}, s16[144,512]{1,0:T(8,128)(2,1)S(1)}, u32[]{:S(2)}, u32[]{:S(2)}) collective-permute-start(s16[144,512]{1,0:T(8,128)(2,1)S(1)} %get-tuple-element.72), channel_id=1, source_target_pairs={{0,4},{1,5},{2,6},{3,7},{4,0},{5,1},{6,2},{7,3},{8,12},{9,13},{10,... | collective-permute-start | bytes 442376 | tf_op jit(solution)/shard_map/ppermute | solution.py:24
  141.4 8.1 %collective-permute-start.40 = (s16[144,512]{1,0:T(8,128)(2,1)S(1)}, s16[144,512]{1,0:T(8,128)(2,1)S(1)}, u32[]{:S(2)}, u32[]{:S(2)}) collective-permute-start(s16[144,512]{1,0:T(8,128)(2,1)S(1)} %get-tuple-element.73), channel_id=1, source_target_pairs={{0,2},{1,3},{2,0},{3,1},{4,6},{5,7},{6,4},{7,5},{8,10},{9,11},{10,... | collective-permute-start | bytes 442376 | tf_op jit(solution)/shard_map/ppermute | solution.py:24
  150.6 9.6 %collective-permute-start.41 = (s16[144,512]{1,0:T(8,128)(2,1)S(1)}, s16[144,512]{1,0:T(8,128)(2,1)S(1)}, u32[]{:S(2)}, u32[]{:S(2)}) collective-permute-start(s16[144,512]{1,0:T(8,128)(2,1)S(1)} %shard_map.120.own), channel_id=1, source_target_pairs={{0,16},{1,17},{2,18},{3,19},{4,20},{5,21},{6,22},{7,23},{8,24},{9,... | collective-permute-start | bytes 442376 | tf_op jit(solution)/shard_map/ppermute | solution.py:24
  160.9 11.1 %collective-permute-start.43 = (s16[144,512]{1,0:T(8,128)(2,1)S(1)}, s16[144,512]{1,0:T(8,128)(2,1)S(1)}, u32[]{:S(2)}, u32[]{:S(2)}) collective-permute-start(s16[144,512]{1,0:T(8,128)(2,1)S(1)} %shard_map.121), channel_id=1, source_target_pairs={{0,12},{1,13},{2,14},{3,15},{4,8},{5,9},{6,10},{7,11},{8,4},{9,5},... | collective-permute-start | bytes 442376 | tf_op jit(solution)/shard_map/ppermute | solution.py:24
  164.2 7.9 %collective-permute-start.44 = (s16[144,512]{1,0:T(8,128)(2,1)S(1)}, s16[144,512]{1,0:T(8,128)(2,1)S(1)}, u32[]{:S(2)}, u32[]{:S(2)}) collective-permute-start(s16[144,512]{1,0:T(8,128)(2,1)S(1)} %shard_map.121), channel_id=1, source_target_pairs={{0,10},{1,11},{2,8},{3,9},{4,14},{5,15},{6,12},{7,13},{8,2},{9,3},... | collective-permute-start | bytes 442376 | tf_op jit(solution)/shard_map/ppermute | solution.py:24
  164.2 12.6 %collective-permute-start.45 = (s16[144,512]{1,0:T(8,128)(2,1)S(1)}, s16[144,512]{1,0:T(8,128)(2,1)S(1)}, u32[]{:S(2)}, u32[]{:S(2)}) collective-permute-start(s16[144,512]{1,0:T(8,128)(2,1)S(1)} %shard_map.121), channel_id=1, source_target_pairs={{0,8},{1,9},{2,10},{3,11},{4,12},{5,13},{6,14},{7,15},{8,0},{9,1},... | collective-permute-start | bytes 442376 | tf_op jit(solution)/shard_map/ppermute | solution.py:24
  165.6 11.2 %collective-permute-start.46 = (s16[144,512]{1,0:T(8,128)(2,1)S(1)}, s16[144,512]{1,0:T(8,128)(2,1)S(1)}, u32[]{:S(2)}, u32[]{:S(2)}) collective-permute-start(s16[144,512]{1,0:T(8,128)(2,1)S(1)} %shard_map.121), channel_id=1, source_target_pairs={{0,6},{1,7},{2,4},{3,5},{4,2},{5,3},{6,0},{7,1},{8,14},{9,15},{10,... | collective-permute-start | bytes 442376 | tf_op jit(solution)/shard_map/ppermute | solution.py:24
  167.3 10.9 %collective-permute-start.47 = (s16[144,512]{1,0:T(8,128)(2,1)S(1)}, s16[144,512]{1,0:T(8,128)(2,1)S(1)}, u32[]{:S(2)}, u32[]{:S(2)}) collective-permute-start(s16[144,512]{1,0:T(8,128)(2,1)S(1)} %shard_map.121), channel_id=1, source_target_pairs={{0,4},{1,5},{2,6},{3,7},{4,0},{5,1},{6,2},{7,3},{8,12},{9,13},{10,... | collective-permute-start | bytes 442376 | tf_op jit(solution)/shard_map/ppermute | solution.py:24
  196.3 9.8 %collective-permute-start.51 = (s16[144,512]{1,0:T(8,128)(2,1)S(1)}, s16[144,512]{1,0:T(8,128)(2,1)S(1)}, u32[]{:S(2)}, u32[]{:S(2)}) collective-permute-start(s16[144,512]{1,0:T(8,128)(2,1)S(1)} %get-tuple-element.78), channel_id=1, source_target_pairs={{0,14},{1,15},{2,12},{3,13},{4,10},{5,11},{6,8},{7,9},{8,6},{9,7},... | collective-permute-start | bytes 442376 | tf_op jit(solution)/shard_map/ppermute | solution.py:24
  196.3 10.2 %collective-permute-start.52 = (s16[144,512]{1,0:T(8,128)(2,1)S(1)}, s16[144,512]{1,0:T(8,128)(2,1)S(1)}, u32[]{:S(2)}, u32[]{:S(2)}) collective-permute-start(s16[144,512]{1,0:T(8,128)(2,1)S(1)} %get-tuple-element.79), channel_id=1, source_target_pairs={{0,12},{1,13},{2,14},{3,15},{4,8},{5,9},{6,10},{7,11},{8,4},{9,5},... | collective-permute-start | bytes 442376 | tf_op jit(solution)/shard_map/ppermute | solution.py:24
  199.2 13.7 %collective-permute-start.53 = (s16[144,512]{1,0:T(8,128)(2,1)S(1)}, s16[144,512]{1,0:T(8,128)(2,1)S(1)}, u32[]{:S(2)}, u32[]{:S(2)}) collective-permute-start(s16[144,512]{1,0:T(8,128)(2,1)S(1)} %get-tuple-element.80), channel_id=1, source_target_pairs={{0,10},{1,11},{2,8},{3,9},{4,14},{5,15},{6,12},{7,13},{8,2},{9,3},... | collective-permute-start | bytes 442376 | tf_op jit(solution)/shard_map/ppermute | solution.py:24
  199.8 13.3 %collective-permute-start.54 = (s16[144,512]{1,0:T(8,128)(2,1)S(1)}, s16[144,512]{1,0:T(8,128)(2,1)S(1)}, u32[]{:S(2)}, u32[]{:S(2)}) collective-permute-start(s16[144,512]{1,0:T(8,128)(2,1)S(1)} %get-tuple-element.81), channel_id=1, source_target_pairs={{0,8},{1,9},{2,10},{3,11},{4,12},{5,13},{6,14},{7,15},{8,0},{9,1},... | collective-permute-start | bytes 442376 | tf_op jit(solution)/shard_map/ppermute | solution.py:24
  203.2 9.9 %collective-permute-start.55 = (s16[144,512]{1,0:T(8,128)(2,1)S(1)}, s16[144,512]{1,0:T(8,128)(2,1)S(1)}, u32[]{:S(2)}, u32[]{:S(2)}) collective-permute-start(s16[144,512]{1,0:T(8,128)(2,1)S(1)} %get-tuple-element.82), channel_id=1, source_target_pairs={{0,6},{1,7},{2,4},{3,5},{4,2},{5,3},{6,0},{7,1},{8,14},{9,15},{10,... | collective-permute-start | bytes 442376 | tf_op jit(solution)/shard_map/ppermute | solution.py:24
  206.1 7.0 %collective-permute-start.56 = (s16[144,512]{1,0:T(8,128)(2,1)S(1)}, s16[144,512]{1,0:T(8,128)(2,1)S(1)}, u32[]{:S(2)}, u32[]{:S(2)}) collective-permute-start(s16[144,512]{1,0:T(8,128)(2,1)S(1)} %get-tuple-element.83), channel_id=1, source_target_pairs={{0,4},{1,5},{2,6},{3,7},{4,0},{5,1},{6,2},{7,3},{8,12},{9,13},{10,... | collective-permute-start | bytes 442376 | tf_op jit(solution)/shard_map/ppermute | solution.py:24
  206.5 8.9 %collective-permute-start.57 = (s16[144,512]{1,0:T(8,128)(2,1)S(1)}, s16[144,512]{1,0:T(8,128)(2,1)S(1)}, u32[]{:S(2)}, u32[]{:S(2)}) collective-permute-start(s16[144,512]{1,0:T(8,128)(2,1)S(1)} %get-tuple-element.84), channel_id=1, source_target_pairs={{0,2},{1,3},{2,0},{3,1},{4,6},{5,7},{6,4},{7,5},{8,10},{9,11},{10,... | collective-permute-start | bytes 442376 | tf_op jit(solution)/shard_map/ppermute | solution.py:24
  217.3 9.2 %collective-permute-start.59 = (bf16[128,512]{1,0:T(8,128)(2,1)S(1)}, bf16[128,512]{1,0:T(8,128)(2,1)S(1)}, u32[]{:S(2)}, u32[]{:S(2)}) collective-permute-start(bf16[128,512]{1,0:T(8,128)(2,1)S(1)} %shard_map.129), channel_id=1, source_target_pairs={{0,12},{1,13},{2,14},{3,15},{4,8},{5,9},{6,10},{7,11},{8,4},{9,5},... | collective-permute-start | bytes 393224 | tf_op jit(solution)/shard_map/ppermute | solution.py:24
  220.6 8.8 %collective-permute-start.61 = (bf16[128,512]{1,0:T(8,128)(2,1)S(1)}, bf16[128,512]{1,0:T(8,128)(2,1)S(1)}, u32[]{:S(2)}, u32[]{:S(2)}) collective-permute-start(bf16[128,512]{1,0:T(8,128)(2,1)S(1)} %shard_map.129), channel_id=1, source_target_pairs={{0,8},{1,9},{2,10},{3,11},{4,12},{5,13},{6,14},{7,15},{8,0},{9,1},... | collective-permute-start | bytes 393224 | tf_op jit(solution)/shard_map/ppermute | solution.py:24
  221.1 8.4 %collective-permute-start.62 = (bf16[128,512]{1,0:T(8,128)(2,1)S(1)}, bf16[128,512]{1,0:T(8,128)(2,1)S(1)}, u32[]{:S(2)}, u32[]{:S(2)}) collective-permute-start(bf16[128,512]{1,0:T(8,128)(2,1)S(1)} %shard_map.129), channel_id=1, source_target_pairs={{0,6},{1,7},{2,4},{3,5},{4,2},{5,3},{6,0},{7,1},{8,14},{9,15},{10,... | collective-permute-start | bytes 393224 | tf_op jit(solution)/shard_map/ppermute | solution.py:24
  222.2 10.8 %collective-permute-start.63 = (bf16[128,512]{1,0:T(8,128)(2,1)S(1)}, bf16[128,512]{1,0:T(8,128)(2,1)S(1)}, u32[]{:S(2)}, u32[]{:S(2)}) collective-permute-start(bf16[128,512]{1,0:T(8,128)(2,1)S(1)} %shard_map.129), channel_id=1, source_target_pairs={{0,4},{1,5},{2,6},{3,7},{4,0},{5,1},{6,2},{7,3},{8,12},{9,13},{10,... | collective-permute-start | bytes 393224 | tf_op jit(solution)/shard_map/ppermute | solution.py:24
  (36 other events, 412.1 us)

commit v3 on v2

--- a/solution.py
+++ b/solution.py
@@ -16,7 +16,7 @@
 GROUP = 2 * NEAR
 BATCHES = ((4, 4), (0, 4))
 PAD = 16
-VMEM = 12 << 20
+VMEM = 8 << 20
 
 
 def swap(block, offset):
@@ -110,6 +110,20 @@
     )(place, *args)
 
 
+def held_call(kernel, place, outs, scratch, args, flops, moved, before=()):
+    return pl.pallas_call(
+        kernel,
+        in_specs=[pl.BlockSpec(memory_space=pltpu.SMEM)]
+        + [pl.BlockSpec(memory_space=pltpu.VMEM) for _ in args]
+        + [pl.BlockSpec(memory_space=pl.ANY) for _ in before],
+        out_specs=[pl.BlockSpec(memory_space=pltpu.VMEM) for _ in outs],
+        out_shape=[jax.ShapeDtypeStruct(shape, dtype) for shape, dtype in outs],
+        scratch_shapes=scratch,
+        compiler_params=pltpu.CompilerParams(vmem_limit_bytes=VMEM),
+        cost_estimate=pl.CostEstimate(flops=flops, bytes_accessed=moved, transcendentals=0),
+    )(place, *args, *before)
+
+
 def whole(shape):
     return pl.BlockSpec(shape, lambda *_: (0,) * len(shape))
 
@@ -151,6 +165,14 @@
         return pl.BlockSpec(shape, lambda k, p: index(chunk_at(arrival(k * per + at), p, flip)))
 
     return spec
+
+
+def columns_of(factor, chunk, depth):
+    return factor[:, pl.ds(pl.multiple_of(chunk * depth, depth), depth)]
+
+
+def all_of(conditions):
+    return functools.reduce(jnp.logical_and, conditions)
 
 
 def arrived(at, per, place, flip):
@@ -209,6 +231,52 @@
     return kept
 
 
+def reduced_held(place, kernel, args, shape, scratch, flops, moved):
+    coded = (shape[0] + PAD, shape[1])
+    sent = held_call(
+        functools.partial(kernel, 1, 0, NEAR),
+        place,
+        [((NEAR, *coded), I16)],
+        scratch,
+        args,
+        flops // 2,
+        moved // 2,
+    )
+    received = swap(sent[0], 1)
+    kept = [None] * NEAR
+    for first, count in BATCHES:
+        kept[first : first + count] = held_call(
+            functools.partial(kernel, 0, first, count),
+            place,
+            [(shape, F32) if at == 0 else (coded, I16) for at in range(first, first + count)],
+            scratch,
+            [*args, received],
+            flops * count // GROUP,
+            moved * count // GROUP,
+        )
+    return kept
+
+
+def in_pairs(flip, first, count, values, sent, received, outs):
+    def pair(begin):
+        both = values([begin, begin + 1])
+        for at in range(2):
+            if flip:
+                put(sent.at[begin + at], encode(both[at]))
+            else:
+                value = both[at] + decode(received[begin + at])
+                if begin + at == 0:
+                    outs[0][...] = value
+                else:
+                    put(outs[begin + at - first], encode(value))
+
+    if flip:
+        pl.loop(0, count // 2)(lambda number: pair(2 * number))
+    else:
+        for begin in range(first, first + count, 2):
+            pair(begin)
+
+
 def leaf_low_value(size, chunk, place, block, spread, rounded, rhs):
     value = -dot(masked(block[0, 0], spread, chunk, size), rounded[...])
     return with_rows(value, chunk, place[2], rhs)
@@ -268,18 +336,15 @@
 
 def summed(place, own, received, final, before=()):
     rows, columns = received[0].shape
-    return call(
+    return held_call(
         functools.partial(sum_kernel, final, len(before)),
         place,
-        1,
-        [whole(own.shape)]
-        + [whole(r.shape) for r in received]
-        + [pl.BlockSpec(memory_space=pl.ANY) for _ in before],
-        [out_whole((rows - PAD if final else rows, columns), BF16 if final else I16)],
+        [((rows - PAD if final else rows, columns), BF16 if final else I16)],
         [],
-        [own, *received, *before],
+        [own, *received],
         rows * columns * 8,
         rows * columns * 20,
+        before,
     )[0]
 
 
@@ -293,205 +358,168 @@
     return mine, swap(mine, 1)
 
 
-def factor_kernel(start_at, flip, per, place, *rest):
-    factors, stack, rest = rest[:per], rest[per], rest[per + 1 :]
+def factor_kernel(start_at, flip, place, factor, stack, *rest):
     before, rest = (rest[0], rest[1:]) if flip else (None, rest)
     out, wide, narrow = rest[0], rest[-2], rest[-1]
-    depth = factors[0].shape[1]
+    rows, size = factor.shape
+    depth = size // GROUP
     columns = narrow.shape[1]
-
-    @pl.when(pl.program_id(0) == 0)
-    def _():
-        wide[...] = jnp.zeros_like(wide)
-        narrow[...] = jnp.zeros_like(narrow)
-
     start = place[start_at]
-    rows = factors[0].shape[0]
-    chunks = [arrived(at, per, place, flip) for at in range(per)]
-    below = functools.reduce(
-        jnp.logical_and, [(chunk + 1) * depth <= start + 1 for chunk in chunks]
-    )
-
-    def add(wanted, cut):
-        highs, lows, uppers, lowers = [], [], [], []
-        for at in wanted:
-            block = factors[at][...]
-            high, low = halves(triangular(block, start, chunks[at] * depth) if cut else block)
-            upper, lower = halves(decode(stack[at]))
-            highs, lows = highs + [high], lows + [low]
-            uppers, lowers = uppers + [upper], lowers + [lower]
-        upper = jnp.concatenate(uppers, 0)
-        both = jnp.concatenate([upper, jnp.concatenate(lowers, 0)], 1)
-        wide[...] += dot(jnp.concatenate(highs, 1), both)
-        narrow[...] += dot(jnp.concatenate(lows, 1), upper)
-
-    @pl.when(below)
-    def _():
-        add(range(per), False)
-
-    for at in range(per):
-
-        @pl.when(jnp.logical_not(below) & (chunks[at] * depth < start + rows))
-        def _(at=at):
-            add([at], True)
-
-    @pl.when(pl.program_id(0) == pl.num_programs(0) - 1)
-    def _():
-        value = wide[:, :columns] + wide[:, columns:] + narrow[...]
-        if flip:
-            value = value + before[...]
-            rest[1][...] = value.T
-        out[...] = value
+    wide[...] = jnp.zeros_like(wide)
+    narrow[...] = jnp.zeros_like(narrow)
+
+    @pl.loop(0, NEAR // 2)
+    def _(number):
+        entries = [2 * number, 2 * number + 1]
+        chunks = [chunk_at(arrival(entry), place, flip) for entry in entries]
+        below = all_of([(chunk + 1) * depth <= start + 1 for chunk in chunks])
+
+        def add(wanted, cut):
+            highs, lows, uppers, lowers = [], [], [], []
+            for at in wanted:
+                block = columns_of(factor, chunks[at], depth)
+                high, low = halves(triangular(block, start, chunks[at] * depth) if cut else block)
+                upper, lower = halves(decode(stack[entries[at]]))
+                highs, lows = highs + [high], lows + [low]
+                uppers, lowers = uppers + [upper], lowers + [lower]
+            upper = jnp.concatenate(uppers, 0)
+            both = jnp.concatenate([upper, jnp.concatenate(lowers, 0)], 1)
+            wide[...] += dot(jnp.concatenate(highs, 1), both)
+            narrow[...] += dot(jnp.concatenate(lows, 1), upper)
+
+        @pl.when(below)
+        def _():
+            add(range(2), False)
+
+        for at in range(2):
+
+            @pl.when(jnp.logical_not(below) & (chunks[at] * depth < start + rows))
+            def _(at=at):
+                add([at], True)
+
+    value = wide[:, :columns] + wide[:, columns:] + narrow[...]
+    if flip:
+        value = value + before[...]
+        rest[1][...] = value.T
+    out[...] = value
 
 
 def factor_apply(place, factor, stacks, start_at):
     count, size = factor.shape
-    depth = size // GROUP
     columns = stacks[0].shape[2]
-    per = 2
-    block = over_arrived((count, depth), lambda chunk: (0, chunk))
     result = ()
     for flip in range(2):
-        result = call(
-            functools.partial(factor_kernel, start_at, flip, per),
+        result = held_call(
+            functools.partial(factor_kernel, start_at, flip),
             place,
-            NEAR // per,
-            [block(at, per, flip) for at in range(per)]
-            + [in_steps(per, stacks[flip].shape[1:])]
-            + [whole(r.shape) for r in result],
-            [out_whole((count, columns), F32)] + [out_whole((columns, count), F32)] * flip,
+            [((count, columns), F32)] + [((columns, count), F32)] * flip,
             [pltpu.VMEM((count, 2 * columns), F32), pltpu.VMEM((count, columns), F32)],
-            [factor] * per + [stacks[flip], *result],
+            [factor, stacks[flip], *result],
             4 * count * size * columns,
             2 * count * size,
         )
     return result
 
 
-def coupled_kernel(flip, first, per, place, *rest):
-    couplings, parts, rest = rest[:per], rest[per : 2 * per], rest[2 * per :]
-    rows, rhs, packed = rest[0], rest[1], rest[-1]
+def coupled_kernel(flip, first, count, place, coupling, part, rows, rhs, *rest):
+    packed = rest[-1]
     columns = rows.shape[1]
-
-    @pl.when(pl.program_id(0) == 0)
-    def _():
-        high, low = halves(rows[...])
-        packed[:, :columns] = high
-        packed[:, columns:] = low
-
-    values = []
-    for at in range(per):
-        chunk = chunk_at(steps_of(first, at, per), place, flip)
-        high, low = halves(couplings[at][0])
-        product = dot(high, packed[...])
-        value = product[:, :columns] + product[:, columns:] + dot(low, packed[:, :columns])
-        values.append(with_rows(-(parts[at][0] + value), chunk, place[3], rhs))
-    for at in range(per):
-        if flip:
-            put(rest[2].at[at], encode(values[at]))
-        else:
-            emit(first, per, at, rest[3:-1], values[at] + decode(rest[2][at]))
-
-
-def back_kernel(start_at, flip, first, per, place, *rest):
-    factors, vector, rest = rest[:per], rest[per], rest[per + 1 :]
-    packed = rest[-1]
+    high, low = halves(rows[...])
+    packed[:, :columns] = high
+    packed[:, columns:] = low
+
+    def values(steps):
+        result = []
+        for step in steps:
+            chunk = chunk_at(step, place, flip)
+            high, low = halves(coupling[chunk])
+            product = dot(high, packed[...])
+            value = product[:, :columns] + product[:, columns:] + dot(low, packed[:, :columns])
+            result.append(with_rows(-(part[chunk] + value), chunk, place[3], rhs))
+        return result
+
+    in_pairs(flip, first, count, values, rest[0], rest[0], rest[1:-1])
+
+
+def back_kernel(start_at, flip, first, count, place, factor, vector, *rest):
+    packed, total = rest[-2:]
     columns = vector.shape[0]
-
-    @pl.when(pl.program_id(0) == 0)
-    def _():
-        high, low = halves(vector[...])
-        packed[:columns, :] = high
-        packed[columns:, :] = low
-
-    rows, depth = factors[0].shape
+    rows, size = factor.shape
+    depth = size // GROUP
     start = place[start_at]
-    chunks = [chunk_at(steps_of(first, at, per), place, flip) for at in range(per)]
-    below = functools.reduce(
-        jnp.logical_and, [(chunk + 1) * depth <= start + 1 for chunk in chunks]
-    )
-    above = functools.reduce(jnp.logical_and, [chunk * depth >= start + rows for chunk in chunks])
-
-    def finish(values):
-        for at in range(per):
-            if flip:
-                put(rest[0].at[at], encode(values[at]))
-            else:
-                emit(first, per, at, rest[1:-1], values[at] + decode(rest[0][at]))
-
-    def products(cut):
-        values = []
-        for at in range(per):
-            block = factors[at][...]
-            high, low = halves(triangular(block, start, chunks[at] * depth) if cut else block)
-            product = dot(packed[...], high)
-            values.append(
-                product[:columns, :] + product[columns:, :] + dot(packed[:columns, :], low)
-            )
-        return values
-
-    @pl.when(below)
-    def _():
-        finish(products(False))
-
-    @pl.when(above)
-    def _():
-        finish([jnp.zeros((columns, depth), F32)] * per)
-
-    @pl.when(jnp.logical_not(below | above))
-    def _():
-        finish(products(True))
+    high, low = halves(vector[...])
+    packed[:columns, :] = high
+    packed[columns:, :] = low
+
+    def values(steps):
+        chunks = [chunk_at(step, place, flip) for step in steps]
+        below = all_of([(chunk + 1) * depth <= start + 1 for chunk in chunks])
+        above = all_of([chunk * depth >= start + rows for chunk in chunks])
+
+        def products(cut):
+            for at, chunk in enumerate(chunks):
+                block = columns_of(factor, chunk, depth)
+                high, low = halves(triangular(block, start, chunk * depth) if cut else block)
+                product = dot(packed[...], high)
+                total[at] = (
+                    product[:columns, :] + product[columns:, :] + dot(packed[:columns, :], low)
+                )
+
+        @pl.when(below)
+        def _():
+            products(False)
+
+        @pl.when(above)
+        def _():
+            total[...] = jnp.zeros_like(total)
+
+        @pl.when(jnp.logical_not(below | above))
+        def _():
+            products(True)
+
+        return [total[at] for at in range(len(chunks))]
+
+    in_pairs(flip, first, count, values, rest[0], rest[0], rest[1:-2])
 
 
 def back_apply(place, factor, vector, start_at):
     count, size = factor.shape
     columns = vector.shape[0]
     chunk = size // GROUP
-    block = over((count, chunk), lambda c: (0, c))
-    per = 2
-
-    def specs(first, per, flip):
-        return [block(first, at, per, flip) for at in range(per)] + [whole(vector.shape)]
-
-    return reduced(
+    return reduced_held(
         place,
         functools.partial(back_kernel, start_at),
-        specs,
-        [factor] * per + [vector],
+        [factor, vector],
         (columns, chunk),
-        [pltpu.VMEM((2 * columns, count), BF16)],
+        [pltpu.VMEM((2 * columns, count), BF16), pltpu.VMEM((2, columns, chunk), F32)],
         8 * count * size * columns,
         4 * count * size,
-        per,
     )
 
 
-def carry_kernel(flip, per, place, *rest):
-    couplings, (stack, before, gap, rounded, wide, narrow) = rest[:per], rest[per:]
+def carry_kernel(flip, place, coupling, stack, before, gap, rounded, wide, narrow):
     columns = before.shape[0]
-
-    @pl.when(pl.program_id(0) == 0)
-    def _():
-        wide[...] = jnp.zeros_like(wide)
-        narrow[...] = jnp.zeros_like(narrow)
-
-    @pl.when(pl.program_id(0) >= 0)
-    def _():
-        highs, lows, uppers, lowers = [], [], [], []
-        for at in range(per):
-            high, low = halves(couplings[at][0])
-            upper, lower = halves(decode(stack[at]))
-            rounded[at] = upper
-            highs, lows = highs + [high], lows + [low]
-            uppers, lowers = uppers + [upper], lowers + [lower]
-        upper = jnp.concatenate(uppers, 1)
-        both = jnp.concatenate([upper, jnp.concatenate(lowers, 1)], 0)
-        wide[...] += dot(both, jnp.concatenate(highs, 0))
-        narrow[...] += dot(upper, jnp.concatenate(lows, 0))
-
-    @pl.when(pl.program_id(0) == pl.num_programs(0) - 1)
-    def _():
-        gap[...] = before[...] - (wide[:columns, :] + wide[columns:, :] + narrow[...])
+    wide[...] = jnp.zeros_like(wide)
+    narrow[...] = jnp.zeros_like(narrow)
+
+    @pl.loop(0, NEAR // 2)
+    def _(number):
+        @pl.when(number >= 0)
+        def _():
+            highs, lows, uppers, lowers = [], [], [], []
+            for at in range(2):
+                entry = 2 * number + at
+                high, low = halves(coupling[chunk_at(arrival(entry), place, flip)])
+                upper, lower = halves(decode(stack[entry]))
+                rounded[entry] = upper
+                highs, lows = highs + [high], lows + [low]
+                uppers, lowers = uppers + [upper], lowers + [lower]
+            upper = jnp.concatenate(uppers, 1)
+            both = jnp.concatenate([upper, jnp.concatenate(lowers, 1)], 0)
+            wide[...] += dot(both, jnp.concatenate(highs, 0))
+            narrow[...] += dot(upper, jnp.concatenate(lows, 0))
+
+    gap[...] = before[...] - (wide[:columns, :] + wide[columns:, :] + narrow[...])
 
 
 def own_kernel(place, mine, other, out):
@@ -580,7 +608,7 @@
     tiles = at_rest(jnp.transpose(tile_mask, (2, 0, 1)))
     coupling = at_rest(leaf_coupling.reshape(levels, GROUP, chunk, local_rows))
     low_blocks = low_coupling.reshape(GROUP, chunk, low_count)
-    low_rhs, top_rhs = at_rest(low_rhs), at_rest(top_rhs)
+    low_rhs = at_rest(low_rhs)
 
     leaf_flops = 2 * sep_size * local_rows * columns
     leaf_moved = 2 * sep_size * local_rows
@@ -652,28 +680,14 @@
 
     coupled_flops = 8 * sep_size * low_count * columns
     coupled_moved = 4 * sep_size * low_count
-    low_block = over((1, chunk, low_count), lambda c: (c, 0, 0))
-    low_arrived = over_arrived((1, chunk, low_count), lambda c: (c, 0, 0))
-    part_block = over((1, chunk, columns), lambda c: (c, 0, 0))
-    per = 2
-
-    def coupled_specs(first, per, flip):
-        return (
-            [low_block(first, at, per, flip) for at in range(per)]
-            + [part_block(first, at, per, flip) for at in range(per)]
-            + [whole(first_rows.shape), whole(top_rhs.shape)]
-        )
-
-    kept = reduced(
+    kept = reduced_held(
         place,
         coupled_kernel,
-        coupled_specs,
-        [low_blocks] * per + [part] * per + [first_rows, top_rhs],
+        [low_blocks, part, first_rows, top_rhs],
         (chunk, columns),
         [pltpu.VMEM((low_count, 2 * columns), BF16)],
         coupled_flops,
         coupled_moved,
-        per,
     )
     top_input = reduce_and_gather(place, kept, top_far)
     _, forward_columns = factor_apply(place, top_inverse, top_input, 3)
@@ -683,15 +697,12 @@
     turned = (columns, chunk)
     gap, rounded = first_columns, []
     for flip in range(2):
-        gap, near = call(
-            functools.partial(carry_kernel, flip, per),
+        gap, near = held_call(
+            functools.partial(carry_kernel, flip),
             place,
-            NEAR // per,
-            [low_arrived(at, per, flip) for at in range(per)]
-            + [in_steps(per, solution_blocks[flip].shape[1:]), whole(gap.shape)],
-            [out_whole(gap.shape, F32), in_steps(per, turned, BF16, NEAR)],
+            [(gap.shape, F32), ((NEAR, *turned), BF16)],
             [pltpu.VMEM((2 * columns, low_count), F32), pltpu.VMEM((columns, low_count), F32)],
-            [low_blocks] * per + [solution_blocks[flip], gap],
+            [low_blocks, solution_blocks[flip], gap],
             coupled_flops // 2,
             coupled_moved // 2,
         )
@@ -714,6 +725,7 @@
     )[0]
     top_solution = lax.dynamic_slice_in_dim(top_own, top_start % chunk, top_count, 0)
     kept = back_apply(place, low_inverse, gap, 2)
+    per = 2
     back_top = call(
         functools.partial(leaf_back_top_kernel, size, per),
         place,

time: 243 us -> 236 us (0.971)
  Pallas kernels: 80.8 us -> 72.6 us
  waiting for transfers between devices: 84.3 us -> 87.1 us
    pallas_call x28 -> x7, Pallas kernels: 80.8 us -> 27.5 us  [call(): pl.pallas_call(kernel, grid_spec=pltpu.PrefetchScalarGridSpec(num_scalar_...]
    pallas_call x0 -> x21, Pallas kernels: none -> 45.1 us  [held_call(): pl.pallas_call(kernel, in_specs=[pl.BlockSpec(memory_space=pltpu.SMEM)] +...]
    ppermute x66, waiting for transfers between devices: 84.3 us -> 87.1 us  [swap(): return lax.ppermute(block, AXES, [(at, at ^ offset) for at in range(count)])]
  transfers between devices with their start and end apart: 66 -> 66, of which waited for: 36 -> 34; matrix products, arithmetic and copies ran while one was open for 0% -> 0% of each run, Pallas kernels for 13% -> 12%
where the time goes in v3:
time: 236 us
  waiting for transfers between devices  87.1 us (37%)
  starting transfers between devices  72.7 us (31%)
  Pallas kernels  72.6 us (31%)
    ppermute x66, waiting for transfers between devices, swap(): return lax.ppermute(block, AXES, [(at, at ^ offset) for at in range(count)])  87.1 us
    ppermute x66, starting transfers between devices, swap(): return lax.ppermute(block, AXES, [(at, at ^ offset) for at in range(count)])  72.7 us
    pallas_call x21, Pallas kernels, held_call(): pl.pallas_call(kernel, in_specs=[pl.BlockSpec(memory_space=pltpu.SMEM)] +...  45.1 us
    pallas_call x7, Pallas kernels, call(): pl.pallas_call(kernel, grid_spec=pltpu.PrefetchScalarGridSpec(num_scalar_...  27.5 us
  transfers between devices with their start and end apart: 66, of which 34 were waited for; matrix products, arithmetic and copies ran while one was open for 0% of the time, Pallas kernels for 12%

profile of v3, /device:TPU:25, one launch (start us, length us, event | category | flops | bytes accessed | tf_op | source)
XLA Modules:
  0.0 235.7 jit_solution(9897505684536286138)
XLA Ops:
  0.8 4.6 %shard_map.104 = (s16[8,528,128]{2,1,0:T(8,128)(2,1)S(1)}, f32[384,128]{1,0:T(8,128)S(1)}, bf16[384,128]{1,0:T(8,128)(2,1)S(1)}, f32[2,128,384]{2,1,0:T(8,128)S(1)}) custom-call(s32[4]{0:T(128)S(1)} %pad_add_fusion.place, bf16[2,16,512,384]{3,2,1,0:T(8,128)(2,1)} %bitcast.83, bf16[2,16,512,384]{3,2,1,0:T(8,128)(2,1)} %bitcast.84, ...), custom_call_target="tpu_custom_call" | custom-call | flops 402653184 | bytes 3145728 | tf_op jit(solution)/shard_map/pallas_call | solution.py:98
  6.1 2.3 collective-permute-done.rest_7_
  8.4 4.7 %shard_map.106 = (f32[512,128]{1,0:T(8,128)S(1)}, s16[528,128]{1,0:T(8,128)(2,1)S(1)}, s16[528,128]{1,0:T(8,128)(2,1)S(1)}, s16[528,128]{1,0:T(8,128)(2,1)S(1)},...) custom-call(s32[4]{0:T(128)S(1)} %pad_add_fusion.place, ...), custom_call_target="tpu_custom_call" | custom-call | flops 402653184 | bytes 3145728 | tf_op jit(solution)/shard_map/pallas_call | solution.py:98
  17.9 2.2 collective-permute-start.5
  21.1 2.7 %collective-permute-done.2.rest_1_ = s16[528,128]{1,0:T(8,128)(2,1)S(1)} collective-permute-done((s16[528,128]{1,0:T(8,128)(2,1)S(1)}, s16[528,128]{1,0:T(8,128)(2,1)S(1)}, u32[]{:S(2)}, u32[]{:S(2)}) %collective-permute-start.2) | collective-permute-done | bytes 135200 | tf_op jit(solution)/shard_map/ppermute | solution.py:24
  24.4 5.3 %shard_map.105.rest_7_.part = f32[16,512,128]{2,1,0:T(8,128)S(1)} custom-call(s32[4]{0:T(128)S(1)} %pad_add_fusion.place, f32[2,128,384]{2,1,0:T(8,128)S(1)} %get-tuple-element.45.spread.rest_4_, bf16[384,128]{1,0:T(8,128)(2,1)S(1)} %get-tuple-element.46.rounded.rest_5_, bf16[2,16,512,384]{3,2,1,0:T(8,128)(2,1)} %bitcast.91), custom_call_target="tpu_custom_call" | custom-call | flops 805306368 | bytes 6291456 | tf_op jit(solution)/shard_map/pallas_call | solution.py:98
  39.1 2.6 %collective-permute-done.10 = s16[528,128]{1,0:T(8,128)(2,1)S(1)} collective-permute-done((s16[528,128]{1,0:T(8,128)(2,1)S(1)}, s16[528,128]{1,0:T(8,128)(2,1)S(1)}, u32[]{:S(2)}, u32[]{:S(2)}) %collective-permute-start.10) | collective-permute-done | bytes 135200 | tf_op jit(solution)/shard_map/ppermute | solution.py:24
  41.7 2.4 %collective-permute-done.11 = s16[528,128]{1,0:T(8,128)(2,1)S(1)} collective-permute-done((s16[528,128]{1,0:T(8,128)(2,1)S(1)}, s16[528,128]{1,0:T(8,128)(2,1)S(1)}, u32[]{:S(2)}, u32[]{:S(2)}) %collective-permute-start.11) | collective-permute-done | bytes 135200 | tf_op jit(solution)/shard_map/ppermute | solution.py:24
  47.2 2.6 %collective-permute-start.15 = (s16[8,528,128]{2,1,0:T(8,128)(2,1)S(1)}, s16[8,528,128]{2,1,0:T(8,128)(2,1)S(1)}, u32[]{:S(2)}, u32[]{:S(2)}) collective-permute-start(s16[8,528,128]{2,1,0:T(8,128)(2,1)S(1)} %bitcast_dynamic-update-slice_fusion.16.stack), channel_id=1, source_target_pairs={{0,1},{1,0},{2,3},{3,2},{4,5},{5,4},{6,7},{7,6},{8,9},{9,8},{10,11... | collective-permute-start | bytes 3244040 | tf_op jit(solution)/shard_map/ppermute | solution.py:24
  49.8 2.9 %shard_map.108.rest_0_ = f32[512,128]{1,0:T(8,128)S(1)} custom-call(s32[4]{0:T(128)S(1)} %pad_add_fusion.place, f32[512,8192]{1,0:T(8,128)S(1)} %bitcast.80, s16[8,528,128]{2,1,0:T(8,128)(2,1)S(1)} %bitcast_dynamic-update-slice_fusion.16.stack), custom_call_target="tpu_custom_call" | custom-call | flops 2147483648 | bytes 8388608 | tf_op jit(solution)/shard_map/pallas_call | solution.py:114
  52.8 2.8 %shard_map.109 = (f32[512,128]{1,0:T(8,128)S(1)}, f32[128,512]{1,0:T(8,128)S(1)}) custom-call(s32[4]{0:T(128)S(1)} %pad_add_fusion.place, f32[512,8192]{1,0:T(8,128)S(1)} %bitcast.80, s16[8,528,128]{2,1,0:T(8,128)(2,1)S(1)} %collective-permute-done.15.stack, f32[512,128]{1,0:T(8,128)S(1)} %shard_map.108.rest_0_), custom_call_target="tpu_custom_call" | custom-call | flops 2147483648 | bytes 8388608 | tf_op jit(solution)/shard_map/pallas_call | solution.py:114
  56.2 4.2 %shard_map.110 = s16[8,528,128]{2,1,0:T(8,128)(2,1)S(1)} custom-call(s32[4]{0:T(128)S(1)} %pad_add_fusion.place, f32[16,512,512]{2,1,0:T(8,128)S(1)} %bitcast.74, f32[16,512,128]{2,1,0:T(8,128)S(1)} %shard_map.105.rest_7_.part, f32[512,128]{1,0:T(8,128)S(1)} %get-tuple-element.56.rows, f32[256,128]{1,0:T(8,128)S(1)} %copy-done), custom_call_target="tpu_custom_call" | custom-call | flops 2147483648 | bytes 8388608 | tf_op jit(solution)/shard_map/pallas_call | solution.py:114
  60.6 2.7 %collective-permute-done.16.rest_0_ = s16[8,528,128]{2,1,0:T(8,128)(2,1)S(1)} collective-permute-done((s16[8,528,128]{2,1,0:T(8,128)(2,1)S(1)}, s16[8,528,128]{2,1,0:T(8,128)(2,1)S(1)}, u32[]{:S(2)}, u32[]{:S(2)}) %collective-permute-start.16) | collective-permute-done | bytes 1081376 | tf_op jit(solution)/shard_map/ppermute | solution.py:24
  72.3 3.1 %collective-permute-start.21 = (s16[528,128]{1,0:T(8,128)(2,1)S(1)}, s16[528,128]{1,0:T(8,128)(2,1)S(1)}, u32[]{:S(2)}, u32[]{:S(2)}) collective-permute-start(s16[528,128]{1,0:T(8,128)(2,1)S(1)} %get-tuple-element.62), channel_id=1, source_target_pairs={{0,6},{1,7},{2,4},{3,5},{4,2},{5,3},{6,0},{7,1},{8,14},{9,15},{10,... | collective-permute-start | bytes 405512 | tf_op jit(solution)/shard_map/ppermute | solution.py:24
  76.2 3.8 %collective-permute-done.19.rest_2_ = s16[528,128]{1,0:T(8,128)(2,1)S(1)} collective-permute-done((s16[528,128]{1,0:T(8,128)(2,1)S(1)}, s16[528,128]{1,0:T(8,128)(2,1)S(1)}, u32[]{:S(2)}, u32[]{:S(2)}) %collective-permute-start.19) | collective-permute-done | bytes 135200 | tf_op jit(solution)/shard_map/ppermute | solution.py:24
  82.0 2.7 %collective-permute-done.23.rest_6_ = s16[528,128]{1,0:T(8,128)(2,1)S(1)} collective-permute-done((s16[528,128]{1,0:T(8,128)(2,1)S(1)}, s16[528,128]{1,0:T(8,128)(2,1)S(1)}, u32[]{:S(2)}, u32[]{:S(2)}) %collective-permute-start.23) | collective-permute-done | bytes 135200 | tf_op jit(solution)/shard_map/ppermute | solution.py:24
  85.9 8.9 %collective-permute-done.24.rest_0_ = s16[528,128]{1,0:T(8,128)(2,1)S(1)} collective-permute-done((s16[528,128]{1,0:T(8,128)(2,1)S(1)}, s16[528,128]{1,0:T(8,128)(2,1)S(1)}, u32[]{:S(2)}, u32[]{:S(2)}) %collective-permute-start.24) | collective-permute-done | bytes 135200 | tf_op jit(solution)/shard_map/ppermute | solution.py:24
  95.6 2.7 %collective-permute-start.26 = (s16[528,128]{1,0:T(8,128)(2,1)S(1)}, s16[528,128]{1,0:T(8,128)(2,1)S(1)}, u32[]{:S(2)}, u32[]{:S(2)}) collective-permute-start(s16[528,128]{1,0:T(8,128)(2,1)S(1)} %shard_map.114), channel_id=1, source_target_pairs={{0,12},{1,13},{2,14},{3,15},{4,8},{5,9},{6,10},{7,11},{8,4},{9,5},... | collective-permute-start | bytes 405512 | tf_op jit(solution)/shard_map/ppermute | solution.py:24
  102.9 2.5 %collective-permute-done.26 = s16[528,128]{1,0:T(8,128)(2,1)S(1)} collective-permute-done((s16[528,128]{1,0:T(8,128)(2,1)S(1)}, s16[528,128]{1,0:T(8,128)(2,1)S(1)}, u32[]{:S(2)}, u32[]{:S(2)}) %collective-permute-start.26) | collective-permute-done | bytes 135200 | tf_op jit(solution)/shard_map/ppermute | solution.py:24
  107.6 3.3 %collective-permute-done.30 = s16[528,128]{1,0:T(8,128)(2,1)S(1)} collective-permute-done((s16[528,128]{1,0:T(8,128)(2,1)S(1)}, s16[528,128]{1,0:T(8,128)(2,1)S(1)}, u32[]{:S(2)}, u32[]{:S(2)}) %collective-permute-start.30) | collective-permute-done | bytes 135200 | tf_op jit(solution)/shard_map/ppermute | solution.py:24
  113.0 2.2 shard_map.115.rest_0_
  115.3 3.2 %shard_map.116 = (f32[256,128]{1,0:T(8,128)}, f32[128,256]{1,0:T(8,128)S(1)}) custom-call(s32[4]{0:T(128)S(1)} %pad_add_fusion.place, f32[256,8192]{1,0:T(8,128)S(1)} %bitcast.82, s16[8,528,128]{2,1,0:T(8,128)(2,1)S(1)} %collective-permute-done.32.stack, f32[256,128]{1,0:T(8,128)S(1)} %shard_map.115.rest_0_), custom_call_target="tpu_custom_call" | custom-call | flops 1073741824 | bytes 4194304 | tf_op jit(solution)/shard_map/pallas_call | solution.py:114
  118.5 2.9 %shard_map.117 = s16[8,144,512]{2,1,0:T(8,128)(2,1)S(1)} custom-call(s32[4]{0:T(128)S(1)} %pad_add_fusion.place, f32[256,8192]{1,0:T(8,128)S(1)} %bitcast.82, f32[128,256]{1,0:T(8,128)S(1)} %get-tuple-element.65.vector), custom_call_target="tpu_custom_call" | custom-call | flops 1073741824 | bytes 4194304 | tf_op jit(solution)/shard_map/pallas_call | solution.py:114
  121.5 2.8 %collective-permute-done.33.rest_0_ = s16[8,144,512]{2,1,0:T(8,128)(2,1)S(1)} collective-permute-done((s16[8,144,512]{2,1,0:T(8,128)(2,1)S(1)}, s16[8,144,512]{2,1,0:T(8,128)(2,1)S(1)}, u32[]{:S(2)}, u32[]{:S(2)}) %collective-permute-start.33) | collective-permute-done | bytes 1179680 | tf_op jit(solution)/shard_map/ppermute | solution.py:24
  126.2 2.8 %collective-permute-start.35 = (s16[144,512]{1,0:T(8,128)(2,1)S(1)}, s16[144,512]{1,0:T(8,128)(2,1)S(1)}, u32[]{:S(2)}, u32[]{:S(2)}) collective-permute-start(s16[144,512]{1,0:T(8,128)(2,1)S(1)} %get-tuple-element.68), channel_id=1, source_target_pairs={{0,12},{1,13},{2,14},{3,15},{4,8},{5,9},{6,10},{7,11},{8,4},{9,5},... | collective-permute-start | bytes 442376 | tf_op jit(solution)/shard_map/ppermute | solution.py:24
  137.2 2.5 %collective-permute-done.36.rest_2_ = s16[144,512]{1,0:T(8,128)(2,1)S(1)} collective-permute-done((s16[144,512]{1,0:T(8,128)(2,1)S(1)}, s16[144,512]{1,0:T(8,128)(2,1)S(1)}, u32[]{:S(2)}, u32[]{:S(2)}) %collective-permute-start.36) | collective-permute-done | bytes 147488 | tf_op jit(solution)/shard_map/ppermute | solution.py:24
  139.7 2.6 %collective-permute-done.37.rest_3_ = s16[144,512]{1,0:T(8,128)(2,1)S(1)} collective-permute-done((s16[144,512]{1,0:T(8,128)(2,1)S(1)}, s16[144,512]{1,0:T(8,128)(2,1)S(1)}, u32[]{:S(2)}, u32[]{:S(2)}) %collective-permute-start.37) | collective-permute-done | bytes 147488 | tf_op jit(solution)/shard_map/ppermute | solution.py:24
  142.3 2.7 %collective-permute-done.40.rest_6_ = s16[144,512]{1,0:T(8,128)(2,1)S(1)} collective-permute-done((s16[144,512]{1,0:T(8,128)(2,1)S(1)}, s16[144,512]{1,0:T(8,128)(2,1)S(1)}, u32[]{:S(2)}, u32[]{:S(2)}) %collective-permute-start.40) | collective-permute-done | bytes 147488 | tf_op jit(solution)/shard_map/ppermute | solution.py:24
  146.2 9.7 %collective-permute-done.41.rest_0_ = s16[144,512]{1,0:T(8,128)(2,1)S(1)} collective-permute-done((s16[144,512]{1,0:T(8,128)(2,1)S(1)}, s16[144,512]{1,0:T(8,128)(2,1)S(1)}, u32[]{:S(2)}, u32[]{:S(2)}) %collective-permute-start.41) | collective-permute-done | bytes 147488 | tf_op jit(solution)/shard_map/ppermute | solution.py:24
  156.7 2.3 collective-permute-start.43
  159.0 2.4 %collective-permute-start.45 = (s16[144,512]{1,0:T(8,128)(2,1)S(1)}, s16[144,512]{1,0:T(8,128)(2,1)S(1)}, u32[]{:S(2)}, u32[]{:S(2)}) collective-permute-start(s16[144,512]{1,0:T(8,128)(2,1)S(1)} %shard_map.121), channel_id=1, source_target_pairs={{0,8},{1,9},{2,10},{3,11},{4,12},{5,13},{6,14},{7,15},{8,0},{9,1},... | collective-permute-start | bytes 442376 | tf_op jit(solution)/shard_map/ppermute | solution.py:24
  163.6 3.5 %collective-permute-done.43 = s16[144,512]{1,0:T(8,128)(2,1)S(1)} collective-permute-done((s16[144,512]{1,0:T(8,128)(2,1)S(1)}, s16[144,512]{1,0:T(8,128)(2,1)S(1)}, u32[]{:S(2)}, u32[]{:S(2)}) %collective-permute-start.43) | collective-permute-done | bytes 147488 | tf_op jit(solution)/shard_map/ppermute | solution.py:24
  168.1 3.8 %collective-permute-done.45 = s16[144,512]{1,0:T(8,128)(2,1)S(1)} collective-permute-done((s16[144,512]{1,0:T(8,128)(2,1)S(1)}, s16[144,512]{1,0:T(8,128)(2,1)S(1)}, u32[]{:S(2)}, u32[]{:S(2)}) %collective-permute-start.45) | collective-permute-done | bytes 147488 | tf_op jit(solution)/shard_map/ppermute | solution.py:24
  174.9 3.3 %shard_map.122 = (f32[128,512]{1,0:T(8,128)S(1)}, bf16[8,128,512]{2,1,0:T(8,128)(2,1)S(1)}) custom-call(s32[4]{0:T(128)S(1)} %pad_add_fusion.place, f32[16,512,512]{2,1,0:T(8,128)S(1)} %bitcast.77, s16[8,144,512]{2,1,0:T(8,128)(2,1)S(1)} %bitcast_dynamic-update-slice_fusion.stack.mine, f32[128,512]{1,0:T(8,128)S(1)} %get-tuple-element.74.before), custom_call_target="tpu_custom_call" | custom-call | flops 2147483648 | bytes 8388608 | tf_op jit(solution)/shard_map/pallas_call | solution.py:114
  178.2 3.3 %shard_map.123 = (f32[128,512]{1,0:T(8,128)S(1)}, bf16[8,128,512]{2,1,0:T(8,128)(2,1)S(1)}) custom-call(s32[4]{0:T(128)S(1)} %pad_add_fusion.place, f32[16,512,512]{2,1,0:T(8,128)S(1)} %bitcast.78, s16[8,144,512]{2,1,0:T(8,128)(2,1)S(1)} %collective-permute-done.49.stack.other, f32[128,512]{1,0:T(8,128)S(1)} %get-tuple-element.75.before), custom_call_target="tpu_custom_call" | custom-call | flops 2147483648 | bytes 8388608 | tf_op jit(solution)/shard_map/pallas_call | solution.py:114
  181.5 3.2 %shard_map.124 = s16[8,144,512]{2,1,0:T(8,128)(2,1)S(1)} custom-call(s32[4]{0:T(128)S(1)} %pad_add_fusion.place, f32[512,8192]{1,0:T(8,128)S(1)} %bitcast.80, f32[128,512]{1,0:T(8,128)S(1)} %get-tuple-element.76.vector), custom_call_target="tpu_custom_call" | custom-call | flops 2147483648 | bytes 8388608 | tf_op jit(solution)/shard_map/pallas_call | solution.py:114
  184.8 2.8 %collective-permute-done.50.rest_0_ = s16[8,144,512]{2,1,0:T(8,128)(2,1)S(1)} collective-permute-done((s16[8,144,512]{2,1,0:T(8,128)(2,1)S(1)}, s16[8,144,512]{2,1,0:T(8,128)(2,1)S(1)}, u32[]{:S(2)}, u32[]{:S(2)}) %collective-permute-start.50) | collective-permute-done | bytes 1179680 | tf_op jit(solution)/shard_map/ppermute | solution.py:24
  187.6 2.2 shard_map.126
  189.9 3.0 %collective-permute-start.52 = (s16[144,512]{1,0:T(8,128)(2,1)S(1)}, s16[144,512]{1,0:T(8,128)(2,1)S(1)}, u32[]{:S(2)}, u32[]{:S(2)}) collective-permute-start(s16[144,512]{1,0:T(8,128)(2,1)S(1)} %get-tuple-element.79), channel_id=1, source_target_pairs={{0,12},{1,13},{2,14},{3,15},{4,8},{5,9},{6,10},{7,11},{8,4},{9,5},... | collective-permute-start | bytes 442376 | tf_op jit(solution)/shard_map/ppermute | solution.py:24
  196.7 2.2 collective-permute-start.55
  201.7 4.9 %shard_map.127.rest_7_.rest_6_ = f32[128,384]{1,0:T(8,128)S(1)} custom-call(s32[4]{0:T(128)S(1)} %pad_add_fusion.place, bf16[2,16,512,384]{3,2,1,0:T(8,128)(2,1)} %bitcast.92, bf16[2,16,512,384]{3,2,1,0:T(8,128)(2,1)} %bitcast.93, bf16[2,16,512,384]{3,2,1,0:T(8,128)(2,1)} %bitcast.94, bf16[2,16,512,384]{3,2,1,0:T(8,128)(2,1)} %bitcast.95, ...), custom_call_target="tpu_custom_call" | custom-call | flops 805306368 | bytes 6291456 | tf_op jit(solution)/shard_map/pallas_call | solution.py:98
  207.2 3.3 %collective-permute-done.57.rest_6_ = s16[144,512]{1,0:T(8,128)(2,1)S(1)} collective-permute-done((s16[144,512]{1,0:T(8,128)(2,1)S(1)}, s16[144,512]{1,0:T(8,128)(2,1)S(1)}, u32[]{:S(2)}, u32[]{:S(2)}) %collective-permute-start.57) | collective-permute-done | bytes 147488 | tf_op jit(solution)/shard_map/ppermute | solution.py:24
  213.1 3.0 %collective-permute-start.61 = (bf16[128,512]{1,0:T(8,128)(2,1)S(1)}, bf16[128,512]{1,0:T(8,128)(2,1)S(1)}, u32[]{:S(2)}, u32[]{:S(2)}) collective-permute-start(bf16[128,512]{1,0:T(8,128)(2,1)S(1)} %shard_map.129), channel_id=1, source_target_pairs={{0,8},{1,9},{2,10},{3,11},{4,12},{5,13},{6,14},{7,15},{8,0},{9,1},... | collective-permute-start | bytes 393224 | tf_op jit(solution)/shard_map/ppermute | solution.py:24
  218.2 2.5 %collective-permute-start.64 = (bf16[128,512]{1,0:T(8,128)(2,1)S(1)}, bf16[128,512]{1,0:T(8,128)(2,1)S(1)}, u32[]{:S(2)}, u32[]{:S(2)}) collective-permute-start(bf16[128,512]{1,0:T(8,128)(2,1)S(1)} %shard_map.129), channel_id=1, source_target_pairs={{0,2},{1,3},{2,0},{3,1},{4,6},{5,7},{6,4},{7,5},{8,10},{9,11},{10,... | collective-permute-start | bytes 393224 | tf_op jit(solution)/shard_map/ppermute | solution.py:24
  220.7 2.8 %collective-permute-done.61 = bf16[128,512]{1,0:T(8,128)(2,1)S(1)} collective-permute-done((bf16[128,512]{1,0:T(8,128)(2,1)S(1)}, bf16[128,512]{1,0:T(8,128)(2,1)S(1)}, u32[]{:S(2)}, u32[]{:S(2)}) %collective-permute-start.61) | collective-permute-done | bytes 131104 | tf_op jit(solution)/shard_map/ppermute | solution.py:24
  224.8 3.0 %collective-permute-start.65 = (bf16[8,128,512]{2,1,0:T(8,128)(2,1)S(1)}, bf16[8,128,512]{2,1,0:T(8,128)(2,1)S(1)}, u32[]{:S(2)}, u32[]{:S(2)}) collective-permute-start(bf16[8,128,512]{2,1,0:T(8,128)(2,1)S(1)} %bitcast_dynamic-update-slice_fusion.24.rest_5_), channel_id=1, source_target_pairs={{0,1},{1,0},{2,3},{3,2},{4,5},{5,4},{6,7},{7,6},{8,9},{9,8},{10,11... | collective-permute-start | bytes 3145736 | tf_op jit(solution)/shard_map/ppermute | solution.py:24
  228.5 3.0 %shard_map.130.rest_6_ = f32[128,384]{1,0:T(8,128)S(1)} custom-call(s32[4]{0:T(128)S(1)} %pad_add_fusion.place, bf16[2,16,512,384]{3,2,1,0:T(8,128)(2,1)} %bitcast.96, bf16[2,16,512,384]{3,2,1,0:T(8,128)(2,1)} %bitcast.97, bf16[2,16,512,384]{3,2,1,0:T(8,128)(2,1)} %bitcast.98, bf16[2,16,512,384]{3,2,1,0:T(8,128)(2,1)} %bitcast.99, ...), custom_call_target="tpu_custom_call" | custom-call | flops 402653184 | bytes 3145728 | tf_op jit(solution)/shard_map/pallas_call | solution.py:98
  231.4 4.3 %shard_map.131 = f32[384,128]{1,0:T(8,128)} custom-call(s32[4]{0:T(128)S(1)} %pad_add_fusion.place, bf16[2,16,512,384]{3,2,1,0:T(8,128)(2,1)} %bitcast.100, bf16[2,16,512,384]{3,2,1,0:T(8,128)(2,1)} %bitcast.101, bf16[2,16,512,384]{3,2,1,0:T(8,128)(2,1)} %bitcast.102, bf16[2,16,512,384]{3,2,1,0:T(8,128)(2,1)} %bitcast.103, ...), custom_call_target="tpu_custom_call" | custom-call | flops 402653184 | bytes 3145728 | tf_op jit(solution)/shard_map/pallas_call | solution.py:98
  (171 shorter events, 75.2 us)
Async XLA Ops:
  13.1 7.0 %collective-permute-start.1 = (s16[528,128]{1,0:T(8,128)(2,1)S(1)}, s16[528,128]{1,0:T(8,128)(2,1)S(1)}, u32[]{:S(2)}, u32[]{:S(2)}) collective-permute-start(s16[528,128]{1,0:T(8,128)(2,1)S(1)} %get-tuple-element.49), channel_id=1, source_target_pairs={{0,14},{1,15},{2,12},{3,13},{4,10},{5,11},{6,8},{7,9},{8,6},{9,7},... | collective-permute-start | bytes 405512 | tf_op jit(solution)/shard_map/ppermute | solution.py:24
  15.3 8.5 %collective-permute-start.2 = (s16[528,128]{1,0:T(8,128)(2,1)S(1)}, s16[528,128]{1,0:T(8,128)(2,1)S(1)}, u32[]{:S(2)}, u32[]{:S(2)}) collective-permute-start(s16[528,128]{1,0:T(8,128)(2,1)S(1)} %get-tuple-element.50), channel_id=1, source_target_pairs={{0,12},{1,13},{2,14},{3,15},{4,8},{5,9},{6,10},{7,11},{8,4},{9,5},... | collective-permute-start | bytes 405512 | tf_op jit(solution)/shard_map/ppermute | solution.py:24
  16.5 13.2 %collective-permute-start.3 = (s16[528,128]{1,0:T(8,128)(2,1)S(1)}, s16[528,128]{1,0:T(8,128)(2,1)S(1)}, u32[]{:S(2)}, u32[]{:S(2)}) collective-permute-start(s16[528,128]{1,0:T(8,128)(2,1)S(1)} %get-tuple-element.51), channel_id=1, source_target_pairs={{0,10},{1,11},{2,8},{3,9},{4,14},{5,15},{6,12},{7,13},{8,2},{9,3},... | collective-permute-start | bytes 405512 | tf_op jit(solution)/shard_map/ppermute | solution.py:24
  16.6 13.1 %collective-permute-start.4 = (s16[528,128]{1,0:T(8,128)(2,1)S(1)}, s16[528,128]{1,0:T(8,128)(2,1)S(1)}, u32[]{:S(2)}, u32[]{:S(2)}) collective-permute-start(s16[528,128]{1,0:T(8,128)(2,1)S(1)} %get-tuple-element.52), channel_id=1, source_target_pairs={{0,8},{1,9},{2,10},{3,11},{4,12},{5,13},{6,14},{7,15},{8,0},{9,1},... | collective-permute-start | bytes 405512 | tf_op jit(solution)/shard_map/ppermute | solution.py:24
  17.9 11.8 %collective-permute-start.5 = (s16[528,128]{1,0:T(8,128)(2,1)S(1)}, s16[528,128]{1,0:T(8,128)(2,1)S(1)}, u32[]{:S(2)}, u32[]{:S(2)}) collective-permute-start(s16[528,128]{1,0:T(8,128)(2,1)S(1)} %get-tuple-element.53), channel_id=1, source_target_pairs={{0,6},{1,7},{2,4},{3,5},{4,2},{5,3},{6,0},{7,1},{8,14},{9,15},{10,... | collective-permute-start | bytes 405512 | tf_op jit(solution)/shard_map/ppermute | solution.py:24
  20.1 9.6 %collective-permute-start.6 = (s16[528,128]{1,0:T(8,128)(2,1)S(1)}, s16[528,128]{1,0:T(8,128)(2,1)S(1)}, u32[]{:S(2)}, u32[]{:S(2)}) collective-permute-start(s16[528,128]{1,0:T(8,128)(2,1)S(1)} %get-tuple-element.54), channel_id=1, source_target_pairs={{0,4},{1,5},{2,6},{3,7},{4,0},{5,1},{6,2},{7,3},{8,12},{9,13},{10,... | collective-permute-start | bytes 405512 | tf_op jit(solution)/shard_map/ppermute | solution.py:24
  34.0 7.7 %collective-permute-start.10 = (s16[528,128]{1,0:T(8,128)(2,1)S(1)}, s16[528,128]{1,0:T(8,128)(2,1)S(1)}, u32[]{:S(2)}, u32[]{:S(2)}) collective-permute-start(s16[528,128]{1,0:T(8,128)(2,1)S(1)} %shard_map.107), channel_id=1, source_target_pairs={{0,10},{1,11},{2,8},{3,9},{4,14},{5,15},{6,12},{7,13},{8,2},{9,3},... | collective-permute-start | bytes 405512 | tf_op jit(solution)/shard_map/ppermute | solution.py:24
  34.7 9.5 %collective-permute-start.11 = (s16[528,128]{1,0:T(8,128)(2,1)S(1)}, s16[528,128]{1,0:T(8,128)(2,1)S(1)}, u32[]{:S(2)}, u32[]{:S(2)}) collective-permute-start(s16[528,128]{1,0:T(8,128)(2,1)S(1)} %shard_map.107), channel_id=1, source_target_pairs={{0,8},{1,9},{2,10},{3,11},{4,12},{5,13},{6,14},{7,15},{8,0},{9,1},... | collective-permute-start | bytes 405512 | tf_op jit(solution)/shard_map/ppermute | solution.py:24
  35.6 8.6 %collective-permute-start.12 = (s16[528,128]{1,0:T(8,128)(2,1)S(1)}, s16[528,128]{1,0:T(8,128)(2,1)S(1)}, u32[]{:S(2)}, u32[]{:S(2)}) collective-permute-start(s16[528,128]{1,0:T(8,128)(2,1)S(1)} %shard_map.107), channel_id=1, source_target_pairs={{0,6},{1,7},{2,4},{3,5},{4,2},{5,3},{6,0},{7,1},{8,14},{9,15},{10,... | collective-permute-start | bytes 405512 | tf_op jit(solution)/shard_map/ppermute | solution.py:24
  37.3 9.0 %collective-permute-start.13 = (s16[528,128]{1,0:T(8,128)(2,1)S(1)}, s16[528,128]{1,0:T(8,128)(2,1)S(1)}, u32[]{:S(2)}, u32[]{:S(2)}) collective-permute-start(s16[528,128]{1,0:T(8,128)(2,1)S(1)} %shard_map.107), channel_id=1, source_target_pairs={{0,4},{1,5},{2,6},{3,7},{4,0},{5,1},{6,2},{7,3},{8,12},{9,13},{10,... | collective-permute-start | bytes 405512 | tf_op jit(solution)/shard_map/ppermute | solution.py:24
  38.2 9.0 %collective-permute-start.14 = (s16[528,128]{1,0:T(8,128)(2,1)S(1)}, s16[528,128]{1,0:T(8,128)(2,1)S(1)}, u32[]{:S(2)}, u32[]{:S(2)}) collective-permute-start(s16[528,128]{1,0:T(8,128)(2,1)S(1)} %shard_map.107), channel_id=1, source_target_pairs={{0,2},{1,3},{2,0},{3,1},{4,6},{5,7},{6,4},{7,5},{8,10},{9,11},{10,... | collective-permute-start | bytes 405512 | tf_op jit(solution)/shard_map/ppermute | solution.py:24
  65.4 10.0 %collective-permute-start.17 = (s16[528,128]{1,0:T(8,128)(2,1)S(1)}, s16[528,128]{1,0:T(8,128)(2,1)S(1)}, u32[]{:S(2)}, u32[]{:S(2)}) collective-permute-start(s16[528,128]{1,0:T(8,128)(2,1)S(1)} %get-tuple-element.58), channel_id=1, source_target_pairs={{0,14},{1,15},{2,12},{3,13},{4,10},{5,11},{6,8},{7,9},{8,6},{9,7},... | collective-permute-start | bytes 405512 | tf_op jit(solution)/shard_map/ppermute | solution.py:24
  66.7 8.7 %collective-permute-start.18 = (s16[528,128]{1,0:T(8,128)(2,1)S(1)}, s16[528,128]{1,0:T(8,128)(2,1)S(1)}, u32[]{:S(2)}, u32[]{:S(2)}) collective-permute-start(s16[528,128]{1,0:T(8,128)(2,1)S(1)} %get-tuple-element.59), channel_id=1, source_target_pairs={{0,12},{1,13},{2,14},{3,15},{4,8},{5,9},{6,10},{7,11},{8,4},{9,5},... | collective-permute-start | bytes 405512 | tf_op jit(solution)/shard_map/ppermute | solution.py:24
  68.6 11.4 %collective-permute-start.19 = (s16[528,128]{1,0:T(8,128)(2,1)S(1)}, s16[528,128]{1,0:T(8,128)(2,1)S(1)}, u32[]{:S(2)}, u32[]{:S(2)}) collective-permute-start(s16[528,128]{1,0:T(8,128)(2,1)S(1)} %get-tuple-element.60), channel_id=1, source_target_pairs={{0,10},{1,11},{2,8},{3,9},{4,14},{5,15},{6,12},{7,13},{8,2},{9,3},... | collective-permute-start | bytes 405512 | tf_op jit(solution)/shard_map/ppermute | solution.py:24
  69.8 12.2 %collective-permute-start.20 = (s16[528,128]{1,0:T(8,128)(2,1)S(1)}, s16[528,128]{1,0:T(8,128)(2,1)S(1)}, u32[]{:S(2)}, u32[]{:S(2)}) collective-permute-start(s16[528,128]{1,0:T(8,128)(2,1)S(1)} %get-tuple-element.61), channel_id=1, source_target_pairs={{0,8},{1,9},{2,10},{3,11},{4,12},{5,13},{6,14},{7,15},{8,0},{9,1},... | collective-permute-start | bytes 405512 | tf_op jit(solution)/shard_map/ppermute | solution.py:24
  72.3 9.8 %collective-permute-start.21 = (s16[528,128]{1,0:T(8,128)(2,1)S(1)}, s16[528,128]{1,0:T(8,128)(2,1)S(1)}, u32[]{:S(2)}, u32[]{:S(2)}) collective-permute-start(s16[528,128]{1,0:T(8,128)(2,1)S(1)} %get-tuple-element.62), channel_id=1, source_target_pairs={{0,6},{1,7},{2,4},{3,5},{4,2},{5,3},{6,0},{7,1},{8,14},{9,15},{10,... | collective-permute-start | bytes 405512 | tf_op jit(solution)/shard_map/ppermute | solution.py:24
  75.4 9.3 %collective-permute-start.23 = (s16[528,128]{1,0:T(8,128)(2,1)S(1)}, s16[528,128]{1,0:T(8,128)(2,1)S(1)}, u32[]{:S(2)}, u32[]{:S(2)}) collective-permute-start(s16[528,128]{1,0:T(8,128)(2,1)S(1)} %get-tuple-element.64), channel_id=1, source_target_pairs={{0,2},{1,3},{2,0},{3,1},{4,6},{5,7},{6,4},{7,5},{8,10},{9,11},{10,... | collective-permute-start | bytes 405512 | tf_op jit(solution)/shard_map/ppermute | solution.py:24
  85.8 9.0 %collective-permute-start.24 = (s16[528,128]{1,0:T(8,128)(2,1)S(1)}, s16[528,128]{1,0:T(8,128)(2,1)S(1)}, u32[]{:S(2)}, u32[]{:S(2)}) collective-permute-start(s16[528,128]{1,0:T(8,128)(2,1)S(1)} %shard_map.113.own), channel_id=1, source_target_pairs={{0,16},{1,17},{2,18},{3,19},{4,20},{5,21},{6,22},{7,23},{8,24},{9,... | collective-permute-start | bytes 405512 | tf_op jit(solution)/shard_map/ppermute | solution.py:24
  95.6 9.8 %collective-permute-start.26 = (s16[528,128]{1,0:T(8,128)(2,1)S(1)}, s16[528,128]{1,0:T(8,128)(2,1)S(1)}, u32[]{:S(2)}, u32[]{:S(2)}) collective-permute-start(s16[528,128]{1,0:T(8,128)(2,1)S(1)} %shard_map.114), channel_id=1, source_target_pairs={{0,12},{1,13},{2,14},{3,15},{4,8},{5,9},{6,10},{7,11},{8,4},{9,5},... | collective-permute-start | bytes 405512 | tf_op jit(solution)/shard_map/ppermute | solution.py:24
  98.3 8.5 %collective-permute-start.27 = (s16[528,128]{1,0:T(8,128)(2,1)S(1)}, s16[528,128]{1,0:T(8,128)(2,1)S(1)}, u32[]{:S(2)}, u32[]{:S(2)}) collective-permute-start(s16[528,128]{1,0:T(8,128)(2,1)S(1)} %shard_map.114), channel_id=1, source_target_pairs={{0,10},{1,11},{2,8},{3,9},{4,14},{5,15},{6,12},{7,13},{8,2},{9,3},... | collective-permute-start | bytes 405512 | tf_op jit(solution)/shard_map/ppermute | solution.py:24
  98.3 9.3 %collective-permute-start.28 = (s16[528,128]{1,0:T(8,128)(2,1)S(1)}, s16[528,128]{1,0:T(8,128)(2,1)S(1)}, u32[]{:S(2)}, u32[]{:S(2)}) collective-permute-start(s16[528,128]{1,0:T(8,128)(2,1)S(1)} %shard_map.114), channel_id=1, source_target_pairs={{0,8},{1,9},{2,10},{3,11},{4,12},{5,13},{6,14},{7,15},{8,0},{9,1},... | collective-permute-start | bytes 405512 | tf_op jit(solution)/shard_map/ppermute | solution.py:24
  100.3 7.3 %collective-permute-start.29 = (s16[528,128]{1,0:T(8,128)(2,1)S(1)}, s16[528,128]{1,0:T(8,128)(2,1)S(1)}, u32[]{:S(2)}, u32[]{:S(2)}) collective-permute-start(s16[528,128]{1,0:T(8,128)(2,1)S(1)} %shard_map.114), channel_id=1, source_target_pairs={{0,6},{1,7},{2,4},{3,5},{4,2},{5,3},{6,0},{7,1},{8,14},{9,15},{10,... | collective-permute-start | bytes 405512 | tf_op jit(solution)/shard_map/ppermute | solution.py:24
  102.0 8.9 %collective-permute-start.30 = (s16[528,128]{1,0:T(8,128)(2,1)S(1)}, s16[528,128]{1,0:T(8,128)(2,1)S(1)}, u32[]{:S(2)}, u32[]{:S(2)}) collective-permute-start(s16[528,128]{1,0:T(8,128)(2,1)S(1)} %shard_map.114), channel_id=1, source_target_pairs={{0,4},{1,5},{2,6},{3,7},{4,0},{5,1},{6,2},{7,3},{8,12},{9,13},{10,... | collective-permute-start | bytes 405512 | tf_op jit(solution)/shard_map/ppermute | solution.py:24
  126.2 8.2 %collective-permute-start.34 = (s16[144,512]{1,0:T(8,128)(2,1)S(1)}, s16[144,512]{1,0:T(8,128)(2,1)S(1)}, u32[]{:S(2)}, u32[]{:S(2)}) collective-permute-start(s16[144,512]{1,0:T(8,128)(2,1)S(1)} %get-tuple-element.67), channel_id=1, source_target_pairs={{0,14},{1,15},{2,12},{3,13},{4,10},{5,11},{6,8},{7,9},{8,6},{9,7},... | collective-permute-start | bytes 442376 | tf_op jit(solution)/shard_map/ppermute | solution.py:24
  126.2 10.0 %collective-permute-start.35 = (s16[144,512]{1,0:T(8,128)(2,1)S(1)}, s16[144,512]{1,0:T(8,128)(2,1)S(1)}, u32[]{:S(2)}, u32[]{:S(2)}) collective-permute-start(s16[144,512]{1,0:T(8,128)(2,1)S(1)} %get-tuple-element.68), channel_id=1, source_target_pairs={{0,12},{1,13},{2,14},{3,15},{4,8},{5,9},{6,10},{7,11},{8,4},{9,5},... | collective-permute-start | bytes 442376 | tf_op jit(solution)/shard_map/ppermute | solution.py:24
  129.1 10.6 %collective-permute-start.36 = (s16[144,512]{1,0:T(8,128)(2,1)S(1)}, s16[144,512]{1,0:T(8,128)(2,1)S(1)}, u32[]{:S(2)}, u32[]{:S(2)}) collective-permute-start(s16[144,512]{1,0:T(8,128)(2,1)S(1)} %get-tuple-element.69), channel_id=1, source_target_pairs={{0,10},{1,11},{2,8},{3,9},{4,14},{5,15},{6,12},{7,13},{8,2},{9,3},... | collective-permute-start | bytes 442376 | tf_op jit(solution)/shard_map/ppermute | solution.py:24
  129.2 13.1 %collective-permute-start.37 = (s16[144,512]{1,0:T(8,128)(2,1)S(1)}, s16[144,512]{1,0:T(8,128)(2,1)S(1)}, u32[]{:S(2)}, u32[]{:S(2)}) collective-permute-start(s16[144,512]{1,0:T(8,128)(2,1)S(1)} %get-tuple-element.70), channel_id=1, source_target_pairs={{0,8},{1,9},{2,10},{3,11},{4,12},{5,13},{6,14},{7,15},{8,0},{9,1},... | collective-permute-start | bytes 442376 | tf_op jit(solution)/shard_map/ppermute | solution.py:24
  132.6 9.7 %collective-permute-start.38 = (s16[144,512]{1,0:T(8,128)(2,1)S(1)}, s16[144,512]{1,0:T(8,128)(2,1)S(1)}, u32[]{:S(2)}, u32[]{:S(2)}) collective-permute-start(s16[144,512]{1,0:T(8,128)(2,1)S(1)} %get-tuple-element.71), channel_id=1, source_target_pairs={{0,6},{1,7},{2,4},{3,5},{4,2},{5,3},{6,0},{7,1},{8,14},{9,15},{10,... | collective-permute-start | bytes 442376 | tf_op jit(solution)/shard_map/ppermute | solution.py:24
  134.4 8.0 %collective-permute-start.39 = (s16[144,512]{1,0:T(8,128)(2,1)S(1)}, s16[144,512]{1,0:T(8,128)(2,1)S(1)}, u32[]{:S(2)}, u32[]{:S(2)}) collective-permute-start(s16[144,512]{1,0:T(8,128)(2,1)S(1)} %get-tuple-element.72), channel_id=1, source_target_pairs={{0,4},{1,5},{2,6},{3,7},{4,0},{5,1},{6,2},{7,3},{8,12},{9,13},{10,... | collective-permute-start | bytes 442376 | tf_op jit(solution)/shard_map/ppermute | solution.py:24
  136.2 8.9 %collective-permute-start.40 = (s16[144,512]{1,0:T(8,128)(2,1)S(1)}, s16[144,512]{1,0:T(8,128)(2,1)S(1)}, u32[]{:S(2)}, u32[]{:S(2)}) collective-permute-start(s16[144,512]{1,0:T(8,128)(2,1)S(1)} %get-tuple-element.73), channel_id=1, source_target_pairs={{0,2},{1,3},{2,0},{3,1},{4,6},{5,7},{6,4},{7,5},{8,10},{9,11},{10,... | collective-permute-start | bytes 442376 | tf_op jit(solution)/shard_map/ppermute | solution.py:24
  146.1 9.8 %collective-permute-start.41 = (s16[144,512]{1,0:T(8,128)(2,1)S(1)}, s16[144,512]{1,0:T(8,128)(2,1)S(1)}, u32[]{:S(2)}, u32[]{:S(2)}) collective-permute-start(s16[144,512]{1,0:T(8,128)(2,1)S(1)} %shard_map.120.own), channel_id=1, source_target_pairs={{0,16},{1,17},{2,18},{3,19},{4,20},{5,21},{6,22},{7,23},{8,24},{9,... | collective-permute-start | bytes 442376 | tf_op jit(solution)/shard_map/ppermute | solution.py:24
  156.6 6.9 %collective-permute-start.42 = (s16[144,512]{1,0:T(8,128)(2,1)S(1)}, s16[144,512]{1,0:T(8,128)(2,1)S(1)}, u32[]{:S(2)}, u32[]{:S(2)}) collective-permute-start(s16[144,512]{1,0:T(8,128)(2,1)S(1)} %shard_map.121), channel_id=1, source_target_pairs={{0,14},{1,15},{2,12},{3,13},{4,10},{5,11},{6,8},{7,9},{8,6},{9,7},... | collective-permute-start | bytes 442376 | tf_op jit(solution)/shard_map/ppermute | solution.py:24
  156.7 10.3 %collective-permute-start.43 = (s16[144,512]{1,0:T(8,128)(2,1)S(1)}, s16[144,512]{1,0:T(8,128)(2,1)S(1)}, u32[]{:S(2)}, u32[]{:S(2)}) collective-permute-start(s16[144,512]{1,0:T(8,128)(2,1)S(1)} %shard_map.121), channel_id=1, source_target_pairs={{0,12},{1,13},{2,14},{3,15},{4,8},{5,9},{6,10},{7,11},{8,4},{9,5},... | collective-permute-start | bytes 442376 | tf_op jit(solution)/shard_map/ppermute | solution.py:24
  159.0 9.0 %collective-permute-start.44 = (s16[144,512]{1,0:T(8,128)(2,1)S(1)}, s16[144,512]{1,0:T(8,128)(2,1)S(1)}, u32[]{:S(2)}, u32[]{:S(2)}) collective-permute-start(s16[144,512]{1,0:T(8,128)(2,1)S(1)} %shard_map.121), channel_id=1, source_target_pairs={{0,10},{1,11},{2,8},{3,9},{4,14},{5,15},{6,12},{7,13},{8,2},{9,3},... | collective-permute-start | bytes 442376 | tf_op jit(solution)/shard_map/ppermute | solution.py:24
  159.0 12.9 %collective-permute-start.45 = (s16[144,512]{1,0:T(8,128)(2,1)S(1)}, s16[144,512]{1,0:T(8,128)(2,1)S(1)}, u32[]{:S(2)}, u32[]{:S(2)}) collective-permute-start(s16[144,512]{1,0:T(8,128)(2,1)S(1)} %shard_map.121), channel_id=1, source_target_pairs={{0,8},{1,9},{2,10},{3,11},{4,12},{5,13},{6,14},{7,15},{8,0},{9,1},... | collective-permute-start | bytes 442376 | tf_op jit(solution)/shard_map/ppermute | solution.py:24
  161.4 10.5 %collective-permute-start.46 = (s16[144,512]{1,0:T(8,128)(2,1)S(1)}, s16[144,512]{1,0:T(8,128)(2,1)S(1)}, u32[]{:S(2)}, u32[]{:S(2)}) collective-permute-start(s16[144,512]{1,0:T(8,128)(2,1)S(1)} %shard_map.121), channel_id=1, source_target_pairs={{0,6},{1,7},{2,4},{3,5},{4,2},{5,3},{6,0},{7,1},{8,14},{9,15},{10,... | collective-permute-start | bytes 442376 | tf_op jit(solution)/shard_map/ppermute | solution.py:24
  163.5 10.0 %collective-permute-start.47 = (s16[144,512]{1,0:T(8,128)(2,1)S(1)}, s16[144,512]{1,0:T(8,128)(2,1)S(1)}, u32[]{:S(2)}, u32[]{:S(2)}) collective-permute-start(s16[144,512]{1,0:T(8,128)(2,1)S(1)} %shard_map.121), channel_id=1, source_target_pairs={{0,4},{1,5},{2,6},{3,7},{4,0},{5,1},{6,2},{7,3},{8,12},{9,13},{10,... | collective-permute-start | bytes 442376 | tf_op jit(solution)/shard_map/ppermute | solution.py:24
  189.8 9.0 %collective-permute-start.51 = (s16[144,512]{1,0:T(8,128)(2,1)S(1)}, s16[144,512]{1,0:T(8,128)(2,1)S(1)}, u32[]{:S(2)}, u32[]{:S(2)}) collective-permute-start(s16[144,512]{1,0:T(8,128)(2,1)S(1)} %get-tuple-element.78), channel_id=1, source_target_pairs={{0,14},{1,15},{2,12},{3,13},{4,10},{5,11},{6,8},{7,9},{8,6},{9,7},... | collective-permute-start | bytes 442376 | tf_op jit(solution)/shard_map/ppermute | solution.py:24
  189.9 10.2 %collective-permute-start.52 = (s16[144,512]{1,0:T(8,128)(2,1)S(1)}, s16[144,512]{1,0:T(8,128)(2,1)S(1)}, u32[]{:S(2)}, u32[]{:S(2)}) collective-permute-start(s16[144,512]{1,0:T(8,128)(2,1)S(1)} %get-tuple-element.79), channel_id=1, source_target_pairs={{0,12},{1,13},{2,14},{3,15},{4,8},{5,9},{6,10},{7,11},{8,4},{9,5},... | collective-permute-start | bytes 442376 | tf_op jit(solution)/shard_map/ppermute | solution.py:24
  192.9 13.8 %collective-permute-start.53 = (s16[144,512]{1,0:T(8,128)(2,1)S(1)}, s16[144,512]{1,0:T(8,128)(2,1)S(1)}, u32[]{:S(2)}, u32[]{:S(2)}) collective-permute-start(s16[144,512]{1,0:T(8,128)(2,1)S(1)} %get-tuple-element.80), channel_id=1, source_target_pairs={{0,10},{1,11},{2,8},{3,9},{4,14},{5,15},{6,12},{7,13},{8,2},{9,3},... | collective-permute-start | bytes 442376 | tf_op jit(solution)/shard_map/ppermute | solution.py:24
  193.9 13.3 %collective-permute-start.54 = (s16[144,512]{1,0:T(8,128)(2,1)S(1)}, s16[144,512]{1,0:T(8,128)(2,1)S(1)}, u32[]{:S(2)}, u32[]{:S(2)}) collective-permute-start(s16[144,512]{1,0:T(8,128)(2,1)S(1)} %get-tuple-element.81), channel_id=1, source_target_pairs={{0,8},{1,9},{2,10},{3,11},{4,12},{5,13},{6,14},{7,15},{8,0},{9,1},... | collective-permute-start | bytes 442376 | tf_op jit(solution)/shard_map/ppermute | solution.py:24
  196.7 10.6 %collective-permute-start.55 = (s16[144,512]{1,0:T(8,128)(2,1)S(1)}, s16[144,512]{1,0:T(8,128)(2,1)S(1)}, u32[]{:S(2)}, u32[]{:S(2)}) collective-permute-start(s16[144,512]{1,0:T(8,128)(2,1)S(1)} %get-tuple-element.82), channel_id=1, source_target_pairs={{0,6},{1,7},{2,4},{3,5},{4,2},{5,3},{6,0},{7,1},{8,14},{9,15},{10,... | collective-permute-start | bytes 442376 | tf_op jit(solution)/shard_map/ppermute | solution.py:24
  198.8 8.4 %collective-permute-start.56 = (s16[144,512]{1,0:T(8,128)(2,1)S(1)}, s16[144,512]{1,0:T(8,128)(2,1)S(1)}, u32[]{:S(2)}, u32[]{:S(2)}) collective-permute-start(s16[144,512]{1,0:T(8,128)(2,1)S(1)} %get-tuple-element.83), channel_id=1, source_target_pairs={{0,4},{1,5},{2,6},{3,7},{4,0},{5,1},{6,2},{7,3},{8,12},{9,13},{10,... | collective-permute-start | bytes 442376 | tf_op jit(solution)/shard_map/ppermute | solution.py:24
  200.1 10.4 %collective-permute-start.57 = (s16[144,512]{1,0:T(8,128)(2,1)S(1)}, s16[144,512]{1,0:T(8,128)(2,1)S(1)}, u32[]{:S(2)}, u32[]{:S(2)}) collective-permute-start(s16[144,512]{1,0:T(8,128)(2,1)S(1)} %get-tuple-element.84), channel_id=1, source_target_pairs={{0,2},{1,3},{2,0},{3,1},{4,6},{5,7},{6,4},{7,5},{8,10},{9,11},{10,... | collective-permute-start | bytes 442376 | tf_op jit(solution)/shard_map/ppermute | solution.py:24
  211.3 6.8 %collective-permute-start.58 = (bf16[128,512]{1,0:T(8,128)(2,1)S(1)}, bf16[128,512]{1,0:T(8,128)(2,1)S(1)}, u32[]{:S(2)}, u32[]{:S(2)}) collective-permute-start(bf16[128,512]{1,0:T(8,128)(2,1)S(1)} %shard_map.129), channel_id=1, source_target_pairs={{0,14},{1,15},{2,12},{3,13},{4,10},{5,11},{6,8},{7,9},{8,6},{9,7},... | collective-permute-start | bytes 393224 | tf_op jit(solution)/shard_map/ppermute | solution.py:24
  212.8 7.9 %collective-permute-start.60 = (bf16[128,512]{1,0:T(8,128)(2,1)S(1)}, bf16[128,512]{1,0:T(8,128)(2,1)S(1)}, u32[]{:S(2)}, u32[]{:S(2)}) collective-permute-start(bf16[128,512]{1,0:T(8,128)(2,1)S(1)} %shard_map.129), channel_id=1, source_target_pairs={{0,10},{1,11},{2,8},{3,9},{4,14},{5,15},{6,12},{7,13},{8,2},{9,3},... | collective-permute-start | bytes 393224 | tf_op jit(solution)/shard_map/ppermute | solution.py:24
  213.1 10.4 %collective-permute-start.61 = (bf16[128,512]{1,0:T(8,128)(2,1)S(1)}, bf16[128,512]{1,0:T(8,128)(2,1)S(1)}, u32[]{:S(2)}, u32[]{:S(2)}) collective-permute-start(bf16[128,512]{1,0:T(8,128)(2,1)S(1)} %shard_map.129), channel_id=1, source_target_pairs={{0,8},{1,9},{2,10},{3,11},{4,12},{5,13},{6,14},{7,15},{8,0},{9,1},... | collective-permute-start | bytes 393224 | tf_op jit(solution)/shard_map/ppermute | solution.py:24
  216.1 7.4 %collective-permute-start.62 = (bf16[128,512]{1,0:T(8,128)(2,1)S(1)}, bf16[128,512]{1,0:T(8,128)(2,1)S(1)}, u32[]{:S(2)}, u32[]{:S(2)}) collective-permute-start(bf16[128,512]{1,0:T(8,128)(2,1)S(1)} %shard_map.129), channel_id=1, source_target_pairs={{0,6},{1,7},{2,4},{3,5},{4,2},{5,3},{6,0},{7,1},{8,14},{9,15},{10,... | collective-permute-start | bytes 393224 | tf_op jit(solution)/shard_map/ppermute | solution.py:24
  (29 other events, 354.2 us)
